TPU v7x, 32 devices: a whole 2x2x4 slice. The times are simulated.
32 devices in a mesh: seq: 4 (over x, core), group: 8 (over z, y).
Axes of the slice: x: 2, y: 2, z: 4, core: 2. Of those that a mesh axis runs over, the one named last changes fastest.
Arguments:
- token_ids: int32 [4, 1024], P(None, 'group'), may hold values from 0 to 50256
- target_ids: int32 [4, 1024], P(None, 'group'), may hold values from 0 to 50256
- doc_lengths: int32 [4, 8], replicated, may hold values from 1 to 1017, as said below
- expert_ids: int32 [4, 1024, 1], P('seq', 'group'), may hold values from 0 to 15; in each aligned block of 128 rows (0 to 127, 128 to 255, ..., all dimensions but the last counted through in order) at most 16 rows name the same one
- vocab_table: float32 [50304, 768], P(('seq', 'group'))
- vocab_table_mom: float32 [50304, 768], P(('seq', 'group')), may hold values from -5.340576e-05 to 5.340576e-05
- vocab_table_ema: float32 [50304, 768], P(('seq', 'group')), may hold values from -0.4375 to 0.4375
- mixer_in: float32 [768, 3072], P('group'), may hold values from -0.21875 to 0.21875
- mixer_in_mom: float32 [768, 3072], P('group'), may hold values from -5.340576e-05 to 5.340576e-05
- mixer_in_ema: float32 [768, 3072], P('group'), may hold values from -0.21875 to 0.21875
- mixer_x: float32 [1536, 128], P('group'), may hold values from -0.15625 to 0.15625
- mixer_x_mom: float32 [1536, 128], P('group'), may hold values from -5.340576e-05 to 5.340576e-05
- mixer_x_ema: float32 [1536, 128], P('group'), may hold values from -0.15625 to 0.15625
- mixer_out: float32 [1536, 768], P('group'), may hold values from -0.15625 to 0.15625
- mixer_out_mom: float32 [1536, 768], P('group'), may hold values from -5.340576e-05 to 5.340576e-05
- mixer_out_ema: float32 [1536, 768], P('group'), may hold values from -0.15625 to 0.15625
- channel: float32 [23, 1536], P(None, 'group')
- channel_mom: float32 [23, 1536], P(None, 'group'), may hold values from -5.340576e-05 to 5.340576e-05
- channel_ema: float32 [23, 1536], P(None, 'group'), may hold values from -6 to 6
- norm_gains: float32 [3, 768], P(None, 'group'), may hold values from 0.5 to 1.5
- norm_gains_mom: float32 [3, 768], P(None, 'group'), may hold values from -5.340576e-05 to 5.340576e-05
- norm_gains_ema: float32 [3, 768], P(None, 'group'), may hold values from 0.5 to 1.5
- router: float32 [768, 16], P('group'), may hold values from -0.109375 to 0.109375
- router_mom: float32 [768, 16], P('group'), may hold values from -5.340576e-05 to 5.340576e-05
- router_ema: float32 [768, 16], P('group'), may hold values from -0.109375 to 0.109375
- experts: float32 [2, 16, 3072, 768], P(None, 'seq', 'group'), may hold values from -0.21875 to 0.21875
- experts_mom: float32 [2, 16, 3072, 768], P(None, 'seq', 'group'), may hold values from -5.340576e-05 to 5.340576e-05
- experts_ema: float32 [2, 16, 3072, 768], P(None, 'seq', 'group'), may hold values from -0.21875 to 0.21875
Outputs:
- loss_sum: float32 [], replicated
- grad_norm: float32 [], replicated
- moe_branch: float32 [4, 1024, 768], P('seq', 'group')
- vocab_table_new: float32 [50304, 768], P(('seq', 'group'))
- vocab_table_mom_new: float32 [50304, 768], P(('seq', 'group'))
- vocab_table_ema_new: float32 [50304, 768], P(('seq', 'group'))
- mixer_in_new: float32 [768, 3072], P('group')
- mixer_in_mom_new: float32 [768, 3072], P('group')
- mixer_in_ema_new: float32 [768, 3072], P('group')
- mixer_x_new: float32 [1536, 128], P('group')
- mixer_x_mom_new: float32 [1536, 128], P('group')
- mixer_x_ema_new: float32 [1536, 128], P('group')
- mixer_out_new: float32 [1536, 768], P('group')
- mixer_out_mom_new: float32 [1536, 768], P('group')
- mixer_out_ema_new: float32 [1536, 768], P('group')
- channel_new: float32 [23, 1536], P(None, 'group')
- channel_mom_new: float32 [23, 1536], P(None, 'group')
- channel_ema_new: float32 [23, 1536], P(None, 'group')
- norm_gains_new: float32 [3, 768], P(None, 'group')
- norm_gains_mom_new: float32 [3, 768], P(None, 'group')
- norm_gains_ema_new: float32 [3, 768], P(None, 'group')
- router_new: float32 [768, 16], P('group')
- router_mom_new: float32 [768, 16], P('group')
- router_ema_new: float32 [768, 16], P('group')
- experts_new: float32 [2, 16, 3072, 768], P(None, 'seq', 'group')
- experts_mom_new: float32 [2, 16, 3072, 768], P(None, 'seq', 'group')
- experts_ema_new: float32 [2, 16, 3072, 768], P(None, 'seq', 'group')
Inputs may be any that keep to these rules, and one draw needn't show every extreme that they name: `doc_lengths`: each row sums to 1024; the second document of every sequence starts within its first 128 positions and ends within its last 128. `expert_ids`: among the 128 rows of one device no expert is named more than 16 times, and in every draw some device names some expert exactly 16 times.
All inputs are finite; a program needn't handle non-finite values.
Results may differ from a plain program's by a relative error of at most 0.0095.
The roundings to bfloat16 on the way count: a program that leaves them out, or rounds other values in their place, can miss the bound.
Values may be sent and summed in bfloat16 or wider, within the bound.
A program may use at most 448 MiB of HBM per device.

v0:
```python
import functools

import jax
import jax.numpy as jnp
from jax import lax
from jax.experimental import pallas as pl
from jax.experimental.pallas import tpu as pltpu
from jax.sharding import PartitionSpec as P

D = 768
DI = 1536
STATE = 16
RANK = 48
CONV = 4
VOCAB_REAL = 50257


EPS = 1e-05
CLIP = 0.1
MOMENTUM = 0.9
LRATE = 1000.0
CHANNEL_LRATE = 10000.0
EMA_KEEP = 0.8
HIGHEST = lax.Precision.HIGHEST
MESH = pl.DeviceIdType.MESH
VMEM_LIMIT = 56 << 20
LANES = 128


def axis_sizes():
    seq, group = (lax.axis_size("seq"), lax.axis_size("group"))
    core = 2 if seq % 2 == 0 else 1
    y = 1
    while 4 * y * y <= group and group % (2 * y) == 0:
        y *= 2
    return {"x": seq // core, "core": core, "z": group // y, "y": y}


def my_place(sizes):
    seq, group = (lax.axis_index("seq"), lax.axis_index("group"))
    return {
        "x": seq // sizes["core"],
        "core": seq % sizes["core"],
        "z": group // sizes["y"],
        "y": group % sizes["y"],
    }


def device_of(place, sizes):
    return (place["x"] * sizes["core"] + place["core"], place["z"] * sizes["y"] + place["y"])


def moved(place, axis, by, sizes):
    return {**place, axis: lax.rem(place[axis] + by + sizes[axis], sizes[axis])}


def block_of(place, sizes):
    seq, group = device_of(place, sizes)
    return seq * (sizes["z"] * sizes["y"]) + group


def meet(peers):
    barrier = pltpu.get_barrier_semaphore()
    for peer in peers:
        pl.semaphore_signal(barrier, inc=1, device_id=peer, device_id_type=MESH)
    pl.semaphore_wait(barrier, len(peers))


def line_peers(place, sizes):
    return [
        device_of(moved(place, axis, by, sizes), sizes)
        for axis in ("x", "core", "z", "y")
        for by in range(1, sizes[axis])
    ]


GATHER_ORDERS = (
    ("z", "y", "x", "core"),
    ("z", "x", "y", "core"),
    ("x", "z", "y", "core"),
    ("y", "z", "x", "core"),
)


def gather_kernel(sizes, pieces, own_ref, all_ref, local_sem, send_sem, recv_sem):
    place = my_place(sizes)
    meet(line_peers(place, sizes))
    keep_own = pltpu.make_async_copy(own_ref, all_ref.at[block_of(place, sizes)], local_sem)
    keep_own.start()
    held = [[(place, None)] for _ in pieces]
    sends = []
    for phase in range(4):
        fresh = [[] for _ in pieces]
        for turn in range(max(len(blocks) for blocks in held)):
            for which, (order, first, rows) in enumerate(pieces):
                if turn >= len(held[which]):
                    continue
                axis = order[phase]
                where, arrival = held[which][turn]
                if arrival is not None:
                    copy, seen = arrival
                    if not seen:
                        copy.wait_recv()
                        held[which][turn] = (where, (copy, True))
                span = pl.ds(first, rows)
                for by in range(1, sizes[axis]):
                    block = block_of(where, sizes)
                    source = own_ref.at[span] if arrival is None else all_ref.at[block, span]
                    number = len(sends)
                    copy = pltpu.make_async_remote_copy(
                        src_ref=source,
                        dst_ref=all_ref.at[block, span],
                        send_sem=send_sem.at[number],
                        recv_sem=recv_sem.at[number],
                        device_id=device_of(moved(place, axis, by, sizes), sizes),
                        device_id_type=MESH,
                    )
                    copy.start()
                    sends.append(copy)
                    fresh[which].append((moved(where, axis, -by, sizes), (copy, False)))
        held = [old + new for old, new in zip(held, fresh)]
    for blocks in held:
        for _, arrival in blocks:
            if arrival is not None and not arrival[1]:
                arrival[0].wait_recv()
    for copy in sends:
        copy.wait_send()
    keep_own.wait()


def split_rows(rows, orders):
    unit = 32 if rows % 32 == 0 else 16
    count = rows // unit
    pieces, first = ([], 0)
    for which in range(min(count, 4)):
        size = (count * (which + 1) // min(count, 4)) * unit - first
        pieces.append((orders[which % len(orders)], first, size))
        first += size
    return pieces


def gather_all(rows, collective_id):
    sizes = axis_sizes()
    devices = sizes["x"] * sizes["core"] * sizes["z"] * sizes["y"]
    pieces = split_rows(rows.shape[0], GATHER_ORDERS)
    copies = (devices - 1) * len(pieces)
    return pl.pallas_call(
        functools.partial(gather_kernel, sizes, pieces),
        out_shape=jax.ShapeDtypeStruct((devices,) + rows.shape, rows.dtype),
        in_specs=[pl.BlockSpec(memory_space=pltpu.VMEM)],
        out_specs=pl.BlockSpec(memory_space=pl.ANY),
        scratch_shapes=[
            pltpu.SemaphoreType.DMA,
            pltpu.SemaphoreType.DMA((copies,)),
            pltpu.SemaphoreType.DMA((copies,)),
        ],
        compiler_params=pltpu.CompilerParams(
            collective_id=collective_id, has_side_effects=True, vmem_limit_bytes=VMEM_LIMIT
        ),
        name="gather_all",
    )(rows)


SCATTER_ORDERS = (("core", "x", "y", "z"), ("core", "y", "x", "z"))
GATHER_PAIR = (("z", "y", "x", "core"), ("z", "x", "y", "core"))
NATURAL = ("x", "core", "z", "y")
PIECE = 16
SPAN = 2 * PIECE


def unravel(number, extents):
    places = []
    for extent in reversed(extents):
        places.append(lax.rem(number, extent))
        number = lax.div(number, extent)
    return tuple(reversed(places))


def piece_rows(pair, kind):
    first = pair * SPAN + kind * PIECE
    if not isinstance(first, int):
        first = pl.multiple_of(first, PIECE)
    return pl.ds(first, PIECE)


def scatter_scratch(sizes, pairs, width, keep):
    scratch = []
    for order in SCATTER_ORDERS:
        landings, sums, semaphores = ([], [], [])
        for phase in range(4):
            left = tuple(sizes[a] for a in NATURAL if a not in order[: phase + 1])
            others = max(1, sizes[order[phase]] - 1)
            landings.append(pltpu.VMEM((pairs, others) + left + (PIECE, width), jnp.bfloat16))
            if phase < 3:
                sums.append(pltpu.VMEM((pairs,) + left + (PIECE, width), jnp.bfloat16))
            semaphores.append(pltpu.SemaphoreType.DMA((pairs, others)))
            semaphores.append(pltpu.SemaphoreType.DMA((pairs, others)))
        scratch += landings + sums + semaphores
        scratch += [pltpu.SemaphoreType.DMA((pairs,))] if keep else []
    return scratch


class Scatter:
    def __init__(self, sizes, pairs, full_ref, own_ref, scratch, keep):
        self.sizes, self.pairs, self.keep = (sizes, pairs, keep)
        self.full_ref, self.own_ref = (full_ref, own_ref)
        self.place = my_place(sizes)
        size = len(scratch) // 2
        self.refs = (scratch[:size], scratch[size:])

    def kept(self, kind, pair):
        order = SCATTER_ORDERS[kind]
        index = tuple(self.place[a] if a == order[0] else slice(None) for a in NATURAL)
        return pltpu.make_async_copy(
            self.full_ref.at[index + (piece_rows(pair, kind),)],
            self.refs[kind][4].at[pair],
            self.refs[kind][15].at[pair],
        )

    def copies(self, kind, pair, phase):
        order, refs, sizes = (SCATTER_ORDERS[kind], self.refs[kind], self.sizes)
        axis = order[phase]
        left = [a for a in NATURAL if a not in order[:phase]]
        made = []
        for by in range(1, sizes[axis]):
            to = moved(self.place, axis, by, sizes)
            index = tuple(to[axis] if a == axis else slice(None) for a in left)
            if phase == 0:
                source = self.full_ref.at[index + (piece_rows(pair, kind),)]
            else:
                source = refs[3 + phase].at[(pair,) + index]
            made.append(
                pltpu.make_async_remote_copy(
                    src_ref=source,
                    dst_ref=refs[phase].at[pair, by - 1],
                    send_sem=refs[7 + 2 * phase].at[pair, by - 1],
                    recv_sem=refs[8 + 2 * phase].at[pair, by - 1],
                    device_id=device_of(to, sizes),
                    device_id_type=MESH,
                )
            )
        return made

    def launch(self, pair, phase):
        for kind in range(2):
            for copy in self.copies(kind, pair, phase):
                copy.start()

    def absorb(self, kind, pair, phase):
        order, refs, sizes, place = (
            SCATTER_ORDERS[kind],
            self.refs[kind],
            self.sizes,
            self.place,
        )
        axis = order[phase]
        before = [a for a in NATURAL if a not in order[:phase]]
        after = [a for a in before if a != axis]
        if phase == 0 and self.keep:
            self.kept(kind, pair).wait()
        for copy in self.copies(kind, pair, phase):
            copy.wait_recv()
        extents = tuple(sizes[a] for a in after)
        number = 1
        for extent in extents:
            number *= extent

        def add(step, carry):
            spot = dict(zip(after, unravel(step, extents)))
            mine = tuple(place[axis] if a == axis else spot[a] for a in before)
            there = tuple(spot[a] for a in after)
            if phase > 0:
                kept_part = refs[3 + phase][(pair,) + mine]
            elif self.keep:
                kept_part = refs[4][(pair,) + there]
            else:
                kept_part = self.full_ref[mine + (piece_rows(pair, kind),)]
            total = kept_part.astype(jnp.float32)
            for by in range(1, sizes[axis]):
                total = total + refs[phase][(pair, by - 1) + there].astype(jnp.float32)
            if phase == 3:
                self.own_ref[piece_rows(pair, kind)] = total
            else:
                refs[4 + phase][(pair,) + there] = total.astype(jnp.bfloat16)
            return carry

        if number == 1:
            add(0, 0)
        else:
            lax.fori_loop(0, number, add, 0)

    def advance(self, pair, phase):
        for kind in range(2):
            self.absorb(kind, pair, phase)
            if phase < 3:
                for copy in self.copies(kind, pair, phase + 1):
                    copy.start()

    def finish(self):
        def one(pair, carry):
            for kind in range(2):
                for phase in range(4):
                    for copy in self.copies(kind, pair, phase):
                        copy.wait_send()
            return carry

        lax.fori_loop(0, self.pairs, one, 0)


def wave(pairs, phases, act):
    def step(turn, carry):
        for phase in range(phases - 1, -1, -1):
            pair = turn - phase

            @pl.when((pair >= 0) & (pair < pairs))
            def _(pair=pair, phase=phase):
                act(pair, phase)

        return carry

    lax.fori_loop(0, pairs + phases - 1, step, 0)


def scatter_kernel(sizes, pairs, full_ref, own_ref, *scratch):
    meet(line_peers(my_place(sizes), sizes))
    scatter = Scatter(sizes, pairs, full_ref, own_ref, scratch, True)
    for pair in range(pairs):
        scatter.launch(pair, 0)
        for kind in range(2):
            scatter.kept(kind, pair).start()
    wave(pairs, 4, scatter.advance)
    scatter.finish()


def scatter_all(blocks, collective_id):
    sizes = axis_sizes()
    rows, width = blocks.shape[-2:]
    pairs = rows // SPAN
    shaped = blocks.reshape(tuple(sizes[a] for a in NATURAL) + (rows, width))
    return pl.pallas_call(
        functools.partial(scatter_kernel, sizes, pairs),
        out_shape=jax.ShapeDtypeStruct((rows, width), jnp.float32),
        in_specs=[pl.BlockSpec(memory_space=pl.ANY)],
        out_specs=pl.BlockSpec(memory_space=pltpu.VMEM),
        scratch_shapes=scatter_scratch(sizes, pairs, width, True),
        compiler_params=pltpu.CompilerParams(
            collective_id=collective_id, has_side_effects=True, vmem_limit_bytes=VMEM_LIMIT
        ),
        name="scatter_all",
    )(shaped)


class Gather:
    def __init__(self, sizes, pairs, own_ref, all_ref, semaphores):
        self.sizes, self.pairs = (sizes, pairs)
        self.own_ref, self.all_ref = (own_ref, all_ref)
        self.semaphores = semaphores
        self.place = my_place(sizes)

    def copies(self, kind, pair, phase):
        order = GATHER_PAIR[kind]
        axis, span = (order[phase], piece_rows(pair, kind))
        block = tuple(slice(None) if a in order[:phase] else self.place[a] for a in NATURAL)
        there = self.all_ref.at[block + (span,)]
        send_sem, recv_sem = (self.semaphores[2 * phase], self.semaphores[2 * phase + 1])
        return [
            pltpu.make_async_remote_copy(
                src_ref=self.own_ref.at[span] if phase == 0 else there,
                dst_ref=there,
                send_sem=send_sem.at[kind, pair, by - 1],
                recv_sem=recv_sem.at[kind, pair, by - 1],
                device_id=device_of(moved(self.place, axis, by, self.sizes), self.sizes),
                device_id_type=MESH,
            )
            for by in range(1, self.sizes[axis])
        ]

    def advance(self, pair, phase):
        for kind in range(2):
            if phase > 0:
                for copy in self.copies(kind, pair, phase - 1):
                    copy.wait_recv()
            if phase < 4:
                for copy in self.copies(kind, pair, phase):
                    copy.start()

    def finish(self):
        def one(pair, carry):
            for kind in range(2):
                for phase in range(4):
                    for copy in self.copies(kind, pair, phase):
                        copy.wait_send()
            return carry

        lax.fori_loop(0, self.pairs, one, 0)


def gather_semaphores(sizes, pairs):
    longest = max(sizes.values())
    return [pltpu.SemaphoreType.DMA((2, pairs, longest)) for _ in range(8)]


def seq_place(seq, sizes):
    return (lax.div(seq, sizes["core"]), lax.rem(seq, sizes["core"]))


def merge_stats(first, second):
    high = jnp.maximum(first[0], second[0])
    mass = first[1] * jnp.exp(first[0] - high) + second[1] * jnp.exp(second[0] - high)
    return (high, mass, first[2] + second[2])


def span_rows(pair):
    return pl.ds(pl.multiple_of(pair * SPAN, SPAN), SPAN)


def masked_logits(table_ref, rows_in, first_masked, limit):
    logits = matmul_nt(table_ref[...], rows_in)
    tail = logits[first_masked:]
    numbers = first_masked + lax.broadcasted_iota(jnp.int32, tail.shape, 0)
    return jnp.concatenate([logits[:first_masked], jnp.where(numbers < limit, tail, -1e30)], axis=0)


def vocab_limit(own_vocab):
    devices, _, me = flat_place()
    least = max(0, VOCAB_REAL - (devices - 1) * own_vocab)
    limit = jnp.minimum(own_vocab, VOCAB_REAL - me * own_vocab)
    return (min(least, own_vocab) // 16 * 16, limit)


def head_forward_kernel(
    sizes,
    pairs,
    own_vocab,
    own_ref,
    table_ref,
    target_ref,
    all_ref,
    stats_ref,
    mine_ref,
    landing_ref,
    local_sem,
    stat_send,
    stat_recv,
    *semaphores,
):
    place = my_place(sizes)
    meet(line_peers(place, sizes))
    gather = Gather(sizes, pairs, own_ref, all_ref, semaphores)
    keep_own = pltpu.make_async_copy(
        own_ref, all_ref.at[tuple(place[a] for a in NATURAL)], local_sem
    )
    keep_own.start()
    groups = sizes["z"] * sizes["y"]
    seqs = sizes["x"] * sizes["core"]
    first_masked, limit = vocab_limit(own_vocab)

    def seq_stats(pair, seq):
        x, core = seq_place(seq, sizes)
        rows_in = all_ref[x, core, :, :, span_rows(pair), :].reshape(groups * SPAN, D)
        logits = masked_logits(table_ref, rows_in, first_masked, limit)
        spot = pl.ds(pair * seqs + seq, 1)
        numbers = lax.broadcasted_iota(jnp.int32, logits.shape, 0)
        top = jnp.max(logits, axis=0, keepdims=True)
        mine_ref[0, 0, spot] = top
        mine_ref[0, 1, spot] = jnp.sum(jnp.exp(logits - top), axis=0, keepdims=True)
        mine_ref[0, 2, spot] = jnp.sum(
            jnp.where(numbers == target_ref[spot], logits, 0.0), axis=0, keepdims=True
        )

    def turn_step(turn, carry):
        for phase in range(4, -1, -1):
            pair = turn - phase

            @pl.when((pair >= 0) & (pair < pairs))
            def _(pair=pair, phase=phase):
                gather.advance(pair, phase)

        @pl.when(turn == 0)
        def _():
            keep_own.wait()

        @pl.when(turn >= 4)
        def _():
            def one(seq, carry):
                seq_stats(turn - 4, seq)
                return carry

            lax.fori_loop(0, seqs, one, 0)

        return carry

    lax.fori_loop(0, pairs + 4, turn_step, 0)
    started = []
    stats = tuple(mine_ref[0, k] for k in range(3))
    for phase, axis in enumerate(("core", "x", "y", "z")):
        arrivals = []
        for by in range(1, sizes[axis]):
            slot = len(started)
            copy = pltpu.make_async_remote_copy(
                src_ref=mine_ref.at[phase],
                dst_ref=landing_ref.at[slot],
                send_sem=stat_send.at[slot],
                recv_sem=stat_recv.at[slot],
                device_id=device_of(moved(place, axis, by, sizes), sizes),
                device_id_type=MESH,
            )
            copy.start()
            arrivals.append((copy, slot))
            started.append(copy)
        for copy, slot in arrivals:
            copy.wait_recv()
            stats = merge_stats(stats, tuple(landing_ref[slot, k] for k in range(3)))
        if phase < 3:
            for k in range(3):
                mine_ref[phase + 1, k] = stats[k]
    stats_ref[0] = stats[0] + jnp.log(stats[1])
    stats_ref[1] = stats[2]
    gather.finish()
    for copy in started:
        copy.wait_send()


def head_forward(rows, table, own_vocab, targets, collective_id):
    sizes = axis_sizes()
    pairs = rows.shape[0] // SPAN
    hops = sum(extent - 1 for extent in sizes.values())
    natural = tuple(sizes[a] for a in NATURAL)
    packed = (3,) + targets.shape
    vmem = pl.BlockSpec(memory_space=pltpu.VMEM)
    return pl.pallas_call(
        functools.partial(head_forward_kernel, sizes, pairs, own_vocab),
        out_shape=(
            jax.ShapeDtypeStruct(natural + rows.shape, rows.dtype),
            jax.ShapeDtypeStruct((2,) + targets.shape, jnp.float32),
        ),
        in_specs=[vmem] * 3,
        out_specs=(vmem,) * 2,
        scratch_shapes=[
            pltpu.VMEM((4,) + packed, jnp.float32),
            pltpu.VMEM((hops,) + packed, jnp.float32),
            pltpu.SemaphoreType.DMA,
            pltpu.SemaphoreType.DMA((hops,)),
            pltpu.SemaphoreType.DMA((hops,)),
        ]
        + gather_semaphores(sizes, pairs),
        compiler_params=pltpu.CompilerParams(
            collective_id=collective_id, has_side_effects=True, vmem_limit_bytes=VMEM_LIMIT
        ),
        name="head_forward",
    )(rows, table, targets)


def head_backward_kernel(
    sizes,
    pairs,
    own_vocab,
    all_ref,
    table_ref,
    turned_ref,
    target_ref,
    level_ref,
    weight_ref,
    own_ref,
    tgrad_ref,
    full_ref,
    grad_ref,
    *scratch,
):
    meet(line_peers(my_place(sizes), sizes))
    scatter = Scatter(sizes, pairs, full_ref, own_ref, scratch, False)
    groups = sizes["z"] * sizes["y"]
    seqs = sizes["x"] * sizes["core"]
    first_masked, limit = vocab_limit(own_vocab)
    height = table_ref.shape[0]
    block = groups * SPAN

    def seq_grads(pair, seq):
        x, core = divmod(seq, sizes["core"])
        rows_in = all_ref[x, core, :, :, span_rows(pair), :].reshape(block, D)
        logits = masked_logits(table_ref, rows_in, first_masked, limit)
        spot = pl.ds(pair * seqs + seq, 1)
        numbers = lax.broadcasted_iota(jnp.int32, logits.shape, 0)
        share = jnp.exp(logits - level_ref[spot])
        share = jnp.where(numbers == target_ref[spot], share - 1.0, share)
        grad_ref[pair, 0:height, seq * block : (seq + 1) * block] = (
            weight_ref[spot] * share
        ).astype(jnp.bfloat16)

    def row_product(pair):
        turned = matmul(turned_ref[...], grad_ref[pair])
        full_ref[:, :, :, :, span_rows(pair), :] = turned.T.astype(jnp.bfloat16).reshape(
            tuple(sizes[a] for a in NATURAL) + (SPAN, D)
        )

    def table_product(pair):
        rows_in = all_ref[:, :, :, :, span_rows(pair), :].reshape(seqs * block, D)
        return matmul(grad_ref[pair, 0:height], rows_in)

    if grad_ref.shape[1] > height:
        grad_ref[:, height:] = jnp.zeros_like(grad_ref[:, height:])

    def turn_step(turn, carry):
        def older(by, phase):
            pair = turn - by

            @pl.when((pair >= 0) & (pair < pairs))
            def _():
                scatter.advance(pair, phase)

        def compute(act):
            @pl.when(turn < pairs)
            def _():
                act()

        for part in range(4):
            for seq in range(part * seqs // 4, (part + 1) * seqs // 4):
                compute(lambda seq=seq: seq_grads(turn, seq))
            if part == 0:
                older(1, 0)
            elif part == 1:
                older(2, 3)
            elif part == 2:
                older(1, 1)
        compute(lambda: row_product(turn))
        older(1, 2)
        compute(lambda: scatter.launch(turn, 0))
        return carry

    lax.fori_loop(0, pairs, turn_step, 0)
    tgrad_ref[...] = table_product(0)
    scatter.advance(pairs - 1, 0)
    if pairs > 1:
        scatter.advance(pairs - 2, 3)

    def late(pair, carry):
        tgrad_ref[...] += table_product(pair)

        @pl.when(pair < 3)
        def _():
            for phase in (1, 2):

                @pl.when(pair == phase)
                def _(phase=phase):
                    scatter.advance(pairs - 1, phase)

        return carry

    lax.fori_loop(1, pairs, late, 0)
    for phase in range(max(1, pairs), 4):
        if phase < 3:
            scatter.advance(pairs - 1, phase)
    scatter.advance(pairs - 1, 3)
    scatter.finish()


def head_backward(all_rows, table, turned, own_vocab, targets, levels, weights, collective_id):
    sizes = axis_sizes()
    tokens = all_rows.shape[-2]
    pairs = tokens // SPAN
    vmem = pl.BlockSpec(memory_space=pltpu.VMEM)
    block = targets.shape[1]
    seqs = sizes["x"] * sizes["core"]
    return pl.pallas_call(
        functools.partial(head_backward_kernel, sizes, pairs, own_vocab),
        out_shape=(
            jax.ShapeDtypeStruct((tokens, D), jnp.float32),
            jax.ShapeDtypeStruct(table.shape, jnp.float32),
        ),
        in_specs=[vmem] * 6,
        out_specs=(vmem,) * 2,
        scratch_shapes=[
            pltpu.VMEM(all_rows.shape, jnp.bfloat16),
            pltpu.VMEM((pairs, turned.shape[1], seqs * block), jnp.bfloat16),
        ]
        + scatter_scratch(sizes, pairs, D, False),
        compiler_params=pltpu.CompilerParams(
            collective_id=collective_id, has_side_effects=True, vmem_limit_bytes=VMEM_LIMIT
        ),
        name="head_backward",
    )(all_rows, table, turned, targets, levels, weights)


def everyone(devices, groups, me, act):
    def step(by, carry):
        peer = lax.rem(me + by, devices)
        act(by, peer, (lax.div(peer, groups), lax.rem(peer, groups)))
        return carry

    lax.fori_loop(1, devices, step, 0)


def greet_everyone(devices, groups, me):
    barrier = pltpu.get_barrier_semaphore()

    def greet(by, peer, address):
        pl.semaphore_signal(barrier, inc=1, device_id=address, device_id_type=MESH)

    everyone(devices, groups, me, greet)
    pl.semaphore_wait(barrier, devices - 1)


def flat_place():
    groups = lax.axis_size("group")
    return (
        lax.axis_size("seq") * groups,
        groups,
        lax.axis_index("seq") * groups + lax.axis_index("group"),
    )


def share_kernel(own_ref, all_ref, send_sem, recv_sem):
    devices, groups, me = flat_place()
    greet_everyone(devices, groups, me)

    def copy_to(by, address):
        return pltpu.make_async_remote_copy(
            src_ref=own_ref,
            dst_ref=all_ref.at[me],
            send_sem=send_sem.at[by],
            recv_sem=recv_sem.at[by],
            device_id=address,
            device_id_type=MESH,
        )

    everyone(devices, groups, me, lambda by, peer, address: copy_to(by, address).start())
    all_ref[me] = own_ref[...]
    everyone(devices, groups, me, lambda by, peer, address: copy_to(by, address).wait())


def share_small(values, collective_id):
    devices = lax.axis_size("seq") * lax.axis_size("group")
    return pl.pallas_call(
        share_kernel,
        out_shape=jax.ShapeDtypeStruct((devices,) + values.shape, values.dtype),
        in_specs=[pl.BlockSpec(memory_space=pltpu.VMEM)],
        out_specs=pl.BlockSpec(memory_space=pltpu.VMEM),
        scratch_shapes=[
            pltpu.SemaphoreType.DMA((devices,)),
            pltpu.SemaphoreType.DMA((devices,)),
        ],
        compiler_params=pltpu.CompilerParams(collective_id=collective_id, has_side_effects=True),
        name="share_small",
    )(values)


def stats_kernel(parts_ref, all_ref, own_ref, got_ref, mine_ref, send_sem, recv_sem):
    devices, groups, me = flat_place()
    greet_everyone(devices, groups, me)

    def part_to(by, peer, address):
        return pltpu.make_async_remote_copy(
            src_ref=parts_ref.at[peer],
            dst_ref=got_ref.at[me],
            send_sem=send_sem.at[0, by],
            recv_sem=recv_sem.at[0, by],
            device_id=address,
            device_id_type=MESH,
        )

    def total_to(by, address):
        return pltpu.make_async_remote_copy(
            src_ref=mine_ref,
            dst_ref=all_ref.at[me],
            send_sem=send_sem.at[1, by],
            recv_sem=recv_sem.at[1, by],
            device_id=address,
            device_id_type=MESH,
        )

    everyone(devices, groups, me, lambda by, peer, address: part_to(by, peer, address).start())
    got_ref[me] = parts_ref[me]
    everyone(devices, groups, me, lambda by, peer, address: part_to(by, peer, address).wait())
    tops = got_ref[:, 0, :]
    top = jnp.max(tops, axis=0, keepdims=True)
    mass = jnp.sum(got_ref[:, 1, :] * jnp.exp(tops - top), axis=0, keepdims=True)
    hit = jnp.sum(got_ref[:, 2, :], axis=0, keepdims=True)
    level = top + jnp.log(mass)
    mine_ref[...] = jnp.broadcast_to(level, mine_ref.shape)
    everyone(devices, groups, me, lambda by, peer, address: total_to(by, address).start())
    all_ref[me] = mine_ref[...]
    own_ref[...] = jnp.broadcast_to(level - hit, own_ref.shape)
    everyone(devices, groups, me, lambda by, peer, address: total_to(by, address).wait())


def combine_stats(parts, collective_id):
    devices = parts.shape[0]
    shape = parts.shape[1:]
    return pl.pallas_call(
        stats_kernel,
        out_shape=(
            jax.ShapeDtypeStruct(parts.shape, jnp.float32),
            jax.ShapeDtypeStruct(shape, jnp.float32),
        ),
        in_specs=[pl.BlockSpec(memory_space=pltpu.VMEM)],
        out_specs=(pl.BlockSpec(memory_space=pltpu.VMEM),) * 2,
        scratch_shapes=[
            pltpu.VMEM(parts.shape, jnp.float32),
            pltpu.VMEM(shape, jnp.float32),
            pltpu.SemaphoreType.DMA((2, devices)),
            pltpu.SemaphoreType.DMA((2, devices)),
        ],
        compiler_params=pltpu.CompilerParams(collective_id=collective_id, has_side_effects=True),
        name="combine_stats",
    )(parts)


def chain_exchange(rates, total_step, flag, end_state, backwards, out_buf, in_buf, sems):
    devices, me = (lax.axis_size("group"), lax.axis_index("group"))
    seq = lax.axis_index("seq")
    send_sem, recv_sem = sems
    width = rates.shape[1]

    def join(first, second):
        return (
            jnp.exp(second[0] * rates) * second[1] * first[2] + second[2],
            first[0] + second[0],
            first[1] * second[1],
        )

    window = (total_step, flag, end_state)
    before = None
    distance, lap = (1, 0)
    copies = []
    while distance < devices:
        to = lax.rem(me + (devices - distance if backwards else distance), devices)
        out_buf[lap, 0:STATE] = window[2]
        out_buf[lap, STATE : STATE + 8] = jnp.concatenate(
            [
                jnp.broadcast_to(window[0], (4, width)),
                jnp.broadcast_to(window[1], (4, width)),
            ],
            axis=0,
        )
        copy = pltpu.make_async_remote_copy(
            src_ref=out_buf.at[lap],
            dst_ref=in_buf.at[lap],
            send_sem=send_sem.at[lap],
            recv_sem=recv_sem.at[lap],
            device_id=(seq, to),
            device_id_type=MESH,
        )
        copy.start()
        copies.append(copy)
        copy.wait_recv()
        reached = (me + distance < devices) if backwards else (me >= distance)
        real = jnp.where(reached, 1.0, 0.0)
        tail = in_buf[lap, STATE : STATE + 8]
        got = (
            tail[0:1] * real,
            tail[4:5] * real + (1.0 - real),
            in_buf[lap, 0:STATE] * real,
        )
        if before is None:
            before = got
        else:
            merged = join(got, before)
            before = (merged[1], merged[2], merged[0])
        merged = join(got, window)
        window = (merged[1], merged[2], merged[0])
        distance *= 2
        lap += 1
    for copy in copies:
        copy.wait_send()
    if before is None:
        return jnp.zeros_like(end_state)
    return before[2]


def chain_peers():
    devices, me = (lax.axis_size("group"), lax.axis_index("group"))
    seq = lax.axis_index("seq")
    distances = []
    distance = 1
    while distance < devices:
        distances += [distance, devices - distance]
        distance *= 2
    return [(seq, lax.rem(me + by, devices)) for by in sorted(set(distances))]


def chain_laps():
    laps, distance = (0, 1)
    while distance < lax.axis_size("group"):
        laps, distance = (laps + 1, distance * 2)
    return max(1, laps)


def spans(width):
    size = 512 if width % 512 == 0 else width
    return [slice(first, first + size) for first in range(0, width, size)]


def wide(value, copies):
    return jnp.concatenate([value] * copies, axis=1)


def folded(value):
    total = value[:, :LANES]
    for first in range(LANES, value.shape[1], LANES):
        total = total + value[:, first : first + LANES]
    return total


def scan_forward_kernel(
    step_ref, act_ref, b_ref, c_ref, keep_ref, rate_ref, y_ref, in_ref, out_buf, in_buf, ss, rs
):
    meet(chain_peers())
    tokens, width = step_ref.shape
    ends = []
    for span in spans(width):
        copies = (span.stop - span.start) // LANES
        rates = rate_ref[:, span]

        def advance(block, state, span=span, copies=copies, rates=rates):
            rows = pl.ds(pl.multiple_of(block * 8, 8), 8)
            steps = step_ref[rows, span]
            drives = steps * act_ref[rows, span]
            keeps = wide(keep_ref[rows, :], copies)
            for r in range(8):
                decay = jnp.exp(steps[r : r + 1] * rates) * keeps[r : r + 1]
                state = decay * state + drives[r : r + 1] * wide(b_ref[block * 8 + r], copies)
            return state

        ends.append(
            lax.fori_loop(
                0, tokens // 8, advance, jnp.zeros((STATE, span.stop - span.start), jnp.float32)
            )
        )
    total_step = jnp.sum(step_ref[...], axis=0, keepdims=True)
    flag = wide(jnp.min(keep_ref[...], axis=0, keepdims=True), width // LANES)
    incoming = chain_exchange(
        rate_ref[...],
        total_step,
        flag,
        jnp.concatenate(ends, axis=1),
        False,
        out_buf,
        in_buf,
        (ss, rs),
    )
    in_ref[...] = incoming
    for span in spans(width):
        copies = (span.stop - span.start) // LANES
        rates = rate_ref[:, span]

        def produce(block, state, span=span, copies=copies, rates=rates):
            rows = pl.ds(pl.multiple_of(block * 8, 8), 8)
            steps = step_ref[rows, span]
            drives = steps * act_ref[rows, span]
            keeps = wide(keep_ref[rows, :], copies)
            results = []
            for r in range(8):
                decay = jnp.exp(steps[r : r + 1] * rates) * keeps[r : r + 1]
                state = decay * state + drives[r : r + 1] * wide(b_ref[block * 8 + r], copies)
                results.append(
                    jnp.sum(state * wide(c_ref[block * 8 + r], copies), axis=0, keepdims=True)
                )
            y_ref[rows, span] = jnp.concatenate(results, axis=0)
            return state

        lax.fori_loop(0, tokens // 8, produce, in_ref[:, span])


def scan_scratch(width):
    laps = chain_laps()
    return [
        pltpu.VMEM((laps, STATE + 8, width), jnp.float32),
        pltpu.VMEM((laps, STATE + 8, width), jnp.float32),
        pltpu.SemaphoreType.DMA((laps,)),
        pltpu.SemaphoreType.DMA((laps,)),
    ]


def scan_forward(step, act, b_wide, c_wide, keep_wide, rates, collective_id):
    tokens, width = step.shape
    return pl.pallas_call(
        scan_forward_kernel,
        out_shape=(
            jax.ShapeDtypeStruct((tokens, width), jnp.float32),
            jax.ShapeDtypeStruct((STATE, width), jnp.float32),
        ),
        in_specs=[pl.BlockSpec(memory_space=pltpu.VMEM)] * 6,
        out_specs=(pl.BlockSpec(memory_space=pltpu.VMEM),) * 2,
        scratch_shapes=scan_scratch(width),
        compiler_params=pltpu.CompilerParams(
            collective_id=collective_id, has_side_effects=True, vmem_limit_bytes=VMEM_LIMIT
        ),
        name="scan_forward",
    )(step, act, b_wide, c_wide, keep_wide, rates)


def scan_backward_kernel(
    step_ref,
    act_ref,
    b_ref,
    c_ref,
    keep_ref,
    rate_ref,
    in_ref,
    grad_ref,
    along_ref,
    decayed_ref,
    gb_ref,
    gc_ref,
    grate_ref,
    prev_ref,
    carry_ref,
    out_buf,
    in_buf,
    ss,
    rs,
):
    meet(chain_peers())
    tokens, width = step_ref.shape
    blocks = tokens // 8
    ends = []
    for number, span in enumerate(spans(width)):
        size = span.stop - span.start
        copies = size // LANES
        rates = rate_ref[:, span]

        def replay(block, state, number=number, span=span, copies=copies, rates=rates):
            rows = pl.ds(pl.multiple_of(block * 8, 8), 8)
            steps = step_ref[rows, span]
            drives = steps * act_ref[rows, span]
            keeps = wide(keep_ref[rows, :], copies)
            grads = grad_ref[rows, span]
            for r in range(8):
                at = block * 8 + r
                prev_ref[at, :, span] = state
                decay = jnp.exp(steps[r : r + 1] * rates) * keeps[r : r + 1]
                state = decay * state + drives[r : r + 1] * wide(b_ref[at], copies)
                share = folded(grads[r : r + 1] * state)
                gc_ref[at] = share if number == 0 else gc_ref[at] + share
            return state

        lax.fori_loop(0, blocks, replay, in_ref[:, span])

        def pull(lap, carry, span=span, copies=copies, rates=rates):
            block = blocks - 1 - lap
            rows = pl.ds(pl.multiple_of(block * 8, 8), 8)
            steps = step_ref[rows, span]
            keeps = wide(keep_ref[rows, :], copies)
            grads = grad_ref[rows, span]
            for r in range(7, -1, -1):
                decay = jnp.exp(steps[r : r + 1] * rates) * keeps[r : r + 1]
                adjoint = grads[r : r + 1] * wide(c_ref[block * 8 + r], copies) + carry
                carry = decay * adjoint
            return carry

        ends.append(lax.fori_loop(0, blocks, pull, jnp.zeros((STATE, size), jnp.float32)))
    total_step = jnp.sum(step_ref[...], axis=0, keepdims=True)
    flag = wide(jnp.min(keep_ref[...], axis=0, keepdims=True), width // LANES)
    carry_ref[...] = chain_exchange(
        rate_ref[...],
        total_step,
        flag,
        jnp.concatenate(ends, axis=1),
        True,
        out_buf,
        in_buf,
        (ss, rs),
    )
    for number, span in enumerate(spans(width)):
        size = span.stop - span.start
        copies = size // LANES
        rates = rate_ref[:, span]

        def settle(lap, carries, number=number, span=span, copies=copies, rates=rates):
            carry, rate_total = carries
            block = blocks - 1 - lap
            rows = pl.ds(pl.multiple_of(block * 8, 8), 8)
            steps = step_ref[rows, span]
            drives = steps * act_ref[rows, span]
            keeps = wide(keep_ref[rows, :], copies)
            grads = grad_ref[rows, span]
            alongs, decays = ([None] * 8, [None] * 8)
            for r in range(7, -1, -1):
                at = block * 8 + r
                decay = jnp.exp(steps[r : r + 1] * rates) * keeps[r : r + 1]
                adjoint = grads[r : r + 1] * wide(c_ref[at], copies) + carry
                carry = decay * adjoint
                grad_exp = carry * prev_ref[at, :, span]
                rate_total = rate_total + grad_exp * steps[r : r + 1]
                alongs[r] = jnp.sum(adjoint * wide(b_ref[at], copies), axis=0, keepdims=True)
                decays[r] = jnp.sum(grad_exp * rates, axis=0, keepdims=True)
                share = folded(adjoint * drives[r : r + 1])
                gb_ref[at] = share if number == 0 else gb_ref[at] + share
            along_ref[rows, span] = jnp.concatenate(alongs, axis=0)
            decayed_ref[rows, span] = jnp.concatenate(decays, axis=0)
            return (carry, rate_total)

        _, rate_total = lax.fori_loop(
            0, blocks, settle, (carry_ref[:, span], jnp.zeros((STATE, size), jnp.float32))
        )
        grate_ref[:, span] = rate_total * rates


def scan_backward(step, act, b_wide, c_wide, keep_wide, rates, incoming, grad, collective_id):
    tokens, width = step.shape
    full = jax.ShapeDtypeStruct((tokens, width), jnp.float32)
    return pl.pallas_call(
        scan_backward_kernel,
        out_shape=(
            full,
            full,
            jax.ShapeDtypeStruct(b_wide.shape, jnp.float32),
            jax.ShapeDtypeStruct(c_wide.shape, jnp.float32),
            jax.ShapeDtypeStruct((STATE, width), jnp.float32),
        ),
        in_specs=[pl.BlockSpec(memory_space=pltpu.VMEM)] * 8,
        out_specs=(pl.BlockSpec(memory_space=pltpu.VMEM),) * 5,
        scratch_shapes=[
            pltpu.VMEM((tokens, STATE, width), jnp.float32),
            pltpu.VMEM((STATE, width), jnp.float32),
        ]
        + scan_scratch(width),
        compiler_params=pltpu.CompilerParams(
            collective_id=collective_id, has_side_effects=True, vmem_limit_bytes=VMEM_LIMIT
        ),
        name="scan_backward",
    )(step, act, b_wide, c_wide, keep_wide, rates, incoming, grad)


def everyone_peer_greeting():
    devices, groups, me = flat_place()
    greet_everyone(devices, groups, me)
    return (devices, groups, me)


def one_hot_turned(ids, height):
    numbers = lax.broadcasted_iota(jnp.int32, (height, ids.shape[1]), 0)
    return (numbers == ids).astype(jnp.float32).astype(jnp.bfloat16)


def start_kernel(
    sizes,
    pairs,
    pack_pairs,
    own_vocab,
    number_ref,
    pack_ref,
    turned_ref,
    numbers_ref,
    packs_ref,
    own_ref,
    full_ref,
    pack_sem,
    send_sem,
    recv_sem,
    *scratch,
):
    devices, groups, me = everyone_peer_greeting()
    place = my_place(sizes)
    seqs = sizes["x"] * sizes["core"]
    gather = Gather(sizes, pack_pairs, pack_ref, packs_ref, scratch[:8])
    scatter = Scatter(sizes, pairs, full_ref, own_ref, scratch[8:], False)
    own_pack = pltpu.make_async_copy(
        pack_ref, packs_ref.at[tuple(place[a] for a in NATURAL)], pack_sem
    )
    own_pack.start()

    def number_copy(by, address):
        return pltpu.make_async_remote_copy(
            src_ref=number_ref,
            dst_ref=numbers_ref.at[me],
            send_sem=send_sem.at[by],
            recv_sem=recv_sem.at[by],
            device_id=address,
            device_id_type=MESH,
        )

    def weights(turn):
        for phase in range(4, -1, -1):
            if 0 <= turn - phase < pack_pairs:
                gather.advance(turn - phase, phase)

    everyone(devices, groups, me, lambda by, peer, address: number_copy(by, address).start())
    weights(0)
    numbers_ref[me] = number_ref[...]
    own_pack.wait()
    everyone(devices, groups, me, lambda by, peer, address: number_copy(by, address).wait())
    weights(1)

    def look_up(step, carry):
        seq, group = (lax.div(step, groups // 2), lax.rem(step, groups // 2) * 2)
        x, core = seq_place(seq, sizes)
        ids = jnp.concatenate(
            [numbers_ref[group, pl.ds(seq, 1)], numbers_ref[group + 1, pl.ds(seq, 1)]], axis=1
        )
        found = one_hot_turned(ids - me * own_vocab, turned_ref.shape[1])
        rows = matmul(turned_ref[...], found).T.astype(jnp.bfloat16)
        tokens = number_ref.shape[1]
        for half in range(2):
            z, y = (lax.div(group + half, sizes["y"]), lax.rem(group + half, sizes["y"]))
            full_ref[x, core, z, y] = rows[half * tokens : (half + 1) * tokens]
        return carry

    chunks = seqs * groups // 2
    for part in range(4):
        lax.fori_loop(part * chunks // 4, (part + 1) * chunks // 4, look_up, 0)
        weights(2 + part)
    for pair in range(pairs):
        scatter.launch(pair, 0)
    for turn in range(max(pairs + 3, pack_pairs - 2)):
        weights(6 + turn)
        for phase in range(3, -1, -1):
            if 0 <= turn - phase < pairs:
                scatter.advance(turn - phase, phase)
    gather.finish()
    scatter.finish()


def start_all(numbers, pack, turned, own_vocab, collective_id):
    sizes = axis_sizes()
    natural = tuple(sizes[a] for a in NATURAL)
    devices = lax.axis_size("seq") * lax.axis_size("group")
    tokens = numbers.shape[1]
    pairs, pack_pairs = (tokens // SPAN, pack.shape[0] // SPAN)
    vmem = pl.BlockSpec(memory_space=pltpu.VMEM)
    return pl.pallas_call(
        functools.partial(start_kernel, sizes, pairs, pack_pairs, own_vocab),
        out_shape=(
            jax.ShapeDtypeStruct((devices,) + numbers.shape, numbers.dtype),
            jax.ShapeDtypeStruct(natural + pack.shape, pack.dtype),
            jax.ShapeDtypeStruct((tokens, D), jnp.float32),
        ),
        in_specs=[vmem] * 3,
        out_specs=(vmem, pl.BlockSpec(memory_space=pl.ANY), vmem),
        scratch_shapes=[
            pltpu.VMEM(natural + (tokens, D), jnp.bfloat16),
            pltpu.SemaphoreType.DMA,
            pltpu.SemaphoreType.DMA((devices,)),
            pltpu.SemaphoreType.DMA((devices,)),
        ]
        + gather_semaphores(sizes, pack_pairs)
        + scatter_scratch(sizes, pairs, D, False),
        compiler_params=pltpu.CompilerParams(
            collective_id=collective_id, has_side_effects=True, vmem_limit_bytes=VMEM_LIMIT
        ),
        name="start_all",
    )(numbers, pack, turned)


def finish_kernel(
    sizes,
    pairs,
    pack_pairs,
    own_ref,
    pack_ref,
    token_ref,
    head_ref,
    scalar_ref,
    tgrad_ref,
    quarters_ref,
    sums_ref,
    all_ref,
    found_ref,
    mine_ref,
    ring_ref,
    own_sem,
    quarter_send,
    quarter_recv,
    ring_send,
    ring_recv,
    *scratch,
):
    place = my_place(sizes)
    meet(line_peers(place, sizes))
    seqs = sizes["x"] * sizes["core"]
    groups = sizes["z"] * sizes["y"]
    block = groups * SPAN
    height = head_ref.shape[0]
    gather = Gather(sizes, pairs, own_ref, all_ref, scratch[:8])
    scatter = Scatter(sizes, pack_pairs, pack_ref, mine_ref, scratch[8:], True)
    keep_own = pltpu.make_async_copy(
        own_ref, all_ref.at[tuple(place[a] for a in NATURAL)], own_sem
    )
    keep_own.start()

    def spread_table(pair):
        for seq in range(seqs):
            ids = token_ref[pair * seqs + seq : pair * seqs + seq + 1]
            found_ref[:, seq * block : (seq + 1) * block] = one_hot_turned(ids, height)
        rows = all_ref[:, :, :, :, pl.ds(pair * SPAN, SPAN), :].reshape(seqs * block, D)
        update = matmul(found_ref[...], rows)
        tgrad_ref[...] = (head_ref[...] if pair == 0 else tgrad_ref[...]) + update

    for pair in range(pack_pairs):
        scatter.launch(pair, 0)
        for kind in range(2):
            scatter.kept(kind, pair).start()
    for turn in range(max(pairs + 4, pack_pairs + 3)):
        if 0 <= turn - 4 < pairs:
            gather.advance(turn - 4, 4)
        for phase in range(3, -1, -1):
            if 0 <= turn - phase < pairs:
                gather.advance(turn - phase, phase)
            if 0 <= turn - phase < pack_pairs:
                scatter.advance(turn - phase, phase)
        if turn == 0:
            keep_own.wait()
        if 0 <= turn - 4 < pairs:
            spread_table(turn - 4)

    seq = place["x"] * sizes["core"] + place["core"]
    quarters_ref[seq] = mine_ref[...].astype(jnp.bfloat16)
    started = []

    def send_quarters(axis, first):
        sent = []
        for by in range(1, sizes[axis]):
            to = moved(place, axis, by, sizes)
            for x in range(sizes["x"] if axis == "core" else 1):
                held = x * sizes["core"] + place["core"] if axis == "core" else seq
                number = first + len(sent)
                copy = pltpu.make_async_remote_copy(
                    src_ref=quarters_ref.at[held],
                    dst_ref=quarters_ref.at[held],
                    send_sem=quarter_send.at[number],
                    recv_sem=quarter_recv.at[number],
                    device_id=device_of(to, sizes),
                    device_id_type=MESH,
                )
                copy.start()
                sent.append(copy)
        started.extend(sent)
        return sent

    x_sent = send_quarters("x", 0)
    square = jnp.sum(tgrad_ref[...] * tgrad_ref[...]) + jnp.sum(mine_ref[...] * mine_ref[...])
    row = lax.broadcasted_iota(jnp.int32, (8, LANES), 0)
    value = scalar_ref[...] + jnp.where(row < 4, square, 0.0)
    core_sent = []
    first = 0
    for axis in ("core", "x", "y", "z"):
        ring_ref[first + place[axis]] = value
        sent = []
        for by in range(1, sizes[axis]):
            copy = pltpu.make_async_remote_copy(
                src_ref=ring_ref.at[first + place[axis]],
                dst_ref=ring_ref.at[first + place[axis]],
                send_sem=ring_send.at[first + by],
                recv_sem=ring_recv.at[first + by],
                device_id=device_of(moved(place, axis, by, sizes), sizes),
                device_id_type=MESH,
            )
            copy.start()
            sent.append(copy)
        started.extend(sent)
        if axis == "y":
            for copy in x_sent:
                copy.wait_recv()
            core_sent = send_quarters("core", len(x_sent))
        for copy in sent:
            copy.wait_recv()
        value = ring_ref[first]
        for other in range(1, sizes[axis]):
            value = value + ring_ref[first + other]
        first += sizes[axis]
    sums_ref[...] = value
    for copy in core_sent:
        copy.wait_recv()
    for copy in started:
        copy.wait_send()
    gather.finish()
    scatter.finish()


def finish_all(rows, packs, token_rows, head_grad, scalars, collective_id):
    sizes = axis_sizes()
    natural = tuple(sizes[a] for a in NATURAL)
    tokens = rows.shape[0]
    seqs = sizes["x"] * sizes["core"]
    pack_rows, pack_width = packs.shape[-2:]
    pairs, pack_pairs = (tokens // SPAN, pack_rows // SPAN)
    slots = sum(sizes.values())
    quarter_copies = (sizes["x"] - 1) + (sizes["core"] - 1) * sizes["x"] + 1
    vmem = pl.BlockSpec(memory_space=pltpu.VMEM)
    return pl.pallas_call(
        functools.partial(finish_kernel, sizes, pairs, pack_pairs),
        out_shape=(
            jax.ShapeDtypeStruct(head_grad.shape, jnp.float32),
            jax.ShapeDtypeStruct((seqs, pack_rows, pack_width), jnp.bfloat16),
            jax.ShapeDtypeStruct((8, LANES), jnp.float32),
        ),
        in_specs=[vmem, pl.BlockSpec(memory_space=pl.ANY), vmem, vmem, vmem],
        out_specs=(vmem,) * 3,
        scratch_shapes=[
            pltpu.VMEM(natural + rows.shape, jnp.bfloat16),
            pltpu.VMEM((head_grad.shape[0], seqs * token_rows.shape[1]), jnp.bfloat16),
            pltpu.VMEM((pack_rows, pack_width), jnp.float32),
            pltpu.VMEM((slots, 8, LANES), jnp.float32),
            pltpu.SemaphoreType.DMA,
            pltpu.SemaphoreType.DMA((quarter_copies,)),
            pltpu.SemaphoreType.DMA((quarter_copies,)),
            pltpu.SemaphoreType.DMA((slots,)),
            pltpu.SemaphoreType.DMA((slots,)),
        ]
        + gather_semaphores(sizes, pairs)
        + scatter_scratch(sizes, pack_pairs, pack_width, True),
        compiler_params=pltpu.CompilerParams(
            collective_id=collective_id, has_side_effects=True, vmem_limit_bytes=VMEM_LIMIT
        ),
        name="finish_all",
    )(rows, packs.reshape(natural + (pack_rows, pack_width)), token_rows, head_grad, scalars)


def own_pack_of(parts, seq_index, seq_count):
    mixer_in, mixer_x, mixer_out, channel, gains, router = [
        part.astype(jnp.bfloat16) for part in parts
    ]
    tall, wide_rows = (mixer_in.shape[0], mixer_x.shape[0] // seq_count)
    sides = jnp.pad(
        jnp.concatenate([router, gains.T], axis=1),
        ((0, 0), (0, LANES - router.shape[1] - gains.shape[0])),
    )
    top = jnp.concatenate(
        [lax.dynamic_slice_in_dim(mixer_in, seq_index * D, D, 1), sides], axis=1
    )
    middle = jnp.concatenate(
        [
            lax.dynamic_slice_in_dim(mixer_out, seq_index * wide_rows, wide_rows, 0),
            lax.dynamic_slice_in_dim(mixer_x, seq_index * wide_rows, wide_rows, 0),
        ],
        axis=1,
    )
    bottom = channel_tiles(
        lax.dynamic_slice_in_dim(channel, seq_index * wide_rows, wide_rows, 1)
    )
    return jnp.concatenate([top, middle, bottom])


def channel_tiles(channel):
    lead = [(0, 0)] * (channel.ndim - 2)
    rows, width = channel.shape[-2:]
    first = jnp.pad(channel[..., :16, :], lead + [(0, 0), (0, LANES - width)])
    second = jnp.pad(channel[..., 16:, :], lead + [(0, 32 - rows), (0, D - width)])
    return jnp.concatenate([first, second], axis=-1)


def weights_of(packs, experts_total):
    seqs, groups = packs.shape[:2]
    tall, wide_rows = (D // groups, DI // (seqs * groups))
    top, middle = (packs[:, :, :tall], packs[:, :, tall : tall + wide_rows])
    bottom = packs[:, :, tall + wide_rows :]
    weight_in = top[..., :D].transpose(1, 2, 0, 3).reshape(D, -1)
    sides = top[0, :, :, D:].reshape(D, LANES)
    weight_out = middle[..., :D].transpose(1, 0, 2, 3).reshape(-1, D)
    weight_x = middle[..., D:].transpose(1, 0, 2, 3).reshape(-1, LANES)
    rows = CONV + 3 + STATE
    channel = jnp.concatenate(
        [
            bottom[..., :16, :wide_rows].transpose(2, 1, 0, 3).reshape(16, -1),
            bottom[..., : rows - 16, LANES : LANES + wide_rows]
            .transpose(2, 1, 0, 3)
            .reshape(rows - 16, -1),
        ]
    )
    router = sides[:, :experts_total]
    gains = sides[:, experts_total : experts_total + 3].T
    return (weight_in, weight_x, weight_out, channel, gains, router)


def grad_packs(parts, seqs, groups):
    grad_in, grad_x, grad_out, grad_channel, grad_gains, grad_router = [
        part.astype(jnp.bfloat16) for part in parts
    ]
    tall, wide_rows = (D // groups, DI // (seqs * groups))
    sides = jnp.pad(
        jnp.concatenate([grad_router, grad_gains.T], axis=1),
        ((0, 0), (0, LANES - grad_router.shape[1] - grad_gains.shape[0])),
    ).reshape(1, groups, tall, LANES)
    sides = jnp.pad(sides, ((0, seqs - 1), (0, 0), (0, 0), (0, 0)))
    top = jnp.concatenate(
        [grad_in.reshape(groups, tall, seqs, D).transpose(2, 0, 1, 3), sides], axis=3
    )
    middle = jnp.concatenate(
        [
            part.reshape(groups, seqs, wide_rows, part.shape[1]).transpose(1, 0, 2, 3)
            for part in (grad_out, grad_x)
        ],
        axis=3,
    )
    rows = grad_channel.shape[0]
    bottom = channel_tiles(
        grad_channel.reshape(rows, groups, seqs, wide_rows).transpose(2, 1, 0, 3)
    )
    return jnp.concatenate([top, middle, bottom], axis=2)


def own_grads_of(quarters, experts_total):
    seqs, _, width = quarters.shape
    tall = quarters.shape[1] - 16 - DI // (seqs * lax.axis_size("group"))
    wide_rows = quarters.shape[1] - 16 - tall
    values = quarters.astype(jnp.float32)
    top, middle = (values[:, :tall], values[:, tall : tall + wide_rows])
    bottom = values[:, tall + wide_rows :]
    grad_in = top[..., :D].transpose(1, 0, 2).reshape(tall, -1)
    sides = top[0, :, D:]
    grad_out = middle[..., :D].reshape(-1, D)
    grad_x = middle[..., D:].reshape(-1, LANES)
    rows = CONV + 3 + STATE
    grad_channel = jnp.concatenate(
        [
            bottom[:, :16, :wide_rows].transpose(1, 0, 2).reshape(16, -1),
            bottom[:, : rows - 16, LANES : LANES + wide_rows]
            .transpose(1, 0, 2)
            .reshape(rows - 16, -1),
        ]
    )
    return (
        grad_in,
        grad_x,
        grad_out,
        grad_channel,
        sides[:, experts_total : experts_total + 3].T,
        sides[:, :experts_total],
    )


def from_behind(value, axis, by):
    devices = lax.axis_size(axis)
    pairs = [(i, i + by) for i in range(devices) if 0 <= i + by < devices]
    return lax.ppermute(value, axis, pairs)


def matmul(left, right):
    return jnp.dot(left, right, preferred_element_type=jnp.float32)


def matmul_nt(left, right):
    return lax.dot_general(
        left, right, (((1,), (1,)), ((), ())), preferred_element_type=jnp.float32
    )


def matmul_tn(left, right):
    return lax.dot_general(
        left, right, (((0,), (0,)), ((), ())), preferred_element_type=jnp.float32
    )


def silu_slope(preact):
    logistic = jax.nn.sigmoid(preact)
    return logistic * (1.0 + preact * (1.0 - logistic))


def inverse_rms(values):
    return lax.rsqrt(jnp.mean(values * values, axis=-1, keepdims=True) + EPS)


def norm_back(values, inv_scale, gain_row, grad_in):
    scaled = grad_in * gain_row
    grad_gain = jnp.sum(grad_in * values * inv_scale, axis=0)
    grad_values = inv_scale * scaled - values * inv_scale**3 * jnp.mean(
        scaled * values, axis=-1, keepdims=True
    )
    return (grad_values, grad_gain)


def neighbour_rows(edge_rows, offset):
    return from_behind(edge_rows, "group", offset)


def doc_layout(doc_lengths, first_pos, span_len):
    doc_ends = jnp.cumsum(doc_lengths, axis=1)
    doc_begins = doc_ends - doc_lengths
    where_at = first_pos + jnp.arange(span_len, dtype=jnp.int32)
    segment = jnp.sum((where_at[None, :, None] >= doc_ends[:, None, :]).astype(jnp.int32), axis=2)
    onehot_doc = (
        segment[:, :, None] == jnp.arange(doc_lengths.shape[1], dtype=jnp.int32)[None, None, :]
    ).astype(jnp.float32)
    weight = jnp.sum(onehot_doc / doc_lengths[:, None, :].astype(jnp.float32), axis=2)
    starting = jnp.sum(
        (where_at[None, :, None] == doc_begins[:, None, :]).astype(jnp.float32), axis=2
    )
    return (segment, weight, 1.0 - starting)


def lane_copies(columns):
    return jnp.broadcast_to(columns[..., None], columns.shape + (LANES,))


def mixer_forward(embedded, segment, keeping, weight_in, weight_x, weight_out, channel, gain_row):
    tokens = embedded.shape[0]
    scale_in = inverse_rms(embedded)
    normed = (embedded * scale_in * gain_row).astype(jnp.bfloat16)
    projected_in = matmul(normed, weight_in)
    conv_input = projected_in[:, :DI].astype(jnp.bfloat16)
    gate_z = projected_in[:, DI:]
    rim_rows = neighbour_rows(conv_input[tokens - CONV + 1 :].astype(jnp.float32), 1)
    padded = jnp.concatenate([rim_rows, conv_input.astype(jnp.float32)])
    same_doc = [
        (segment[conv_tap : conv_tap + tokens] == segment[CONV - 1 :]).astype(jnp.float32)[:, None]
        for conv_tap in range(CONV)
    ]
    conv_out = channel[CONV] + jnp.zeros_like(padded[CONV - 1 :])
    for conv_tap in range(CONV):
        conv_out = (
            conv_out + channel[conv_tap] * padded[conv_tap : conv_tap + tokens] * same_doc[conv_tap]
        )
    activated = jax.nn.silu(conv_out)
    act_low = activated.astype(jnp.bfloat16)
    projected = matmul(act_low, weight_x[:, : RANK + 2 * STATE])
    dt_input = projected[:, :RANK].astype(jnp.bfloat16)
    dt_pre = matmul_nt(dt_input, weight_x[:, RANK + 2 * STATE :])
    step_size = jax.nn.softplus(dt_pre + channel[CONV + 1])
    decay_rates = -jnp.exp(channel[CONV + 3 :])
    b_wide = lane_copies(projected[:, RANK : RANK + STATE])
    c_wide = lane_copies(projected[:, RANK + STATE :])
    keep_wide = lane_copies(keeping)
    reached, incoming = scan_forward(
        step_size, activated, b_wide, c_wide, keep_wide, decay_rates, 4
    )
    scanned = reached + channel[CONV + 2] * activated
    gate_act = jax.nn.silu(gate_z)
    gated = (scanned * gate_act).astype(jnp.bfloat16)
    mixed_out = embedded + matmul(gated, weight_out)
    kept_values = (
        scale_in,
        normed,
        gate_z,
        padded,
        same_doc,
        conv_out,
        activated,
        act_low,
        b_wide,
        c_wide,
        keep_wide,
        dt_input,
        dt_pre,
        step_size,
        decay_rates,
        incoming,
        scanned,
        gate_act,
        gated,
    )
    return (mixed_out, kept_values)


def mixer_backward(
    grad_out, embedded, kept_values, weight_in, weight_x, weight_out, channel, gain_row
):
    (
        scale_in,
        normed,
        gate_z,
        padded,
        same_doc,
        conv_out,
        activated,
        act_low,
        b_wide,
        c_wide,
        keep_wide,
        dt_input,
        dt_pre,
        step_size,
        decay_rates,
        incoming,
        scanned,
        gate_act,
        gated,
    ) = kept_values
    tokens = embedded.shape[0]
    grad_low = grad_out.astype(jnp.bfloat16)
    grad_wout = matmul_tn(gated, grad_low)
    grad_gated = matmul_nt(grad_low, weight_out)
    grad_scan = grad_gated * gate_act
    grad_z = grad_gated * scanned * silu_slope(gate_z)
    grad_skip = jnp.sum(grad_scan * activated, axis=0)
    along_b, decayed, wide_gb, wide_gc, grad_rates_log = scan_backward(
        step_size, activated, b_wide, c_wide, keep_wide, decay_rates, incoming, grad_scan, 5
    )
    grad_b = jnp.sum(wide_gb, axis=2)
    grad_c = jnp.sum(wide_gc, axis=2)
    grad_act = grad_scan * channel[CONV + 2] + along_b * step_size
    grad_step = decayed + along_b * activated
    grad_dtpre = grad_step * jax.nn.sigmoid(dt_pre + channel[CONV + 1])
    grad_dtbias = jnp.sum(grad_dtpre, axis=0)
    grad_dtlow = grad_dtpre.astype(jnp.bfloat16)
    grad_wdt = matmul_tn(grad_dtlow, dt_input)
    grad_dtin = matmul(grad_dtlow, weight_x[:, RANK + 2 * STATE :])
    grad_proj = jnp.concatenate([grad_dtin, grad_b, grad_c], axis=1).astype(jnp.bfloat16)
    grad_wx = jnp.concatenate([matmul_tn(act_low, grad_proj), grad_wdt], axis=1)
    grad_act = grad_act + matmul_nt(grad_proj, weight_x[:, : RANK + 2 * STATE])
    grad_conv = grad_act * silu_slope(conv_out)
    grad_taps = [
        jnp.sum(grad_conv * padded[conv_tap : conv_tap + tokens] * same_doc[conv_tap], axis=0)
        for conv_tap in range(CONV)
    ]
    grad_padded = sum(
        (
            jnp.pad(
                channel[conv_tap] * grad_conv * same_doc[conv_tap],
                ((conv_tap, CONV - 1 - conv_tap), (0, 0)),
            )
            for conv_tap in range(CONV)
        )
    )
    from_next = neighbour_rows(grad_padded[: CONV - 1], -1)
    grad_input = grad_padded[CONV - 1 :] + jnp.pad(from_next, ((tokens - CONV + 1, 0), (0, 0)))
    grad_both = jnp.concatenate([grad_input, grad_z], axis=1).astype(jnp.bfloat16)
    grad_win = matmul_tn(normed, grad_both)
    grad_normed = matmul_nt(grad_both, weight_in)
    grad_embed, grad_gain = norm_back(embedded, scale_in, gain_row, grad_normed)
    grad_channel = jnp.concatenate(
        [
            jnp.stack(grad_taps),
            jnp.sum(grad_conv, axis=0)[None],
            grad_dtbias[None],
            grad_skip[None],
            grad_rates_log,
        ]
    )
    return (grad_out + grad_embed, grad_win, grad_wx, grad_wout, grad_channel, grad_gain)


def choice_of(route_flat, experts_total):
    return (route_flat[:, None] == jnp.arange(experts_total, dtype=jnp.int32)[None, :]).astype(
        jnp.float32
    )


def dispatch_table(routes, first_expert, experts_here, capacity):
    tokens = routes.shape[1]
    chosen = (
        routes[:, :, None] == first_expert + jnp.arange(experts_here, dtype=jnp.int32)
    ).astype(jnp.float32)
    earlier = jnp.cumsum(chosen, axis=1) - chosen
    rank = jnp.sum(earlier * chosen, axis=2).astype(jnp.int32)
    local = routes - first_expert
    slot = jnp.where((local >= 0) & (local < experts_here), local * capacity + rank, -1)
    return (
        slot[:, None, :] == jnp.arange(experts_here * capacity, dtype=jnp.int32)[None, :, None]
    ).astype(jnp.bfloat16)


def to_slots(select, rows, experts_here, capacity):
    slots = jnp.einsum("bst,btd->bsd", select, rows, preferred_element_type=jnp.float32)
    slots = slots.astype(jnp.bfloat16).reshape(-1, experts_here, capacity, D)
    return jnp.swapaxes(slots, 0, 1).reshape(experts_here, -1, D)


def to_rows(select, slots, capacity):
    experts_here = slots.shape[0]
    slots = slots.astype(jnp.bfloat16).reshape(experts_here, -1, capacity, D)
    slots = jnp.swapaxes(slots, 0, 1).reshape(-1, experts_here * capacity, D)
    return jnp.einsum("bst,bsd->btd", select, slots, preferred_element_type=jnp.float32).astype(
        jnp.bfloat16
    )


def packed_rows(arrays, devices_seq):
    flat = jnp.concatenate([part.reshape(-1) for part in arrays])
    unit = devices_seq * SPAN * D
    size = -(-flat.shape[0] // unit) * unit
    return jnp.pad(flat, (0, size - flat.shape[0])).reshape(-1, D)


def unpacked(flat, shapes):
    parts, first = ([], 0)
    for shape in shapes:
        size = 1
        for extent in shape:
            size *= extent
        parts.append(flat[..., first : first + size].reshape(flat.shape[:-1] + shape))
        first += size
    return parts


def whole_of(shards, axis):
    moved_axis = jnp.moveaxis(shards, 0, axis)
    shape = moved_axis.shape
    return moved_axis.reshape(shape[:axis] + (shape[axis] * shape[axis + 1],) + shape[axis + 2 :])


def shards_of(whole, axis, count):
    shape = whole.shape
    split = whole.reshape(shape[:axis] + (count, shape[axis] // count) + shape[axis + 1 :])
    return jnp.moveaxis(split, axis, 0)


def renewed(master, moment, average, gradient, clip_factor, rate):
    scaled = clip_factor * gradient
    moment_new = MOMENTUM * moment + scaled
    master_new = master - rate * (scaled + MOMENTUM * moment_new)
    return (master_new, moment_new, EMA_KEEP * average + (1.0 - EMA_KEEP) * master_new)


def per_device(
    token_ids,
    target_ids,
    doc_lengths,
    expert_ids,
    vocab_table,
    vocab_table_mom,
    vocab_table_ema,
    mixer_in,
    mixer_in_mom,
    mixer_in_ema,
    mixer_x,
    mixer_x_mom,
    mixer_x_ema,
    mixer_out,
    mixer_out_mom,
    mixer_out_ema,
    channel,
    channel_mom,
    channel_ema,
    norm_gains,
    norm_gains_mom,
    norm_gains_ema,
    router,
    router_mom,
    router_ema,
    experts,
    experts_mom,
    experts_ema,
):
    seq_count = lax.axis_size("seq")
    group_count = lax.axis_size("group")
    seq_index = lax.axis_index("seq")
    group_index = lax.axis_index("group")
    devices = seq_count * group_count
    tokens = token_ids.shape[1]
    sequences = token_ids.shape[0]
    experts_total = router.shape[1]
    local_experts = experts.shape[1]
    capacity = max(2, 2 * tokens // experts_total)
    own_vocab = vocab_table.shape[0]
    routes = expert_ids.reshape(1, tokens)
    numbers = jnp.concatenate([token_ids, target_ids, routes])
    numbers = jnp.pad(numbers, ((0, -numbers.shape[0] % 8), (0, 0)))
    mixer_parts = (mixer_in, mixer_x, mixer_out, channel, norm_gains, router)
    part_axes = (0, 0, 0, 1, 1, 0)
    part_shapes = [part.shape for part in mixer_parts]
    table_low = vocab_table.astype(jnp.bfloat16)
    experts_low = experts.astype(jnp.bfloat16)
    up_weight, down_weight = (experts_low[0], experts_low[1])
    vocab_start = (seq_index * group_count + group_index) * own_vocab
    column_ids = jnp.arange(own_vocab, dtype=jnp.int32)
    wide_rows = DI // (seq_count * group_count)
    compact = devices * tokens <= 4096 and 2 * DI == seq_count * D
    if compact:
        table_turned = jnp.pad(table_low.T, ((0, 0), (0, -own_vocab % LANES)))
        own_pack = own_pack_of(mixer_parts, seq_index, seq_count)
        numbers_all, packs, embedded = start_all(numbers, own_pack, table_turned, own_vocab, 1)
        packs = packs.reshape((seq_count, group_count) + own_pack.shape)
        weight_in, weight_x, weight_out, channel_low, gains_low, router_low = weights_of(
            packs, experts_total
        )
    else:
        numbers_all = share_small(numbers, 1)
    from_groups = jnp.swapaxes(numbers_all[:group_count, : 2 * sequences], 0, 1)
    tokens_all = from_groups[:sequences].reshape(-1)
    targets_all = from_groups[sequences:].reshape(-1)
    routes_all = numbers_all[:, 2 * sequences]
    if not compact:
        pack = packed_rows([part.astype(jnp.bfloat16) for part in mixer_parts], seq_count)
        pack_rows = pack.shape[0] // seq_count
        own_pack = lax.dynamic_slice_in_dim(pack, seq_index * pack_rows, pack_rows, 0)
        packs = gather_all(own_pack, 2).reshape(seq_count, group_count, pack_rows * D)
        shards = unpacked(jnp.swapaxes(packs, 0, 1).reshape(group_count, -1), part_shapes)
        weight_in, weight_x, weight_out, channel_low, gains_low, router_low = [
            whole_of(shard, axis) for shard, axis in zip(shards, part_axes)
        ]
        held_token = (tokens_all - vocab_start)[:, None] == column_ids[None, :]
        held_token = held_token.astype(jnp.bfloat16)
        looked_up = matmul(held_token, table_low).astype(jnp.bfloat16)
        embedded = scatter_all(looked_up.reshape(devices, tokens, D), 3)
    channel_vals = channel_low.astype(jnp.float32)
    gain_vals = gains_low.astype(jnp.float32)

    segment_all, weight_all, keep_all = doc_layout(
        doc_lengths, group_index * tokens - CONV + 1, tokens + CONV - 1
    )
    own_segment = lax.dynamic_index_in_dim(segment_all, seq_index, 0, keepdims=False)
    keeping = lax.dynamic_index_in_dim(keep_all, seq_index, 0, keepdims=False)[CONV - 1 :]
    own_weight = lax.dynamic_index_in_dim(weight_all, seq_index, 0, keepdims=False)[CONV - 1 :]
    _, every_weight, _ = doc_layout(doc_lengths, 0, tokens * group_count)
    row_weight = every_weight.reshape(-1)
    mixed_out, kept_values = mixer_forward(
        embedded, own_segment, keeping, weight_in, weight_x, weight_out, channel_vals, gain_vals[0]
    )
    scale_mid = inverse_rms(mixed_out)
    moe_in = (mixed_out * scale_mid * gain_vals[1]).astype(jnp.bfloat16)
    chosen = choice_of(expert_ids.reshape(-1), experts_total)
    select = dispatch_table(routes_all, seq_index * local_experts, local_experts, capacity)
    probability = jax.nn.softmax(matmul(moe_in, router_low), axis=-1)
    gate_value = jnp.sum(probability * chosen, axis=1)
    arrived = to_slots(select, gather_all(moe_in, 6), local_experts, capacity)
    before = jnp.einsum("erd,efd->erf", arrived, up_weight, preferred_element_type=jnp.float32)
    inner_act = jax.nn.gelu(before).astype(jnp.bfloat16)
    partial_out = jnp.einsum(
        "erf,efd->erd", inner_act, down_weight, preferred_element_type=jnp.float32
    )
    returned = scatter_all(to_rows(select, partial_out, capacity), 3)
    expert_value = returned.astype(jnp.bfloat16).astype(jnp.float32)
    branch = gate_value[:, None] * expert_value
    hidden = mixed_out + branch
    scale_out = inverse_rms(hidden)
    final_low = (hidden * scale_out * gain_vals[2]).astype(jnp.bfloat16)
    if compact:

        def spread(values):
            split = values.reshape(seq_count, group_count, tokens // SPAN, SPAN)
            return split.transpose(2, 0, 1, 3).reshape(-1, group_count * SPAN)

        table_padded = jnp.pad(table_low, ((0, -own_vocab % 16), (0, 0)))
        target_local = targets_all - vocab_start
        target_local = spread(jnp.where(target_local < own_vocab, target_local, -1))
        all_final, stats = head_forward(final_low, table_padded, own_vocab, target_local, 7)
        own_entropy = (stats[0] - stats[1]).reshape(-1, seq_count, group_count, SPAN)
        own_entropy = lax.dynamic_index_in_dim(own_entropy, seq_index, 1, keepdims=False)
        own_entropy = lax.dynamic_index_in_dim(own_entropy, group_index, 1, keepdims=False)
        loss_part = jnp.sum(own_weight * own_entropy.reshape(-1))
        grad_final, table_grad = head_backward(
            all_final,
            table_padded,
            table_turned,
            own_vocab,
            target_local,
            stats[0],
            spread(row_weight),
            10,
        )
    else:
        all_final = gather_all(final_low, 6).reshape(devices * tokens, D)
        valid_cols = vocab_start + column_ids < VOCAB_REAL
        hit_target = (targets_all - vocab_start)[:, None] == column_ids[None, :]
        logits = jnp.where(valid_cols[None, :], matmul_nt(all_final, table_low), -1e30)
        largest = jnp.max(logits, axis=1)
        exp_total = jnp.sum(jnp.exp(logits - largest[:, None]), axis=1)
        picked = jnp.sum(jnp.where(hit_target, logits, 0.0), axis=1)
        parts = jnp.stack([largest, exp_total, picked]).reshape(3, devices, tokens)
        parts = jnp.pad(jnp.swapaxes(parts, 0, 1), ((0, 0), (0, 5), (0, 0)))
        levels, entropy = combine_stats(parts, 7)
        log_total = levels[:, 0].reshape(-1)
        loss_part = jnp.sum(own_weight * entropy[0])
        grad_logits = (
            row_weight[:, None]
            * (jnp.exp(logits - log_total[:, None]) - hit_target.astype(jnp.float32))
        ).astype(jnp.bfloat16)
        table_grad = matmul_tn(grad_logits, all_final)
        grad_rows = matmul(grad_logits, table_low).astype(jnp.bfloat16)
        grad_final = scatter_all(grad_rows.reshape(devices, tokens, D), 3)
    grad_hidden, grad_gain_out = norm_back(hidden, scale_out, gain_vals[2], grad_final)
    grad_gate = jnp.sum(grad_hidden * expert_value, axis=1)
    grad_expert = (gate_value[:, None] * grad_hidden).astype(jnp.bfloat16)
    grad_arrived = to_slots(select, gather_all(grad_expert, 6), local_experts, capacity)
    grad_inner = jnp.einsum(
        "erd,efd->erf", grad_arrived, down_weight, preferred_element_type=jnp.float32
    )
    grad_before = jax.vjp(jax.nn.gelu, before)[1](grad_inner)[0].astype(jnp.bfloat16)
    grad_down = jnp.einsum(
        "erf,erd->efd", inner_act, grad_arrived, preferred_element_type=jnp.float32
    )
    grad_up = jnp.einsum("erf,erd->efd", grad_before, arrived, preferred_element_type=jnp.float32)
    grad_part = jnp.einsum(
        "erf,efd->erd", grad_before, up_weight, preferred_element_type=jnp.float32
    )
    grad_moe_in = scatter_all(to_rows(select, grad_part, capacity), 3)
    grad_moe_in = grad_moe_in.astype(jnp.bfloat16).astype(jnp.float32)
    grad_router_logits = (grad_gate * gate_value)[:, None] * (chosen - probability)
    grad_moe_in = grad_moe_in + jnp.dot(
        grad_router_logits, router_low.astype(jnp.float32).T, precision=HIGHEST
    )
    grad_router = jnp.dot(moe_in.astype(jnp.float32).T, grad_router_logits, precision=HIGHEST)
    grad_mid, grad_gain_mid = norm_back(mixed_out, scale_mid, gain_vals[1], grad_moe_in)
    grad_mixed = grad_hidden + grad_mid
    grad_embedded, grad_win, grad_wx, grad_wout, grad_channel, grad_gain_in = mixer_backward(
        grad_mixed,
        embedded,
        kept_values,
        weight_in,
        weight_x,
        weight_out,
        channel_vals,
        gain_vals[0],
    )
    grad_gains = jnp.stack([grad_gain_in, grad_gain_mid, grad_gain_out])
    mixer_wholes = (grad_win, grad_wx, grad_wout, grad_channel, grad_gains, grad_router)
    grad_experts = jnp.stack([grad_up, grad_down])
    experts_square = jnp.sum(grad_experts * grad_experts)
    if compact:
        token_local = tokens_all - vocab_start
        token_local = spread(jnp.where(token_local < own_vocab, token_local, -1))
        scalars = jnp.concatenate(
            [jnp.full((4, LANES), experts_square), jnp.full((4, LANES), loss_part)], axis=0
        )
        table_grad, quarters, sums = finish_all(
            grad_embedded.astype(jnp.bfloat16),
            grad_packs(mixer_wholes, seq_count, group_count),
            token_local,
            table_grad,
            scalars,
            9,
        )
        table_grad = table_grad[:own_vocab]
        mixer_grads = own_grads_of(quarters, experts_total)
    else:
        all_grad_embed = gather_all(grad_embedded.astype(jnp.bfloat16), 6).reshape(-1, D)
        table_grad = table_grad + matmul_tn(held_token, all_grad_embed)
        wholes_low = [
            shards_of(whole.astype(jnp.bfloat16), axis, group_count).reshape(group_count, -1)
            for whole, axis in zip(mixer_wholes, part_axes)
        ]
        flat = jnp.concatenate(wholes_low, axis=1)
        flat = jnp.pad(flat, ((0, 0), (0, seq_count * pack_rows * D - flat.shape[1])))
        flat = jnp.swapaxes(flat.reshape(group_count, seq_count, pack_rows, D), 0, 1)
        own_quarter = scatter_all(flat.reshape(devices, pack_rows, D), 8)
        quarters = lax.all_gather(own_quarter, "seq", axis=0, tiled=True).reshape(-1)
        mixer_grads = unpacked(quarters, part_shapes)
        local_square = (
            jnp.sum(table_grad * table_grad) + experts_square + jnp.sum(own_quarter * own_quarter)
        )
        two = jnp.concatenate(
            [jnp.full((4, LANES), local_square), jnp.full((4, LANES), loss_part)], axis=0
        )
        sums = jnp.sum(share_small(two, 9), axis=0)
    total_square, loss_sum = (sums[0, 0], sums[4, 0])
    grad_norm = jnp.sqrt(total_square)
    clip_factor = jnp.minimum(1.0, CLIP / (grad_norm + 1e-06))
    table_new = renewed(
        vocab_table, vocab_table_mom, vocab_table_ema, table_grad, clip_factor, LRATE
    )
    in_new = renewed(mixer_in, mixer_in_mom, mixer_in_ema, mixer_grads[0], clip_factor, LRATE)
    x_new = renewed(mixer_x, mixer_x_mom, mixer_x_ema, mixer_grads[1], clip_factor, LRATE)
    out_new = renewed(mixer_out, mixer_out_mom, mixer_out_ema, mixer_grads[2], clip_factor, LRATE)
    channel_new = renewed(
        channel, channel_mom, channel_ema, mixer_grads[3], clip_factor, CHANNEL_LRATE
    )
    gains_new = renewed(
        norm_gains, norm_gains_mom, norm_gains_ema, mixer_grads[4], clip_factor, LRATE
    )
    router_new = renewed(router, router_mom, router_ema, mixer_grads[5], clip_factor, LRATE)
    experts_new = renewed(experts, experts_mom, experts_ema, grad_experts, clip_factor, LRATE)
    return (
        loss_sum,
        grad_norm,
        branch.reshape(1, tokens, D),
        table_new[0],
        table_new[1],
        table_new[2],
        in_new[0],
        in_new[1],
        in_new[2],
        x_new[0],
        x_new[1],
        x_new[2],
        out_new[0],
        out_new[1],
        out_new[2],
        channel_new[0],
        channel_new[1],
        channel_new[2],
        gains_new[0],
        gains_new[1],
        gains_new[2],
        router_new[0],
        router_new[1],
        router_new[2],
        experts_new[0],
        experts_new[1],
        experts_new[2],
    )


def solution(mesh):
    placed = (
        P(None, "group"),
        P(None, "group"),
        P(),
        P("seq", "group", None),
        P(("seq", "group"), None),
        P(("seq", "group"), None),
        P(("seq", "group"), None),
        P("group", None),
        P("group", None),
        P("group", None),
        P("group", None),
        P("group", None),
        P("group", None),
        P("group", None),
        P("group", None),
        P("group", None),
        P(None, "group"),
        P(None, "group"),
        P(None, "group"),
        P(None, "group"),
        P(None, "group"),
        P(None, "group"),
        P("group", None),
        P("group", None),
        P("group", None),
        P(None, "seq", "group", None),
        P(None, "seq", "group", None),
        P(None, "seq", "group", None),
    )
    return jax.shard_map(
        per_device,
        mesh=mesh,
        in_specs=placed,
        out_specs=(
            P(),
            P(),
            P("seq", "group", None),
            P(("seq", "group"), None),
            P(("seq", "group"), None),
            P(("seq", "group"), None),
            P("group", None),
            P("group", None),
            P("group", None),
            P("group", None),
            P("group", None),
            P("group", None),
            P("group", None),
            P("group", None),
            P("group", None),
            P(None, "group"),
            P(None, "group"),
            P(None, "group"),
            P(None, "group"),
            P(None, "group"),
            P(None, "group"),
            P("group", None),
            P("group", None),
            P("group", None),
            P(None, "seq", "group", None),
            P(None, "seq", "group", None),
            P(None, "seq", "group", None),
        ),
        check_vma=False,
    )
```

profile of v0, /device:TPU:0, one launch (start us, length us, event | category | flops | bytes accessed | tf_op | source)
XLA Modules:
  0.0 864.5 jit_solution(5538302250169528371)
XLA Ops:
  4.7 3.8 copy.336
  10.2 1.7 pad.65.turned_ref
  12.6 105.7 %start_all.1 = (s32[32,16,128]{2,1,0:T(8,128)}, bf16[2,2,4,2,160,896]{5,4,3,2,1,0:T(8,128)(2,1)}, f32[128,768]{1,0:T(8,128)}) custom-call(s32[16,128]{1,0:T(8,128)} %pad.61.number_ref, bf16[160,896]{1,0:T(8,128)(2,1)} %fusion.60.pack_ref, bf16[768,1664]{1,0:T(8,128)(2,1)} %pad.65.turned_ref), custom_call_target="tpu_custom_call" | custom-call | tf_op jit(solution)/shard_map/start_all/pallas_call | solution.py:1221
  119.3 2.7 slice_bitcast_fusion
  123.9 3.6 copy.339
  128.6 2.5 fusion.114
  131.9 4.9 collective-permute-start
  139.5 1.8 slice_bitcast_fusion.10
  141.3 3.3 slice_bitcast_fusion.3
  149.8 1.7 fusion.24
  160.0 1.5 fusion.70
  164.7 3.1 copy.398
  170.2 3.3 copy.343
  173.5 6.5 convert_element_type.254
  180.1 1.6 reshape.341.target_ref
  181.7 1.6 pad.66.clone.table_ref
  189.9 3.6 fusion.34
  194.4 1.9 compare_select_fusion.1
  199.8 29.9 %scan_forward.1 = (f32[128,1536]{1,0:T(8,128)}, f32[16,1536]{1,0:T(8,128)}) custom-call(f32[128,1536]{1,0:T(8,128)} %get-tuple-element.309.step_ref, f32[128,1536]{1,0:T(8,128)} %copy-done.1, f32[128,16,128]{2,1,0:T(8,128)} %broadcast_in_dim.17.b_ref, f32[128,16,128]{2,1,0:T(8,128)} %broadcast_in_dim.18.c_ref, f32[128,128]{1,0:T(8,128)} %broadcast_in_dim.20.keep_ref, ...), custom_call_target="tpu_custom_call" | custom-call | tf_op jit(solution)/shard_map/scan_forward/pallas_call | solution.py:976
  229.7 1.6 multiply_convert_fusion.2
  232.7 36.5 %gather_all.2 = bf16[32,128,768]{2,1,0:T(8,128)(2,1)} custom-call(bf16[128,768]{1,0:T(8,128)(2,1)} %copy-done.19), custom_call_target="tpu_custom_call" | custom-call | tf_op jit(solution)/shard_map/gather_all/pallas_call | solution.py:147
  269.3 3.8 convolution_convert_fusion.8
  273.4 3.6 fusion.25
  277.1 1.8 convolution_convert_fusion.6
  279.3 4.5 convolution_convert_fusion.2
  283.8 45.6 %scatter_all.2 = f32[128,768]{1,0:T(8,128)} custom-call(bf16[2,2,4,2,128,768]{5,4,3,2,1,0:T(8,128)(2,1)} %bitcast.179), custom_call_target="tpu_custom_call" | custom-call | tf_op jit(solution)/shard_map/scatter_all/pallas_call | solution.py:340
  329.5 1.9 multiply_reduce_fusion.12
  332.2 70.5 %head_forward.1 = (bf16[2,2,4,2,128,768]{5,4,3,2,1,0:T(8,128)(2,1)}, f32[2,16,256]{2,1,0:T(8,128)}) custom-call(bf16[128,768]{1,0:T(8,128)(2,1)} %multiply_convert_fusion.4.own_ref, bf16[1584,768]{1,0:T(8,128)(2,1)} %pad.66.clone.table_ref, s32[16,256]{1,0:T(8,128)} %reshape.341.target_ref), custom_call_target="tpu_custom_call" | custom-call | tf_op jit(solution)/shard_map/head_forward/pallas_call | solution.py:531
  404.1 73.2 %head_backward.1 = (f32[128,768]{1,0:T(8,128)}, f32[1584,768]{1,0:T(8,128)}) custom-call(bf16[2,2,4,2,128,768]{5,4,3,2,1,0:T(8,128)(2,1)} %get-tuple-element.48.all_ref, bf16[1584,768]{1,0:T(8,128)(2,1)} %pad.66.clone.table_ref, bf16[768,1664]{1,0:T(8,128)(2,1)} %pad.65.turned_ref, s32[16,256]{1,0:T(8,128)} %reshape.341.target_ref, ...), custom_call_target="tpu_custom_call" | custom-call | tf_op jit(solution)/shard_map/head_backward/pallas_call | solution.py:664
  477.3 1.7 multiply_reduce_fusion.6
  481.1 38.3 %gather_all.3 = bf16[32,128,768]{2,1,0:T(8,128)(2,1)} custom-call(bf16[128,768]{1,0:T(8,128)(2,1)} %multiply_convert_fusion.3.own_ref), custom_call_target="tpu_custom_call" | custom-call | tf_op jit(solution)/shard_map/gather_all/pallas_call | solution.py:147
  519.4 3.9 convolution_convert_fusion.7
  523.6 4.8 fusion.19
  528.4 3.8 convolution_bitcast_fusion
  532.3 3.5 convolution_bitcast_fusion.1
  535.8 1.8 convolution_convert_fusion.5
  538.1 5.0 convolution_convert_fusion.1
  543.1 44.8 %scatter_all.3 = f32[128,768]{1,0:T(8,128)} custom-call(bf16[2,2,4,2,128,768]{5,4,3,2,1,0:T(8,128)(2,1)} %bitcast.178), custom_call_target="tpu_custom_call" | custom-call | tf_op jit(solution)/shard_map/scatter_all/pallas_call | solution.py:340
  587.9 1.5 multiply_reduce_fusion.7
  589.7 2.6 multiply_reduce_fusion.1
  592.3 39.2 %scan_backward.1 = (f32[128,1536]{1,0:T(8,128)}, f32[128,1536]{1,0:T(8,128)}, f32[128,16,128]{2,1,0:T(8,128)}, f32[128,16,128]{2,1,0:T(8,128)}, f32[16,1536]{1,0:T(8,128)}) custom-call(f32[128,1536]{1,0:T(8,128)} %get-tuple-element.309.step_ref, f32[128,1536]{1,0:T(8,128)} %copy-done.1, f32[128,16,128]{2,1,0:T(8,128)} %broadcast_in_dim.17.b_ref, ...), custom_call_target="tpu_custom_call" | custom-call | tf_op jit(solution)/shard_map/scan_backward/pallas_call | solution.py:1102
  631.5 1.6 fusion.109
  633.9 1.6 reduce_sum.274
  635.5 1.6 reduce_sum.275
  638.2 4.3 fusion.103
  645.7 1.4 collective-permute-start.1
  647.1 6.8 multiply_reduce_fusion
  660.0 3.0 concatenate.109
  664.3 1.9 copy.360
  667.1 1.6 copy.409
  668.8 1.4 broadcast_in_dim.23
  672.2 3.7 convolution_convert_fusion
  675.9 2.4 multiply_reduce_fusion.8
  678.3 9.7 %reshape.348 = bf16[8,96,4,768]{3,2,1,0:T(4,128)(2,1)} reshape(bf16[768,3072]{1,0:T(8,128)(2,1)} %convolution_convert_fusion) | data formatting | bytes 9437184 | tf_op jit(solution)/shard_map/reshape | solution.py:1476
  688.1 5.5 copy.408
  693.9 1.8 add_convert_fusion.own_ref
  695.7 6.6 fusion.10
  703.0 105.5 %finish_all.1 = (f32[1584,768]{1,0:T(8,128)}, bf16[4,160,896]{2,1,0:T(8,128)(2,1)}, f32[8,128]{1,0:T(8,128)}) custom-call(bf16[128,768]{1,0:T(8,128)(2,1)} %add_convert_fusion.own_ref, bf16[2,2,4,2,160,896]{5,4,3,2,1,0:T(8,128)(2,1)} %bitcast.177, s32[16,256]{1,0:T(8,128)} %reshape.352.token_ref, f32[1584,768]{1,0:T(8,128)} %get-tuple-element.57.head_ref, ...), custom_call_target="tpu_custom_call" | custom-call | tf_op jit(solution)/shard_map/finish_all/pallas_call | solution.py:1380
  808.5 1.4 convert_element_type.279
  822.3 1.5 copy.400
  823.9 24.1 %multiply_add_fusion = (f32[2,4,384,768]{3,2,1,0:T(8,128)}, f32[2,4,384,768]{3,2,1,0:T(8,128)}, f32[2,4,384,768]{3,2,1,0:T(8,128)}) fusion(f32[2,4,384,768]{3,2,1,0:T(8,128)} %param.55, f32[2,4,384,768]{3,2,1,0:T(8,128)} %param.53, f32[1,4,384,768]{3,2,1,0:T(8,128)} %convolution_bitcast_fusion, f32[1,4,384,768]{3,2,1,0:T(8,128)} %convolution_bitcast_fusion.1, ...), kind=kLoop, calls=%fused_computation.15 | loop fusion | flops 25952256 | bytes 66060292 | tf_op jit(solution)/shard_map/add | solution.py:1791
  848.1 2.9 multiply_add_fusion.8
  851.8 2.1 multiply_add_fusion.4
  854.7 7.7 multiply_add_fusion.2
  (383 shorter events, 81.1 us)
Async XLA Ops:
  1.5 7.0 copy-start.63
  123.2 5.4 copy-start.33
  131.2 5.5 copy-start.22
  131.9 58.0 %collective-permute-start = (f32[3,1536]{1,0:T(4,128)}, f32[3,1536]{1,0:T(4,128)}, u32[]{:S(2)}, u32[]{:S(2)}) collective-permute-start(f32[3,1536]{1,0:T(4,128)} %slice_convert_fusion.2), channel_id=1, source_target_pairs={{0,1},{1,2},{2,3},{3,4},{4,5},{5,6},{6,7},{8,9},{9,10},{10,11},{11... | collective-permute-start | bytes 55304 | tf_op jit(solution)/shard_map/ppermute | solution.py:1525
  137.7 9.1 %copy-start.78 = (s32[4,8]{1,0:T(4,128)S(1)}, s32[4,8]{1,0:T(4,128)}, u32[]{:S(2)}) copy-start(s32[4,8]{1,0:T(4,128)} %param.30) | copy-start | bytes 388
  148.9 18.9 %copy-start.36 = (bf16[7,1536]{1,0:T(8,128)(2,1)}, bf16[7,1536]{1,0:T(8,128)(2,1)S(1)}, u32[]{:S(2)}) copy-start(bf16[7,1536]{1,0:T(8,128)(2,1)S(1)} %reshape.332) | copy-start | bytes 64516
  149.0 18.8 %copy-start.62 = (f32[96,16]{0,1:T(8,128)S(1)}, f32[96,16]{0,1:T(8,128)}, u32[]{:S(2)}) copy-start(f32[96,16]{0,1:T(8,128)} %param.50) | copy-start | bytes 18436
  149.0 19.5 %copy-start.76 = (f32[3,96]{1,0:T(4,128)S(1)}, f32[3,96]{1,0:T(4,128)}, u32[]{:S(2)}) copy-start(f32[3,96]{1,0:T(4,128)} %param.47) | copy-start | bytes 3460
  173.5 8.1 copy-start.5
  180.1 8.9 %copy-start.77 = (f32[3,96]{1,0:T(4,128)S(1)}, f32[3,96]{1,0:T(4,128)}, u32[]{:S(2)}) copy-start(f32[3,96]{1,0:T(4,128)} %broadcast_multiply_fusion.3) | copy-start | bytes 3460
  180.1 9.6 %copy-start.30 = (bf16[16,1536]{1,0:T(8,128)(2,1)S(1)}, bf16[16,1536]{1,0:T(8,128)(2,1)}, u32[]{:S(2)}) copy-start(bf16[16,1536]{1,0:T(8,128)(2,1)} %copy-done.29) | copy-start | bytes 147460
  189.8 6.5 copy-start.54
  189.8 6.5 copy-start.56
  189.8 7.9 copy-start.58
  189.8 7.9 copy-start.60
  189.9 39.8 %copy-start.52 = (f32[1536]{0:T(1024)}, f32[1536]{0:T(1024)S(1)}, u32[]{:S(2)}) copy-start(f32[1536]{0:T(1024)S(1)} %get-tuple-element.240) | copy-start | bytes 18436
  193.5 6.4 copy-start.1
  193.5 5.6 copy-start.87
  196.2 33.5 %copy-start.9 = (f32[128,3072]{1,0:T(8,128)S(1)}, f32[128,3072]{1,0:T(8,128)}, u32[]{:S(2)}) copy-start(f32[128,3072]{1,0:T(8,128)} %get-tuple-element.308) | copy-start | bytes 4718596
  199.8 31.6 %copy-start.6 = (bf16[8,4,48,768]{3,2,1,0:T(8,128)(2,1)S(1)}, bf16[8,4,48,768]{3,2,1,0:T(8,128)(2,1)}, u32[]{:S(2)}) copy-start(bf16[8,4,48,768]{3,2,1,0:T(8,128)(2,1)} %copy.343) | copy-start | bytes 7077892
  231.3 38.0 %copy-start.16 = (bf16[128,1536]{1,0:T(8,128)(2,1)}, bf16[128,1536]{1,0:T(8,128)(2,1)S(1)}, u32[]{:S(2)}) copy-start(bf16[128,1536]{1,0:T(8,128)(2,1)S(1)} %multiply_convert_fusion.2) | copy-start | bytes 1179652
  232.7 355.1 %copy-start.37 = (f32[128,16]{0,1:T(8,128)}, f32[128,16]{0,1:T(8,128)S(1)}, u32[]{:S(2)}) copy-start(f32[128,16]{0,1:T(8,128)S(1)} %get-tuple-element.314) | copy-start | bytes 24580
  232.7 355.1 %copy-start.68 = (f32[128]{0:T(128)}, f32[128]{0:T(128)S(1)}, u32[]{:S(2)}) copy-start(f32[128]{0:T(128)S(1)} %get-tuple-element.313) | copy-start | bytes 1540
  283.8 45.7 %copy-start.71 = (s32[1,128,1]{1,2,0:T(1,128)S(1)}, s32[1,128,1]{1,2,0:T(1,128)}, u32[]{:S(2)}) copy-start(s32[1,128,1]{1,2,0:T(1,128)} %param.31) | copy-start | bytes 1540
  283.8 47.6 %copy-start.47 = (f32[768]{0:T(1024)S(1)}, f32[768]{0:T(1024)}, u32[]{:S(2)}) copy-start(f32[768]{0:T(1024)} %get-tuple-element.237) | copy-start | bytes 9220
  329.5 258.4 %copy-start.73 = (f32[128]{0:T(128)}, f32[128]{0:T(128)S(1)}, u32[]{:S(2)}) copy-start(f32[128]{0:T(128)S(1)} %fusion.85) | copy-start | bytes 1540
  404.1 74.9 %copy-start.13 = (f32[128,768]{1,0:T(8,128)S(1)}, f32[128,768]{1,0:T(8,128)}, u32[]{:S(2)}) copy-start(f32[128,768]{1,0:T(8,128)} %scatter_all.2) | copy-start | bytes 1179652
  523.3 12.5 %slice-start.10 = ((s8[4718592]{0:T(1024)(128)(4,1)}), s8[4194304]{0:T(1024)(128)(4,1)S(1)}, s32[]{:S(2)}) async-start(s8[4718592]{0:T(1024)(128)(4,1)} %bitcast.207), calls=%async_computation.10 | async-start | bytes 8388608
  523.6 12.2 %slice-start.11 = ((s8[4718592]{0:T(1024)(128)(4,1)}), s8[524288]{0:T(1024)(128)(4,1)S(1)}, s32[]{:S(2)}) async-start(s8[4718592]{0:T(1024)(128)(4,1)} %bitcast.207), calls=%async_computation.11 | async-start | bytes 1048576
  543.0 44.9 %copy-start.46 = (f32[768]{0:T(1024)S(1)}, f32[768]{0:T(1024)}, u32[]{:S(2)}) copy-start(f32[768]{0:T(1024)} %get-tuple-element.238) | copy-start | bytes 9220
  543.0 46.4 %copy-start.15 = (f32[128,768]{1,0:T(8,128)S(1)}, f32[128,768]{1,0:T(8,128)}, u32[]{:S(2)}) copy-start(f32[128,768]{1,0:T(8,128)} %copy-done.14) | copy-start | bytes 1179652
  543.0 46.6 %copy-start.2 = (f32[128,1536]{1,0:T(8,128)S(1)}, f32[128,1536]{1,0:T(8,128)}, u32[]{:S(2)}) copy-start(f32[128,1536]{1,0:T(8,128)} %copy-done.1) | copy-start | bytes 2359300
  543.0 46.6 %copy-start.7 = (bf16[8,4,48,768]{3,2,1,0:T(8,128)(2,1)S(1)}, bf16[8,4,48,768]{3,2,1,0:T(8,128)(2,1)}, u32[]{:S(2)}) copy-start(bf16[8,4,48,768]{3,2,1,0:T(8,128)(2,1)} %copy.343) | copy-start | bytes 7077892
  543.1 46.6 %copy-start.10 = (f32[128,3072]{1,0:T(8,128)S(1)}, f32[128,3072]{1,0:T(8,128)}, u32[]{:S(2)}) copy-start(f32[128,3072]{1,0:T(8,128)} %get-tuple-element.308) | copy-start | bytes 4718596
  543.1 46.6 %copy-start.28 = (f32[128,1536]{1,0:T(8,128)S(1)}, f32[128,1536]{1,0:T(8,128)}, u32[]{:S(2)}) copy-start(f32[128,1536]{1,0:T(8,128)} %get-tuple-element.46) | copy-start | bytes 2359300
  543.1 46.6 %copy-start.53 = (f32[1536]{0:T(1024)S(1)}, f32[1536]{0:T(1024)}, u32[]{:S(2)}) copy-start(f32[1536]{0:T(1024)} %copy-done.52) | copy-start | bytes 18436
  592.3 39.2 %copy-start.3 = (f32[128,1536]{1,0:T(8,128)S(1)}, f32[128,1536]{1,0:T(8,128)}, u32[]{:S(2)}) copy-start(f32[128,1536]{1,0:T(8,128)} %copy-done.1) | copy-start | bytes 2359300
  592.3 39.2 %copy-start.27 = (f32[128,1536]{1,0:T(8,128)S(1)}, f32[128,1536]{1,0:T(8,128)}, u32[]{:S(2)}) copy-start(f32[128,1536]{1,0:T(8,128)} %get-tuple-element.310) | copy-start | bytes 2359300
  633.1 5.0 copy-start.21
  633.1 5.0 copy-start.55
  633.1 5.0 copy-start.57
  645.6 9.6 %copy-start.83 = (bf16[1536]{0:T(1024)(128)(2,1)S(1)}, bf16[1536]{0:T(1024)(128)(2,1)}, u32[]{:S(2)}) copy-start(bf16[1536]{0:T(1024)(128)(2,1)} %get-tuple-element.234) | copy-start | bytes 9220
  645.6 9.9 %copy-start.82 = (bf16[1536]{0:T(1024)(128)(2,1)S(1)}, bf16[1536]{0:T(1024)(128)(2,1)}, u32[]{:S(2)}) copy-start(bf16[1536]{0:T(1024)(128)(2,1)} %get-tuple-element.236) | copy-start | bytes 9220
  645.6 10.6 %copy-start.81 = (bf16[1536]{0:T(1024)(128)(2,1)S(1)}, bf16[1536]{0:T(1024)(128)(2,1)}, u32[]{:S(2)}) copy-start(bf16[1536]{0:T(1024)(128)(2,1)} %get-tuple-element.233) | copy-start | bytes 9220
  645.7 11.3 %copy-start.80 = (bf16[1536]{0:T(1024)(128)(2,1)S(1)}, bf16[1536]{0:T(1024)(128)(2,1)}, u32[]{:S(2)}) copy-start(bf16[1536]{0:T(1024)(128)(2,1)} %get-tuple-element.232) | copy-start | bytes 9220
  645.7 12.7 %copy-start.42 = (f32[16,1536]{1,0:T(8,128)S(1)}, f32[16,1536]{1,0:T(8,128)}, u32[]{:S(2)}) copy-start(f32[16,1536]{1,0:T(8,128)} %get-tuple-element.56) | copy-start | bytes 294916
  645.7 13.6 %copy-start.79 = (bf16[1536]{0:T(1024)(128)(2,1)S(1)}, bf16[1536]{0:T(1024)(128)(2,1)}, u32[]{:S(2)}) copy-start(bf16[1536]{0:T(1024)(128)(2,1)} %get-tuple-element.271) | copy-start | bytes 9220
  645.7 25.7 %collective-permute-start.1 = (f32[3,1536]{1,0:T(4,128)}, f32[3,1536]{1,0:T(4,128)}, u32[]{:S(2)}, u32[]{:S(2)}) collective-permute-start(f32[3,1536]{1,0:T(4,128)} %pad_add_fusion.1), channel_id=1, source_target_pairs={{1,0},{2,1},{3,2},{4,3},{5,4},{6,5},{7,6},{9,8},{10,9},{11,10},{12... | collective-permute-start | bytes 55304 | tf_op jit(solution)/shard_map/ppermute | solution.py:1525
  663.0 5.7 copy-start.75
  666.2 6.0 copy-start.34
  666.2 6.0 copy-start.67
  667.1 5.1 copy-start.23
  667.1 8.8 %slice-start = ((s8[4718592]{0:T(1024)(128)(4,1)}), s8[4194304]{0:T(1024)(128)(4,1)S(1)}, s32[]{:S(2)}) async-start(s8[4718592]{0:T(1024)(128)(4,1)} %bitcast.174), calls=%async_computation | async-start | bytes 8388608
  688.1 5.8 copy-start.92
  688.1 7.6 copy-start.8
  695.7 6.7 copy-start.93
  813.9 40.0 %slice-start.4 = ((s8[4841472]{0:T(1024)(128)(4,1)}), s8[647168]{0:T(1024)(128)(4,1)S(1)}, s32[]{:S(2)}) async-start(s8[4841472]{0:T(1024)(128)(4,1)} %bitcast.201), calls=%async_computation.4 | async-start | bytes 1294336
  822.3 31.6 %slice-start.6 = ((s8[4866048]{0:T(1024)(128)(4,1)}), s8[4194304]{0:T(1024)(128)(4,1)S(1)}, s32[]{:S(2)}) async-start(s8[4866048]{0:T(1024)(128)(4,1)} %bitcast.203), calls=%async_computation.6 | async-start | bytes 8388608
  823.9 30.1 %slice-start.5 = ((s8[4841472]{0:T(1024)(128)(4,1)}), s8[4194304]{0:T(1024)(128)(4,1)S(1)}, s32[]{:S(2)}) async-start(s8[4841472]{0:T(1024)(128)(4,1)} %bitcast.201), calls=%async_computation.5 | async-start | bytes 8388608
  823.9 30.0 %slice-start.7 = ((s8[4866048]{0:T(1024)(128)(4,1)}), s8[671744]{0:T(1024)(128)(4,1)S(1)}, s32[]{:S(2)}) async-start(s8[4866048]{0:T(1024)(128)(4,1)} %bitcast.203), calls=%async_computation.7 | async-start | bytes 1343488
  854.7 7.7 copy-start.50
  854.7 7.7 copy-start.51
  854.7 7.7 copy-start.64
  854.7 7.7 copy-start.65
  (48 other events, 147.4 us)
where the time goes:
time: 871 us; the launch traced here: 864 us
  Pallas kernels  589 us (68%)
  other arithmetic  109 us (13%)
  local copies, waits for them, and re-layouts  96.7 us (11%)
  matrix products  59.2 us (7%)
    pallas_call x1, Pallas kernels, start_all(): pl.pallas_call(functools.partial(start_kernel, sizes, pairs, pack_pairs,...  106 us
    pallas_call x1, Pallas kernels, finish_all(): pl.pallas_call(functools.partial(finish_kernel, sizes, pairs, pack_pairs)...  105 us
    pallas_call x2, Pallas kernels, scatter_all(): pl.pallas_call(functools.partial(scatter_kernel, sizes, pairs), out_shape...  90.4 us
    pallas_call x2, Pallas kernels, gather_all(): pl.pallas_call(functools.partial(gather_kernel, sizes, pieces), out_shape...  74.9 us
    pallas_call x1, Pallas kernels, head_backward(): pl.pallas_call(functools.partial(head_backward_kernel, sizes, pairs, own_...  73.2 us
    pallas_call x1, Pallas kernels, head_forward(): pl.pallas_call(functools.partial(head_forward_kernel, sizes, pairs, own_v...  70.5 us
    add x8, other arithmetic, renewed(): EMA_KEEP * average + (1.0 - EMA_KEEP) * master_new  40 us
    pallas_call x1, Pallas kernels, scan_backward(): pl.pallas_call(scan_backward_kernel, out_shape=(full, full, jax.ShapeDtyp...  39.2 us
  transfers between devices with their start and end apart: 2, of which 0 were waited for; matrix products, arithmetic and copies ran while one was open for 9% of the time, Pallas kernels for 0%

commit v1 on v0

--- a/solution.py
+++ b/solution.py
@@ -23,8 +23,9 @@
 EMA_KEEP = 0.8
 HIGHEST = lax.Precision.HIGHEST
 MESH = pl.DeviceIdType.MESH
-VMEM_LIMIT = 56 << 20
+VMEM_LIMIT = 58 << 20
 LANES = 128
+SIDE_LANE = 32
 
 
 def axis_sizes():
@@ -901,10 +902,14 @@
     return total
 
 
-def scan_forward_kernel(
+def scan_forward_kernel(*refs):
+    meet(chain_peers())
+    scan_forward_body(*refs)
+
+
+def scan_forward_body(
     step_ref, act_ref, b_ref, c_ref, keep_ref, rate_ref, y_ref, in_ref, out_buf, in_buf, ss, rs
 ):
-    meet(chain_peers())
     tokens, width = step_ref.shape
     ends = []
     for span in spans(width):
@@ -989,7 +994,12 @@
     )(step, act, b_wide, c_wide, keep_wide, rates)
 
 
-def scan_backward_kernel(
+def scan_backward_kernel(*refs):
+    meet(chain_peers())
+    scan_backward_body(*refs)
+
+
+def scan_backward_body(
     step_ref,
     act_ref,
     b_ref,
@@ -1010,7 +1020,6 @@
     ss,
     rs,
 ):
-    meet(chain_peers())
     tokens, width = step_ref.shape
     blocks = tokens // 8
     ends = []
@@ -1140,18 +1149,24 @@
     own_vocab,
     number_ref,
     pack_ref,
-    turned_ref,
+    master_ref,
     numbers_ref,
     packs_ref,
     own_ref,
+    table_ref,
+    turned_ref,
+    token_ref,
+    target_ref,
     full_ref,
+    tall_ref,
     pack_sem,
     send_sem,
     recv_sem,
     *scratch,
 ):
-    devices, groups, me = everyone_peer_greeting()
     place = my_place(sizes)
+    meet(line_peers(place, sizes))
+    _, groups, me = flat_place()
     seqs = sizes["x"] * sizes["core"]
     gather = Gather(sizes, pack_pairs, pack_ref, packs_ref, scratch[:8])
     scatter = Scatter(sizes, pairs, full_ref, own_ref, scratch[8:], False)
@@ -1160,78 +1175,129 @@
     )
     own_pack.start()
 
-    def number_copy(by, address):
-        return pltpu.make_async_remote_copy(
-            src_ref=number_ref,
-            dst_ref=numbers_ref.at[me],
-            send_sem=send_sem.at[by],
-            recv_sem=recv_sem.at[by],
-            device_id=address,
-            device_id_type=MESH,
-        )
+    number_order = ("z", "y", "x", "core")
+
+    def number_copies(phase):
+        axis = number_order[phase]
+        block = tuple(
+            slice(None) if a in number_order[:phase] else place[a] for a in NATURAL
+        )
+        return [
+            pltpu.make_async_remote_copy(
+                src_ref=number_ref if phase == 0 else numbers_ref.at[block],
+                dst_ref=numbers_ref.at[block],
+                send_sem=send_sem.at[phase, by],
+                recv_sem=recv_sem.at[phase, by],
+                device_id=device_of(moved(place, axis, by, sizes), sizes),
+                device_id_type=MESH,
+            )
+            for by in range(1, sizes[axis])
+        ]
+
+    def numbers_next(phase):
+        if phase > 0:
+            for copy in number_copies(phase - 1):
+                copy.wait_recv()
+        if phase < 4:
+            for copy in number_copies(phase):
+                copy.start()
 
     def weights(turn):
-        for phase in range(4, -1, -1):
-            if 0 <= turn - phase < pack_pairs:
-                gather.advance(turn - phase, phase)
-
-    everyone(devices, groups, me, lambda by, peer, address: number_copy(by, address).start())
-    weights(0)
-    numbers_ref[me] = number_ref[...]
+        for phase in range(4, 0, -1):
+            if 0 <= turn + 1 - phase < pack_pairs:
+                gather.advance(turn + 1 - phase, phase)
+
+    numbers_next(0)
+    for pair in range(pack_pairs):
+        gather.advance(pair, 0)
+    numbers_ref[tuple(place[a] for a in NATURAL)] = number_ref[...]
+    numbers_next(1)
     own_pack.wait()
-    everyone(devices, groups, me, lambda by, peer, address: number_copy(by, address).wait())
-    weights(1)
-
-    def look_up(step, carry):
-        seq, group = (lax.div(step, groups // 2), lax.rem(step, groups // 2) * 2)
+    whole_tiles = own_vocab // 8 * 8
+    tall_ref[whole_tiles:] = jnp.zeros_like(tall_ref[whole_tiles:])
+    tall_ref[0:own_vocab] = master_ref[...]
+    table_ref[...] = tall_ref[0 : table_ref.shape[0]].astype(jnp.bfloat16)
+    for first in range(0, tall_ref.shape[0], LANES):
+        turned_ref[:, first : first + LANES] = tall_ref[first : first + LANES].T.astype(
+            jnp.bfloat16
+        )
+    numbers_next(2)
+
+    def look_up(pair, seq):
         x, core = seq_place(seq, sizes)
-        ids = jnp.concatenate(
-            [numbers_ref[group, pl.ds(seq, 1)], numbers_ref[group + 1, pl.ds(seq, 1)]], axis=1
-        )
-        found = one_hot_turned(ids - me * own_vocab, turned_ref.shape[1])
+        found = one_hot_turned(token_ref[pl.ds(pair * seqs + seq, 1)], turned_ref.shape[1])
         rows = matmul(turned_ref[...], found).T.astype(jnp.bfloat16)
-        tokens = number_ref.shape[1]
-        for half in range(2):
-            z, y = (lax.div(group + half, sizes["y"]), lax.rem(group + half, sizes["y"]))
-            full_ref[x, core, z, y] = rows[half * tokens : (half + 1) * tokens]
-        return carry
-
-    chunks = seqs * groups // 2
-    for part in range(4):
-        lax.fori_loop(part * chunks // 4, (part + 1) * chunks // 4, look_up, 0)
-        weights(2 + part)
+        full_ref[x, core, :, :, pl.ds(pair * SPAN, SPAN), :] = rows.reshape(
+            sizes["z"], sizes["y"], SPAN, D
+        )
+
+    per_tile = LANES // SPAN
+    lane = lax.broadcasted_iota(jnp.int32, (2 * seqs, LANES), 1)
     for pair in range(pairs):
-        scatter.launch(pair, 0)
-    for turn in range(max(pairs + 3, pack_pairs - 2)):
-        weights(6 + turn)
+        for tile in range(groups // per_tile):
+            local = jnp.zeros((2 * seqs, LANES), jnp.int32)
+            for part in range(per_tile):
+                z, y = divmod(tile * per_tile + part, sizes["y"])
+                ids = numbers_ref[place["x"], place["core"], z, y, 0 : 2 * seqs]
+                ids = pltpu.roll(ids, (part - pair) * SPAN % LANES, 1)
+                local = jnp.where(lane // SPAN == part, ids, local)
+            local = local - me * own_vocab
+            local = jnp.where(local < own_vocab, local, -1)
+            lanes = pl.ds(tile * LANES, LANES)
+            token_ref[pair * seqs : (pair + 1) * seqs, lanes] = local[0:seqs]
+            target_ref[pair * seqs : (pair + 1) * seqs, lanes] = local[seqs:]
+
+    for turn in range(max(pairs + 4, pack_pairs + 3)):
+        if turn < pairs:
+
+            def one(seq, carry, turn=turn):
+                look_up(turn, seq)
+                return carry
+
+            lax.fori_loop(0, seqs, one, 0)
+            scatter.launch(turn, 0)
         for phase in range(3, -1, -1):
-            if 0 <= turn - phase < pairs:
-                scatter.advance(turn - phase, phase)
+            if 0 <= turn - 1 - phase < pairs:
+                scatter.advance(turn - 1 - phase, phase)
+        weights(turn)
+        if turn < 2:
+            numbers_next(3 + turn)
+    for phase in range(4):
+        for copy in number_copies(phase):
+            copy.wait_send()
     gather.finish()
     scatter.finish()
 
 
-def start_all(numbers, pack, turned, own_vocab, collective_id):
+def start_all(numbers, pack, master, collective_id):
     sizes = axis_sizes()
     natural = tuple(sizes[a] for a in NATURAL)
     devices = lax.axis_size("seq") * lax.axis_size("group")
     tokens = numbers.shape[1]
     pairs, pack_pairs = (tokens // SPAN, pack.shape[0] // SPAN)
+    own_vocab = master.shape[0]
+    short, long = (-(-own_vocab // 16) * 16, -(-own_vocab // LANES) * LANES)
+    spread = (devices * tokens // (SPAN * lax.axis_size("group")), SPAN * lax.axis_size("group"))
     vmem = pl.BlockSpec(memory_space=pltpu.VMEM)
     return pl.pallas_call(
         functools.partial(start_kernel, sizes, pairs, pack_pairs, own_vocab),
         out_shape=(
-            jax.ShapeDtypeStruct((devices,) + numbers.shape, numbers.dtype),
+            jax.ShapeDtypeStruct(natural + numbers.shape, numbers.dtype),
             jax.ShapeDtypeStruct(natural + pack.shape, pack.dtype),
             jax.ShapeDtypeStruct((tokens, D), jnp.float32),
+            jax.ShapeDtypeStruct((short, D), jnp.bfloat16),
+            jax.ShapeDtypeStruct((D, long), jnp.bfloat16),
+            jax.ShapeDtypeStruct(spread, jnp.int32),
+            jax.ShapeDtypeStruct(spread, jnp.int32),
         ),
         in_specs=[vmem] * 3,
-        out_specs=(vmem, pl.BlockSpec(memory_space=pl.ANY), vmem),
+        out_specs=(vmem, pl.BlockSpec(memory_space=pl.ANY)) + (vmem,) * 5,
         scratch_shapes=[
             pltpu.VMEM(natural + (tokens, D), jnp.bfloat16),
+            pltpu.VMEM((long, D), jnp.float32),
             pltpu.SemaphoreType.DMA,
-            pltpu.SemaphoreType.DMA((devices,)),
-            pltpu.SemaphoreType.DMA((devices,)),
+            pltpu.SemaphoreType.DMA((4, max(sizes.values()))),
+            pltpu.SemaphoreType.DMA((4, max(sizes.values()))),
         ]
         + gather_semaphores(sizes, pack_pairs)
         + scatter_scratch(sizes, pairs, D, False),
@@ -1239,7 +1305,7 @@
             collective_id=collective_id, has_side_effects=True, vmem_limit_bytes=VMEM_LIMIT
         ),
         name="start_all",
-    )(numbers, pack, turned)
+    )(numbers, pack, master)
 
 
 def finish_kernel(
@@ -1286,6 +1352,39 @@
         update = matmul(found_ref[...], rows)
         tgrad_ref[...] = (head_ref[...] if pair == 0 else tgrad_ref[...]) + update
 
+    seq = place["x"] * sizes["core"] + place["core"]
+    started = []
+    x_sent, core_sent = ({}, [])
+
+    def send_quarter(pair, axis, held):
+        rows = pl.ds(pair * SPAN, SPAN)
+        sent = []
+        for by in range(1, sizes[axis]):
+            number = len(started)
+            copy = pltpu.make_async_remote_copy(
+                src_ref=quarters_ref.at[held, rows],
+                dst_ref=quarters_ref.at[held, rows],
+                send_sem=quarter_send.at[number],
+                recv_sem=quarter_recv.at[number],
+                device_id=device_of(moved(place, axis, by, sizes), sizes),
+                device_id_type=MESH,
+            )
+            copy.start()
+            sent.append(copy)
+            started.append(copy)
+        return sent
+
+    def own_quarter(pair):
+        rows = pl.ds(pair * SPAN, SPAN)
+        quarters_ref[seq, rows] = mine_ref[rows].astype(jnp.bfloat16)
+        x_sent[pair] = send_quarter(pair, "x", seq)
+
+    def pass_quarter(pair):
+        for copy in x_sent[pair]:
+            copy.wait_recv()
+        for x in range(sizes["x"]):
+            core_sent.extend(send_quarter(pair, "core", x * sizes["core"] + place["core"]))
+
     for pair in range(pack_pairs):
         scatter.launch(pair, 0)
         for kind in range(2):
@@ -1298,41 +1397,21 @@
                 gather.advance(turn - phase, phase)
             if 0 <= turn - phase < pack_pairs:
                 scatter.advance(turn - phase, phase)
+        if 0 <= turn - 3 < pack_pairs:
+            own_quarter(turn - 3)
+        if 0 <= turn - 4 < pack_pairs:
+            pass_quarter(turn - 4)
         if turn == 0:
             keep_own.wait()
         if 0 <= turn - 4 < pairs:
             spread_table(turn - 4)
 
-    seq = place["x"] * sizes["core"] + place["core"]
-    quarters_ref[seq] = mine_ref[...].astype(jnp.bfloat16)
-    started = []
-
-    def send_quarters(axis, first):
-        sent = []
-        for by in range(1, sizes[axis]):
-            to = moved(place, axis, by, sizes)
-            for x in range(sizes["x"] if axis == "core" else 1):
-                held = x * sizes["core"] + place["core"] if axis == "core" else seq
-                number = first + len(sent)
-                copy = pltpu.make_async_remote_copy(
-                    src_ref=quarters_ref.at[held],
-                    dst_ref=quarters_ref.at[held],
-                    send_sem=quarter_send.at[number],
-                    recv_sem=quarter_recv.at[number],
-                    device_id=device_of(to, sizes),
-                    device_id_type=MESH,
-                )
-                copy.start()
-                sent.append(copy)
-        started.extend(sent)
-        return sent
-
-    x_sent = send_quarters("x", 0)
     square = jnp.sum(tgrad_ref[...] * tgrad_ref[...]) + jnp.sum(mine_ref[...] * mine_ref[...])
     row = lax.broadcasted_iota(jnp.int32, (8, LANES), 0)
     value = scalar_ref[...] + jnp.where(row < 4, square, 0.0)
-    core_sent = []
     first = 0
+    ring_started = []
+    last_pair = pack_pairs - 1
     for axis in ("core", "x", "y", "z"):
         ring_ref[first + place[axis]] = value
         sent = []
@@ -1347,11 +1426,9 @@
             )
             copy.start()
             sent.append(copy)
-        started.extend(sent)
-        if axis == "y":
-            for copy in x_sent:
-                copy.wait_recv()
-            core_sent = send_quarters("core", len(x_sent))
+        ring_started.extend(sent)
+        if axis == "x" and max(pairs + 4, pack_pairs + 3) <= last_pair + 4:
+            pass_quarter(last_pair)
         for copy in sent:
             copy.wait_recv()
         value = ring_ref[first]
@@ -1361,7 +1438,7 @@
     sums_ref[...] = value
     for copy in core_sent:
         copy.wait_recv()
-    for copy in started:
+    for copy in started + ring_started:
         copy.wait_send()
     gather.finish()
     scatter.finish()
@@ -1375,7 +1452,8 @@
     pack_rows, pack_width = packs.shape[-2:]
     pairs, pack_pairs = (tokens // SPAN, pack_rows // SPAN)
     slots = sum(sizes.values())
-    quarter_copies = (sizes["x"] - 1) + (sizes["core"] - 1) * sizes["x"] + 1
+    quarter_copies = (sizes["x"] - 1) + (sizes["core"] - 1) * sizes["x"]
+    quarter_copies = max(1, pack_pairs * quarter_copies)
     vmem = pl.BlockSpec(memory_space=pltpu.VMEM)
     return pl.pallas_call(
         functools.partial(finish_kernel, sizes, pairs, pack_pairs),
@@ -1406,117 +1484,527 @@
     )(rows, packs.reshape(natural + (pack_rows, pack_width)), token_rows, head_grad, scalars)
 
 
+def side_lanes(router, gain_columns):
+    first = gain_columns[:, :1]
+    rest = gain_columns[:, 1:]
+    gap = LANES - SIDE_LANE - router.shape[1] - gain_columns.shape[1]
+    return jnp.concatenate([jnp.pad(router, ((0, 0), (SIDE_LANE, gap))), rest, first], axis=1)
+
+
+def row_tiles(values):
+    return values.reshape(-1, 16, LANES).transpose(1, 0, 2).reshape(16, -1)
+
+
 def own_pack_of(parts, seq_index, seq_count):
     mixer_in, mixer_x, mixer_out, channel, gains, router = [
         part.astype(jnp.bfloat16) for part in parts
     ]
-    tall, wide_rows = (mixer_in.shape[0], mixer_x.shape[0] // seq_count)
-    sides = jnp.pad(
-        jnp.concatenate([router, gains.T], axis=1),
-        ((0, 0), (0, LANES - router.shape[1] - gains.shape[0])),
-    )
-    top = jnp.concatenate(
-        [lax.dynamic_slice_in_dim(mixer_in, seq_index * D, D, 1), sides], axis=1
-    )
-    middle = jnp.concatenate(
-        [
-            lax.dynamic_slice_in_dim(mixer_out, seq_index * wide_rows, wide_rows, 0),
-            lax.dynamic_slice_in_dim(mixer_x, seq_index * wide_rows, wide_rows, 0),
+    rows = mixer_x.shape[0] // seq_count
+    some = mixer_in.shape[0] // seq_count
+    top = lax.dynamic_slice_in_dim(mixer_in, seq_index * D, D, 1)
+    middle = lax.dynamic_slice_in_dim(mixer_out, seq_index * rows, rows, 0)
+    x_rows = lax.dynamic_slice_in_dim(mixer_x, seq_index * rows, rows, 0)
+    extra = lax.dynamic_slice_in_dim(channel, seq_index * rows, rows, 1).T
+    extra = jnp.pad(extra, ((0, 0), (0, LANES - extra.shape[1])))
+    sides = lax.dynamic_slice_in_dim(
+        side_lanes(router, gains.T), seq_index * some, some, 0
+    )
+    extra = extra + jnp.pad(sides, ((0, rows - some), (0, 0)))
+    bottom = jnp.concatenate([row_tiles(x_rows), row_tiles(extra)], axis=1)
+    return jnp.concatenate([top, middle, bottom])
+
+
+def small_weights(packs, experts_total):
+    tall, rows = pack_heights()
+    seqs, groups = packs.shape[:2]
+    extra = packs[:, :, tall + rows :, D // 2 :].reshape(seqs, groups, 16, rows // 16, LANES)
+    extra = extra.transpose(1, 0, 3, 2, 4).reshape(groups, seqs, rows, LANES)
+    channel = extra.reshape(-1, LANES)[:, : CONV + 3 + STATE].T
+    sides = extra[:, :, : tall // seqs].reshape(D, LANES)
+    gains = jnp.concatenate([sides[:, -1:], sides[:, -3:-1]], axis=1).T
+    router = sides[:, SIDE_LANE : SIDE_LANE + experts_total]
+    return (channel.astype(jnp.float32), gains.astype(jnp.float32), router)
+
+
+def log_sum(value):
+    return jnp.maximum(value, 0.0) + jnp.log1p(jnp.exp(-jnp.abs(value)))
+
+
+def pack_heights():
+    seqs, groups = (lax.axis_size("seq"), lax.axis_size("group"))
+    return (D // groups, DI // (seqs * groups))
+
+
+def collect_middle(packs_ref, outx_ref):
+    seqs, groups = packs_ref.shape[:2]
+    tall, rows = pack_heights()
+
+    def one(step, carry):
+        group, seq = (lax.div(step, seqs), lax.rem(step, seqs))
+        start = step * rows
+        outx_ref[pl.ds(pl.multiple_of(start, 16), rows), 0:D] = packs_ref[
+            seq, group, tall : tall + rows
+        ]
+        for part in range(rows // 16):
+            outx_ref[pl.ds(pl.multiple_of(start + part * 16, 16), 16), D:] = packs_ref[
+                seq, group, tall + rows :, part * LANES : (part + 1) * LANES
+            ]
+        return carry
+
+    lax.fori_loop(0, seqs * groups, one, 0)
+
+
+def turned_step_weights(outx_ref):
+    both = outx_ref[:, D:].astype(jnp.float32)
+    lane = lax.broadcasted_iota(jnp.int32, both.shape, 1)
+    shifted = pltpu.roll(both, RANK, 1)
+    return jnp.where(lane < RANK, shifted, 0.0).astype(jnp.bfloat16)
+
+
+def mixer_forward_kernel(
+    experts_total,
+    x_ref,
+    packs_ref,
+    vec_ref,
+    gain_ref,
+    mask_ref,
+    router_ref,
+    mixed_ref,
+    moe_ref,
+    prob_ref,
+    z_ref,
+    pad_ref,
+    conv_ref,
+    act_ref,
+    dtin_ref,
+    dtpre_ref,
+    step_ref,
+    b_ref,
+    c_ref,
+    in_ref,
+    y_ref,
+    outx_ref,
+    keep_ref,
+    rate_ref,
+    halo_out,
+    halo_in,
+    out_buf,
+    in_buf,
+    ss,
+    rs,
+    halo_send,
+    halo_recv,
+):
+    meet(chain_peers())
+    seqs, groups = packs_ref.shape[:2]
+    tall, _ = pack_heights()
+    me = lax.axis_index("group")
+    x = x_ref[...]
+    tokens = x.shape[0]
+    normed = (x * inverse_rms(x) * gain_ref[0:1]).astype(jnp.bfloat16)
+    for seq in range(seqs):
+        block = matmul(normed, packs_ref[seq, :, 0:tall, 0:D].reshape(D, D))
+        first = seq * D
+        if first < DI:
+            pad_ref[8:, first : first + D] = block.astype(jnp.bfloat16).astype(jnp.float32)
+        else:
+            z_ref[:, first - DI : first - DI + D] = block
+    halo_out[...] = pad_ref[tokens:]
+    halo = pltpu.make_async_remote_copy(
+        src_ref=halo_out,
+        dst_ref=halo_in,
+        send_sem=halo_send,
+        recv_sem=halo_recv,
+        device_id=(lax.axis_index("seq"), lax.rem(me + 1, groups)),
+        device_id_type=MESH,
+    )
+    halo.start()
+    collect_middle(packs_ref, outx_ref)
+    rate_ref[...] = -jnp.exp(vec_ref[CONV + 3 : CONV + 3 + STATE])
+    keep_ref[...] = jnp.broadcast_to(mask_ref[:, CONV : CONV + 1], keep_ref.shape)
+    halo.wait_recv()
+    pad_ref[0:8] = halo_in[...] * jnp.where(me > 0, 1.0, 0.0)
+    conv = vec_ref[CONV : CONV + 1] + jnp.zeros_like(z_ref)
+    for tap in range(CONV):
+        first = 9 - CONV + tap
+        conv = (
+            conv
+            + vec_ref[tap : tap + 1]
+            * pad_ref[first : first + tokens]
+            * mask_ref[:, tap : tap + 1]
+        )
+    activated = conv * jax.nn.sigmoid(conv)
+    conv_ref[...] = conv
+    act_ref[...] = activated
+    projected = matmul(activated.astype(jnp.bfloat16), outx_ref[:, D:])
+    lane = lax.broadcasted_iota(jnp.int32, projected.shape, 1)
+    dt_input = jnp.where(lane < RANK, projected, 0.0).astype(jnp.bfloat16)
+    dtin_ref[...] = dt_input
+    dt_pre = matmul_nt(dt_input, turned_step_weights(outx_ref))
+    dtpre_ref[...] = dt_pre
+    step_ref[...] = log_sum(dt_pre + vec_ref[CONV + 1 : CONV + 2])
+    for n in range(STATE):
+        at = RANK + n
+        b_ref[:, n, :] = jnp.broadcast_to(projected[:, at : at + 1], (tokens, LANES))
+        at = RANK + STATE + n
+        c_ref[:, n, :] = jnp.broadcast_to(projected[:, at : at + 1], (tokens, LANES))
+    scan_forward_body(
+        step_ref,
+        act_ref,
+        b_ref,
+        c_ref,
+        keep_ref,
+        rate_ref,
+        y_ref,
+        in_ref,
+        out_buf,
+        in_buf,
+        ss,
+        rs,
+    )
+    scanned = y_ref[...] + vec_ref[CONV + 2 : CONV + 3] * act_ref[...]
+    y_ref[...] = scanned
+    gate_z = z_ref[...]
+    gated = (scanned * (gate_z * jax.nn.sigmoid(gate_z))).astype(jnp.bfloat16)
+    mixed = x + matmul(gated, outx_ref[:, :D])
+    mixed_ref[...] = mixed
+    moe_in = (mixed * inverse_rms(mixed) * gain_ref[1:2]).astype(jnp.bfloat16)
+    moe_ref[...] = moe_in
+    scores = matmul(moe_in, router_ref[...])
+    scores = jnp.where(lane < experts_total, scores, -1e30)
+    raised = jnp.exp(scores - jnp.max(scores, axis=1, keepdims=True))
+    prob_ref[...] = raised / jnp.sum(raised, axis=1, keepdims=True)
+    halo.wait_send()
+
+
+def mixer_forward_all(x, packs, vectors, gains, masks, router, collective_id):
+    tokens = x.shape[0]
+    wide_shape = jax.ShapeDtypeStruct((tokens, DI), jnp.float32)
+    state_shape = jax.ShapeDtypeStruct((tokens, STATE, LANES), jnp.float32)
+    vmem = pl.BlockSpec(memory_space=pltpu.VMEM)
+    return pl.pallas_call(
+        functools.partial(mixer_forward_kernel, router.shape[1]),
+        out_shape=(
+            jax.ShapeDtypeStruct((tokens, D), jnp.float32),
+            jax.ShapeDtypeStruct((tokens, D), jnp.bfloat16),
+            jax.ShapeDtypeStruct((tokens, LANES), jnp.float32),
+            wide_shape,
+            jax.ShapeDtypeStruct((tokens + 8, DI), jnp.float32),
+            wide_shape,
+            wide_shape,
+            jax.ShapeDtypeStruct((tokens, LANES), jnp.bfloat16),
+            wide_shape,
+            wide_shape,
+            state_shape,
+            state_shape,
+            jax.ShapeDtypeStruct((STATE, DI), jnp.float32),
+            wide_shape,
+        ),
+        in_specs=[vmem] * 6,
+        out_specs=(vmem,) * 14,
+        scratch_shapes=[
+            pltpu.VMEM((DI, D + LANES), jnp.bfloat16),
+            pltpu.VMEM((tokens, LANES), jnp.float32),
+            pltpu.VMEM((STATE, DI), jnp.float32),
+            pltpu.VMEM((8, DI), jnp.float32),
+            pltpu.VMEM((8, DI), jnp.float32),
+        ]
+        + scan_scratch(DI)
+        + [pltpu.SemaphoreType.DMA, pltpu.SemaphoreType.DMA],
+        compiler_params=pltpu.CompilerParams(
+            collective_id=collective_id, has_side_effects=True, vmem_limit_bytes=VMEM_LIMIT
+        ),
+        name="mixer_forward",
+    )(x, packs, vectors, gains, masks, jnp.pad(router, ((0, 0), (0, LANES - router.shape[1]))))
+
+
+def mixer_backward_kernel(
+    grad_ref,
+    side_ref,
+    x_ref,
+    packs_ref,
+    vec_ref,
+    gain_ref,
+    mask_ref,
+    z_ref,
+    pad_ref,
+    conv_ref,
+    act_ref,
+    dtin_ref,
+    dtpre_ref,
+    step_ref,
+    b_ref,
+    c_ref,
+    in_ref,
+    y_ref,
+    embed_ref,
+    gpack_ref,
+    outx_ref,
+    keep_ref,
+    rate_ref,
+    scan_grad_ref,
+    along_ref,
+    decayed_ref,
+    gb_ref,
+    gc_ref,
+    grate_ref,
+    prev_ref,
+    carry_ref,
+    gout_ref,
+    both_ref,
+    gpad_ref,
+    chan_ref,
+    turned_ref,
+    merged_ref,
+    halo_out,
+    halo_in,
+    out_buf,
+    in_buf,
+    ss,
+    rs,
+    halo_send,
+    halo_recv,
+):
+    meet(chain_peers())
+    seqs, groups = packs_ref.shape[:2]
+    tall, rows = pack_heights()
+    me = lax.axis_index("group")
+    tokens = x_ref.shape[0]
+    collect_middle(packs_ref, outx_ref)
+    rate_ref[...] = -jnp.exp(vec_ref[CONV + 3 : CONV + 3 + STATE])
+    keep_ref[...] = jnp.broadcast_to(mask_ref[:, CONV : CONV + 1], keep_ref.shape)
+    grad_low = grad_ref[...].astype(jnp.bfloat16)
+    grad_gated = matmul_nt(grad_low, outx_ref[:, :D])
+    gate_z, scanned = (z_ref[...], y_ref[...])
+    logistic = jax.nn.sigmoid(gate_z)
+    gate_act = gate_z * logistic
+    gated = (scanned * gate_act).astype(jnp.bfloat16)
+    gout_ref[:, :D] = matmul_tn(gated, grad_low).astype(jnp.bfloat16)
+    grad_scan = grad_gated * gate_act
+    scan_grad_ref[...] = grad_scan
+    grad_z = grad_gated * scanned * (logistic * (1.0 + gate_z * (1.0 - logistic)))
+    both_ref[:, DI:] = grad_z.astype(jnp.bfloat16)
+    chan_ref[...] = jnp.zeros_like(chan_ref)
+    chan_ref[CONV + 2 : CONV + 3] = jnp.sum(grad_scan * act_ref[...], axis=0, keepdims=True)
+    scan_backward_body(
+        step_ref,
+        act_ref,
+        b_ref,
+        c_ref,
+        keep_ref,
+        rate_ref,
+        in_ref,
+        scan_grad_ref,
+        along_ref,
+        decayed_ref,
+        gb_ref,
+        gc_ref,
+        grate_ref,
+        prev_ref,
+        carry_ref,
+        out_buf,
+        in_buf,
+        ss,
+        rs,
+    )
+    chan_ref[CONV + 3 : CONV + 3 + STATE] = grate_ref[...]
+    along, activated = (along_ref[...], act_ref[...])
+    grad_act = scan_grad_ref[...] * vec_ref[CONV + 2 : CONV + 3] + along * step_ref[...]
+    grad_step = decayed_ref[...] + along * activated
+    grad_dtpre = grad_step * jax.nn.sigmoid(dtpre_ref[...] + vec_ref[CONV + 1 : CONV + 2])
+    chan_ref[CONV + 1 : CONV + 2] = jnp.sum(grad_dtpre, axis=0, keepdims=True)
+    grad_dtlow = grad_dtpre.astype(jnp.bfloat16)
+    grad_wdt = matmul_tn(grad_dtlow, dtin_ref[...])
+    grad_proj = matmul(grad_dtlow, turned_step_weights(outx_ref))
+    lane = lax.broadcasted_iota(jnp.int32, grad_proj.shape, 1)
+    for n in range(STATE):
+        for first, ref in ((RANK, gb_ref), (RANK + STATE, gc_ref)):
+            column = jnp.sum(ref[:, n, :], axis=1, keepdims=True)
+            grad_proj = jnp.where(lane == first + n, column, grad_proj)
+    grad_proj = grad_proj.astype(jnp.bfloat16)
+    grad_wx = matmul_tn(activated.astype(jnp.bfloat16), grad_proj)
+    wide_lane = lax.broadcasted_iota(jnp.int32, grad_wx.shape, 1)
+    grad_wx = jnp.where(
+        wide_lane < RANK + 2 * STATE, grad_wx, pltpu.roll(grad_wdt, RANK + 2 * STATE, 1)
+    )
+    gout_ref[:, D:] = grad_wx.astype(jnp.bfloat16)
+    grad_act = grad_act + matmul_nt(grad_proj, outx_ref[:, D:])
+    conv = conv_ref[...]
+    logistic = jax.nn.sigmoid(conv)
+    grad_conv = grad_act * (logistic * (1.0 + conv * (1.0 - logistic)))
+    chan_ref[CONV : CONV + 1] = jnp.sum(grad_conv, axis=0, keepdims=True)
+    gpad_ref[...] = jnp.zeros_like(gpad_ref)
+    for tap in range(CONV):
+        same = grad_conv * mask_ref[:, tap : tap + 1]
+        first = 9 - CONV + tap
+        chan_ref[tap : tap + 1] = jnp.sum(
+            same * pad_ref[first : first + tokens], axis=0, keepdims=True
+        )
+        gpad_ref[first : first + tokens] += vec_ref[tap : tap + 1] * same
+    halo_out[...] = gpad_ref[0:8]
+    halo = pltpu.make_async_remote_copy(
+        src_ref=halo_out,
+        dst_ref=halo_in,
+        send_sem=halo_send,
+        recv_sem=halo_recv,
+        device_id=(lax.axis_index("seq"), lax.rem(me + groups - 1, groups)),
+        device_id_type=MESH,
+    )
+    halo.start()
+    for first in range(0, DI, LANES):
+        turned_ref[first : first + LANES] = chan_ref[:, first : first + LANES].T
+
+    def place_middle(step, carry):
+        group, seq = (lax.div(step, seqs), lax.rem(step, seqs))
+        start = step * rows
+        gpack_ref[seq, group, tall : tall + rows] = gout_ref[
+            pl.ds(pl.multiple_of(start, 16), rows), 0:D
+        ]
+        for part in range(rows // 16):
+            gpack_ref[seq, group, tall + rows :, part * LANES : (part + 1) * LANES] = gout_ref[
+                pl.ds(pl.multiple_of(start + part * 16, 16), 16), D:
+            ]
+        return carry
+
+    lax.fori_loop(0, seqs * groups, place_middle, 0)
+    halo.wait_recv()
+    gpad_ref[tokens : tokens + 8] += halo_in[...] * jnp.where(me < groups - 1, 1.0, 0.0)
+    both_ref[:, :DI] = gpad_ref[8 : 8 + tokens].astype(jnp.bfloat16)
+    x = x_ref[...]
+    scale = inverse_rms(x)
+    normed = (x * scale * gain_ref[0:1]).astype(jnp.bfloat16)
+    grad_normed = jnp.zeros((tokens, D), jnp.float32)
+    for seq in range(seqs):
+        part = both_ref[:, seq * D : (seq + 1) * D]
+        grad_normed += matmul_nt(part, packs_ref[seq, :, 0:tall, 0:D].reshape(D, D))
+        gpack_ref[seq, :, 0:tall, 0:D] = (
+            matmul_tn(normed, part).astype(jnp.bfloat16).reshape(groups, tall, D)
+        )
+    scaled = grad_normed * gain_ref[0:1]
+    grad_x = scale * scaled - x * scale**3 * jnp.mean(scaled * x, axis=-1, keepdims=True)
+    embed_ref[...] = (grad_ref[...] + grad_x).astype(jnp.bfloat16)
+    grad_gain = jnp.sum(grad_normed * x * scale, axis=0, keepdims=True)
+    grad_gain = jnp.broadcast_to(grad_gain, (LANES, D)).T
+    side_lane = lax.broadcasted_iota(jnp.int32, side_ref.shape, 1)
+    merged_ref[...] = jnp.where(side_lane == LANES - 1, grad_gain, side_ref[...])
+    some = tall // seqs
+
+    def place_extra(step, carry):
+        group, seq = (lax.div(step, seqs), lax.rem(step, seqs))
+        start = pl.multiple_of(step * rows, 16)
+        first = pl.multiple_of(group * tall + seq * some, 8)
+        turned_ref[pl.ds(start, some)] += merged_ref[pl.ds(first, some)]
+        for part in range(rows // 16):
+            lanes = pl.ds(D // 2 + part * LANES, LANES)
+            gpack_ref[seq, group, tall + rows :, lanes] = turned_ref[
+                pl.ds(pl.multiple_of(start + part * 16, 16), 16)
+            ].astype(jnp.bfloat16)
+        return carry
+
+    lax.fori_loop(0, seqs * groups, place_extra, 0)
+    halo.wait_send()
+
+
+def mixer_backward_all(grad, sides, x, packs, vectors, gains, masks, saved, collective_id):
+    tokens = x.shape[0]
+    vmem = pl.BlockSpec(memory_space=pltpu.VMEM)
+    wide = (tokens, DI)
+    return pl.pallas_call(
+        mixer_backward_kernel,
+        out_shape=(
+            jax.ShapeDtypeStruct((tokens, D), jnp.bfloat16),
+            jax.ShapeDtypeStruct(packs.shape, jnp.bfloat16),
+        ),
+        in_specs=[vmem] * (7 + len(saved)),
+        out_specs=(vmem,) * 2,
+        scratch_shapes=[
+            pltpu.VMEM((DI, D + LANES), jnp.bfloat16),
+            pltpu.VMEM((tokens, LANES), jnp.float32),
+            pltpu.VMEM((STATE, DI), jnp.float32),
+            pltpu.VMEM(wide, jnp.float32),
+            pltpu.VMEM(wide, jnp.float32),
+            pltpu.VMEM(wide, jnp.float32),
+            pltpu.VMEM((tokens, STATE, LANES), jnp.float32),
+            pltpu.VMEM((tokens, STATE, LANES), jnp.float32),
+            pltpu.VMEM((STATE, DI), jnp.float32),
+            pltpu.VMEM((tokens, STATE, DI), jnp.float32),
+            pltpu.VMEM((STATE, DI), jnp.float32),
+            pltpu.VMEM((DI, D + LANES), jnp.bfloat16),
+            pltpu.VMEM((tokens, 2 * DI), jnp.bfloat16),
+            pltpu.VMEM((tokens + 8, DI), jnp.float32),
+            pltpu.VMEM((LANES, DI), jnp.float32),
+            pltpu.VMEM((DI, LANES), jnp.float32),
+            pltpu.VMEM((D, LANES), jnp.float32),
+            pltpu.VMEM((8, DI), jnp.float32),
+            pltpu.VMEM((8, DI), jnp.float32),
+        ]
+        + scan_scratch(DI)
+        + [pltpu.SemaphoreType.DMA, pltpu.SemaphoreType.DMA],
+        compiler_params=pltpu.CompilerParams(
+            collective_id=collective_id, has_side_effects=True, vmem_limit_bytes=VMEM_LIMIT
+        ),
+        name="mixer_backward",
+    )(grad, sides, x, packs, vectors, gains, masks, *saved)
+
+
+def update_kernel(quarters_ref, sums_ref, *refs):
+    inputs, outputs, turned_ref, side_ref = (refs[:18], refs[18:36], refs[36], refs[37])
+    seqs = quarters_ref.shape[0]
+    tall, rows = pack_heights()
+    norm = jnp.sqrt(sums_ref[0:1, 0:1])
+    clip_factor = jnp.minimum(1.0, CLIP / (norm + 1e-06))
+
+    def renew(which, index, gradient, rate):
+        master, moment, average = (inputs[3 * which + k] for k in range(3))
+        fresh = renewed(
+            master[index], moment[index], average[index], gradient, clip_factor, rate
+        )
+        for k in range(3):
+            outputs[3 * which + k][index] = fresh[k]
+
+    for seq in range(seqs):
+        columns = slice(seq * D, (seq + 1) * D)
+        renew(0, (slice(None), columns), quarters_ref[seq, 0:tall, :D].astype(jnp.float32), LRATE)
+        own = slice(seq * rows, (seq + 1) * rows)
+        middle = quarters_ref[seq, tall : tall + rows, :].astype(jnp.float32)
+        renew(2, (own,), middle, LRATE)
+        bottom = quarters_ref[seq, tall + rows :, :].astype(jnp.float32)
+        for part in range(rows // 16):
+            first = seq * rows + part * 16
+            lanes = slice(part * LANES, (part + 1) * LANES)
+            renew(1, (slice(first, first + 16),), bottom[:, lanes], LRATE)
+            lanes = slice(D // 2 + part * LANES, D // 2 + (part + 1) * LANES)
+            turned_ref[first : first + 16] = bottom[:, lanes]
+        some = tall // seqs
+        side_ref[seq * some : (seq + 1) * some] = turned_ref[seq * rows : seq * rows + some]
+    width = inputs[9].shape[1]
+    turned_ref[seqs * rows :] = jnp.zeros_like(turned_ref[seqs * rows :])
+    side_ref[tall:] = jnp.zeros_like(side_ref[tall:])
+    everything = (slice(None),)
+    renew(3, everything, turned_ref[...].T[0 : CONV + 3 + STATE, 0:width], CHANNEL_LRATE)
+    gains = side_ref[...].T[:, 0:tall]
+    renew(4, everything, jnp.concatenate([gains[-1:], gains[-3:-1]], axis=0), LRATE)
+    router_lanes = slice(SIDE_LANE, SIDE_LANE + inputs[15].shape[1])
+    renew(5, everything, side_ref[0:tall, router_lanes], LRATE)
+
+
+def update_all(quarters, sums, states):
+    vmem = pl.BlockSpec(memory_space=pltpu.VMEM)
+    flat = [part for state in states for part in state]
+    tall, rows = pack_heights()
+    height = -(-quarters.shape[0] * rows // LANES) * LANES
+    return pl.pallas_call(
+        update_kernel,
+        out_shape=tuple(jax.ShapeDtypeStruct(part.shape, part.dtype) for part in flat),
+        in_specs=[vmem] * (2 + len(flat)),
+        out_specs=(vmem,) * len(flat),
+        scratch_shapes=[
+            pltpu.VMEM((height, LANES), jnp.float32),
+            pltpu.VMEM((-(-tall // LANES) * LANES, LANES), jnp.float32),
         ],
-        axis=1,
-    )
-    bottom = channel_tiles(
-        lax.dynamic_slice_in_dim(channel, seq_index * wide_rows, wide_rows, 1)
-    )
-    return jnp.concatenate([top, middle, bottom])
-
-
-def channel_tiles(channel):
-    lead = [(0, 0)] * (channel.ndim - 2)
-    rows, width = channel.shape[-2:]
-    first = jnp.pad(channel[..., :16, :], lead + [(0, 0), (0, LANES - width)])
-    second = jnp.pad(channel[..., 16:, :], lead + [(0, 32 - rows), (0, D - width)])
-    return jnp.concatenate([first, second], axis=-1)
-
-
-def weights_of(packs, experts_total):
-    seqs, groups = packs.shape[:2]
-    tall, wide_rows = (D // groups, DI // (seqs * groups))
-    top, middle = (packs[:, :, :tall], packs[:, :, tall : tall + wide_rows])
-    bottom = packs[:, :, tall + wide_rows :]
-    weight_in = top[..., :D].transpose(1, 2, 0, 3).reshape(D, -1)
-    sides = top[0, :, :, D:].reshape(D, LANES)
-    weight_out = middle[..., :D].transpose(1, 0, 2, 3).reshape(-1, D)
-    weight_x = middle[..., D:].transpose(1, 0, 2, 3).reshape(-1, LANES)
-    rows = CONV + 3 + STATE
-    channel = jnp.concatenate(
-        [
-            bottom[..., :16, :wide_rows].transpose(2, 1, 0, 3).reshape(16, -1),
-            bottom[..., : rows - 16, LANES : LANES + wide_rows]
-            .transpose(2, 1, 0, 3)
-            .reshape(rows - 16, -1),
-        ]
-    )
-    router = sides[:, :experts_total]
-    gains = sides[:, experts_total : experts_total + 3].T
-    return (weight_in, weight_x, weight_out, channel, gains, router)
-
-
-def grad_packs(parts, seqs, groups):
-    grad_in, grad_x, grad_out, grad_channel, grad_gains, grad_router = [
-        part.astype(jnp.bfloat16) for part in parts
-    ]
-    tall, wide_rows = (D // groups, DI // (seqs * groups))
-    sides = jnp.pad(
-        jnp.concatenate([grad_router, grad_gains.T], axis=1),
-        ((0, 0), (0, LANES - grad_router.shape[1] - grad_gains.shape[0])),
-    ).reshape(1, groups, tall, LANES)
-    sides = jnp.pad(sides, ((0, seqs - 1), (0, 0), (0, 0), (0, 0)))
-    top = jnp.concatenate(
-        [grad_in.reshape(groups, tall, seqs, D).transpose(2, 0, 1, 3), sides], axis=3
-    )
-    middle = jnp.concatenate(
-        [
-            part.reshape(groups, seqs, wide_rows, part.shape[1]).transpose(1, 0, 2, 3)
-            for part in (grad_out, grad_x)
-        ],
-        axis=3,
-    )
-    rows = grad_channel.shape[0]
-    bottom = channel_tiles(
-        grad_channel.reshape(rows, groups, seqs, wide_rows).transpose(2, 1, 0, 3)
-    )
-    return jnp.concatenate([top, middle, bottom], axis=2)
-
-
-def own_grads_of(quarters, experts_total):
-    seqs, _, width = quarters.shape
-    tall = quarters.shape[1] - 16 - DI // (seqs * lax.axis_size("group"))
-    wide_rows = quarters.shape[1] - 16 - tall
-    values = quarters.astype(jnp.float32)
-    top, middle = (values[:, :tall], values[:, tall : tall + wide_rows])
-    bottom = values[:, tall + wide_rows :]
-    grad_in = top[..., :D].transpose(1, 0, 2).reshape(tall, -1)
-    sides = top[0, :, D:]
-    grad_out = middle[..., :D].reshape(-1, D)
-    grad_x = middle[..., D:].reshape(-1, LANES)
-    rows = CONV + 3 + STATE
-    grad_channel = jnp.concatenate(
-        [
-            bottom[:, :16, :wide_rows].transpose(1, 0, 2).reshape(16, -1),
-            bottom[:, : rows - 16, LANES : LANES + wide_rows]
-            .transpose(1, 0, 2)
-            .reshape(rows - 16, -1),
-        ]
-    )
-    return (
-        grad_in,
-        grad_x,
-        grad_out,
-        grad_channel,
-        sides[:, experts_total : experts_total + 3].T,
-        sides[:, :experts_total],
-    )
+        compiler_params=pltpu.CompilerParams(vmem_limit_bytes=VMEM_LIMIT),
+        name="update_all",
+    )(quarters, sums, *flat)
 
 
 def from_behind(value, axis, by):
@@ -1576,6 +2064,20 @@
         (where_at[None, :, None] == doc_begins[:, None, :]).astype(jnp.float32), axis=2
     )
     return (segment, weight, 1.0 - starting)
+
+
+def spread_weights(doc_lengths, tokens, groups):
+    ends = jnp.cumsum(doc_lengths, axis=1)
+    begins = ends - doc_lengths
+    shape = (tokens // SPAN, groups * SPAN)
+    pair, lane = (lax.broadcasted_iota(jnp.int32, shape, axis) for axis in range(2))
+    where_at = (lane // SPAN * tokens + pair * SPAN + lane % SPAN)[:, None, :]
+    total = jnp.zeros((shape[0], doc_lengths.shape[0], shape[1]), jnp.float32)
+    for doc in range(doc_lengths.shape[1]):
+        inside = (where_at >= begins[None, :, doc, None]) & (where_at < ends[None, :, doc, None])
+        share = 1.0 / doc_lengths[:, doc].astype(jnp.float32)
+        total = total + jnp.where(inside, share[None, :, None], 0.0)
+    return total.reshape(-1, shape[1])
 
 
 def lane_copies(columns):
@@ -1844,15 +2346,16 @@
     vocab_start = (seq_index * group_count + group_index) * own_vocab
     column_ids = jnp.arange(own_vocab, dtype=jnp.int32)
     wide_rows = DI // (seq_count * group_count)
-    compact = devices * tokens <= 4096 and 2 * DI == seq_count * D
+    compact = devices * tokens <= 4096 and 2 * DI == seq_count * D and 16 * wide_rows == D
     if compact:
-        table_turned = jnp.pad(table_low.T, ((0, 0), (0, -own_vocab % LANES)))
         own_pack = own_pack_of(mixer_parts, seq_index, seq_count)
-        numbers_all, packs, embedded = start_all(numbers, own_pack, table_turned, own_vocab, 1)
+        numbers_all, packs, embedded, table_padded, table_turned, token_local, target_local = (
+            start_all(numbers, own_pack, vocab_table, 1)
+        )
+        numbers_all = numbers_all.reshape((devices,) + numbers.shape)
         packs = packs.reshape((seq_count, group_count) + own_pack.shape)
-        weight_in, weight_x, weight_out, channel_low, gains_low, router_low = weights_of(
-            packs, experts_total
-        )
+        channel_vals, gain_vals, router_low = small_weights(packs, experts_total)
+        router_vals = router_low.astype(jnp.float32)
     else:
         numbers_all = share_small(numbers, 1)
     from_groups = jnp.swapaxes(numbers_all[:group_count, : 2 * sequences], 0, 1)
@@ -1872,8 +2375,9 @@
         held_token = held_token.astype(jnp.bfloat16)
         looked_up = matmul(held_token, table_low).astype(jnp.bfloat16)
         embedded = scatter_all(looked_up.reshape(devices, tokens, D), 3)
-    channel_vals = channel_low.astype(jnp.float32)
-    gain_vals = gains_low.astype(jnp.float32)
+        channel_vals = channel_low.astype(jnp.float32)
+        gain_vals = gains_low.astype(jnp.float32)
+        router_vals = router_low.astype(jnp.float32)
 
     segment_all, weight_all, keep_all = doc_layout(
         doc_lengths, group_index * tokens - CONV + 1, tokens + CONV - 1
@@ -1881,16 +2385,34 @@
     own_segment = lax.dynamic_index_in_dim(segment_all, seq_index, 0, keepdims=False)
     keeping = lax.dynamic_index_in_dim(keep_all, seq_index, 0, keepdims=False)[CONV - 1 :]
     own_weight = lax.dynamic_index_in_dim(weight_all, seq_index, 0, keepdims=False)[CONV - 1 :]
-    _, every_weight, _ = doc_layout(doc_lengths, 0, tokens * group_count)
-    row_weight = every_weight.reshape(-1)
-    mixed_out, kept_values = mixer_forward(
-        embedded, own_segment, keeping, weight_in, weight_x, weight_out, channel_vals, gain_vals[0]
-    )
-    scale_mid = inverse_rms(mixed_out)
-    moe_in = (mixed_out * scale_mid * gain_vals[1]).astype(jnp.bfloat16)
     chosen = choice_of(expert_ids.reshape(-1), experts_total)
+    if compact:
+        same = [
+            (own_segment[tap : tap + tokens] == own_segment[CONV - 1 :]).astype(jnp.float32)
+            for tap in range(CONV)
+        ]
+        masks = jnp.stack(same + [keeping], axis=1)
+        vectors = jnp.pad(channel_vals, ((0, 1), (0, 0)))
+        mixed_out, moe_in, probability, *saved = mixer_forward_all(
+            embedded, packs, vectors, gain_vals, masks, router_low, 4
+        )
+        probability = probability[:, :experts_total]
+        scale_mid = inverse_rms(mixed_out)
+    else:
+        mixed_out, kept_values = mixer_forward(
+            embedded,
+            own_segment,
+            keeping,
+            weight_in,
+            weight_x,
+            weight_out,
+            channel_vals,
+            gain_vals[0],
+        )
+        scale_mid = inverse_rms(mixed_out)
+        moe_in = (mixed_out * scale_mid * gain_vals[1]).astype(jnp.bfloat16)
+        probability = jax.nn.softmax(matmul(moe_in, router_low), axis=-1)
     select = dispatch_table(routes_all, seq_index * local_experts, local_experts, capacity)
-    probability = jax.nn.softmax(matmul(moe_in, router_low), axis=-1)
     gate_value = jnp.sum(probability * chosen, axis=1)
     arrived = to_slots(select, gather_all(moe_in, 6), local_experts, capacity)
     before = jnp.einsum("erd,efd->erf", arrived, up_weight, preferred_element_type=jnp.float32)
@@ -1905,14 +2427,6 @@
     scale_out = inverse_rms(hidden)
     final_low = (hidden * scale_out * gain_vals[2]).astype(jnp.bfloat16)
     if compact:
-
-        def spread(values):
-            split = values.reshape(seq_count, group_count, tokens // SPAN, SPAN)
-            return split.transpose(2, 0, 1, 3).reshape(-1, group_count * SPAN)
-
-        table_padded = jnp.pad(table_low, ((0, -own_vocab % 16), (0, 0)))
-        target_local = targets_all - vocab_start
-        target_local = spread(jnp.where(target_local < own_vocab, target_local, -1))
         all_final, stats = head_forward(final_low, table_padded, own_vocab, target_local, 7)
         own_entropy = (stats[0] - stats[1]).reshape(-1, seq_count, group_count, SPAN)
         own_entropy = lax.dynamic_index_in_dim(own_entropy, seq_index, 1, keepdims=False)
@@ -1925,7 +2439,7 @@
             own_vocab,
             target_local,
             stats[0],
-            spread(row_weight),
+            spread_weights(doc_lengths, tokens, group_count),
             10,
         )
     else:
@@ -1941,6 +2455,8 @@
         levels, entropy = combine_stats(parts, 7)
         log_total = levels[:, 0].reshape(-1)
         loss_part = jnp.sum(own_weight * entropy[0])
+        _, every_weight, _ = doc_layout(doc_lengths, 0, tokens * group_count)
+        row_weight = every_weight.reshape(-1)
         grad_logits = (
             row_weight[:, None]
             * (jnp.exp(logits - log_total[:, None]) - hit_target.astype(jnp.float32))
@@ -1967,41 +2483,52 @@
     grad_moe_in = grad_moe_in.astype(jnp.bfloat16).astype(jnp.float32)
     grad_router_logits = (grad_gate * gate_value)[:, None] * (chosen - probability)
     grad_moe_in = grad_moe_in + jnp.dot(
-        grad_router_logits, router_low.astype(jnp.float32).T, precision=HIGHEST
+        grad_router_logits, router_vals.T, precision=HIGHEST
     )
     grad_router = jnp.dot(moe_in.astype(jnp.float32).T, grad_router_logits, precision=HIGHEST)
     grad_mid, grad_gain_mid = norm_back(mixed_out, scale_mid, gain_vals[1], grad_moe_in)
     grad_mixed = grad_hidden + grad_mid
-    grad_embedded, grad_win, grad_wx, grad_wout, grad_channel, grad_gain_in = mixer_backward(
-        grad_mixed,
-        embedded,
-        kept_values,
-        weight_in,
-        weight_x,
-        weight_out,
-        channel_vals,
-        gain_vals[0],
-    )
-    grad_gains = jnp.stack([grad_gain_in, grad_gain_mid, grad_gain_out])
-    mixer_wholes = (grad_win, grad_wx, grad_wout, grad_channel, grad_gains, grad_router)
+    if compact:
+        gain_columns = jnp.stack([grad_gain_out * 0.0, grad_gain_mid, grad_gain_out], axis=1)
+        grad_embedded, grad_pack = mixer_backward_all(
+            grad_mixed,
+            side_lanes(grad_router, gain_columns),
+            embedded,
+            packs,
+            vectors,
+            gain_vals,
+            masks,
+            saved,
+            5,
+        )
+    else:
+        grad_embedded, grad_win, grad_wx, grad_wout, grad_channel, grad_gain_in = mixer_backward(
+            grad_mixed,
+            embedded,
+            kept_values,
+            weight_in,
+            weight_x,
+            weight_out,
+            channel_vals,
+            gain_vals[0],
+        )
+        grad_gains = jnp.stack([grad_gain_in, grad_gain_mid, grad_gain_out])
+        mixer_wholes = (grad_win, grad_wx, grad_wout, grad_channel, grad_gains, grad_router)
     grad_experts = jnp.stack([grad_up, grad_down])
     experts_square = jnp.sum(grad_experts * grad_experts)
     if compact:
-        token_local = tokens_all - vocab_start
-        token_local = spread(jnp.where(token_local < own_vocab, token_local, -1))
         scalars = jnp.concatenate(
             [jnp.full((4, LANES), experts_square), jnp.full((4, LANES), loss_part)], axis=0
         )
         table_grad, quarters, sums = finish_all(
-            grad_embedded.astype(jnp.bfloat16),
-            grad_packs(mixer_wholes, seq_count, group_count),
+            grad_embedded,
+            grad_pack,
             token_local,
             table_grad,
             scalars,
             9,
         )
         table_grad = table_grad[:own_vocab]
-        mixer_grads = own_grads_of(quarters, experts_total)
     else:
         all_grad_embed = gather_all(grad_embedded.astype(jnp.bfloat16), 6).reshape(-1, D)
         table_grad = table_grad + matmul_tn(held_token, all_grad_embed)
@@ -2028,16 +2555,23 @@
     table_new = renewed(
         vocab_table, vocab_table_mom, vocab_table_ema, table_grad, clip_factor, LRATE
     )
-    in_new = renewed(mixer_in, mixer_in_mom, mixer_in_ema, mixer_grads[0], clip_factor, LRATE)
-    x_new = renewed(mixer_x, mixer_x_mom, mixer_x_ema, mixer_grads[1], clip_factor, LRATE)
-    out_new = renewed(mixer_out, mixer_out_mom, mixer_out_ema, mixer_grads[2], clip_factor, LRATE)
-    channel_new = renewed(
-        channel, channel_mom, channel_ema, mixer_grads[3], clip_factor, CHANNEL_LRATE
-    )
-    gains_new = renewed(
-        norm_gains, norm_gains_mom, norm_gains_ema, mixer_grads[4], clip_factor, LRATE
-    )
-    router_new = renewed(router, router_mom, router_ema, mixer_grads[5], clip_factor, LRATE)
+    mixer_states = (
+        (mixer_in, mixer_in_mom, mixer_in_ema),
+        (mixer_x, mixer_x_mom, mixer_x_ema),
+        (mixer_out, mixer_out_mom, mixer_out_ema),
+        (channel, channel_mom, channel_ema),
+        (norm_gains, norm_gains_mom, norm_gains_ema),
+        (router, router_mom, router_ema),
+    )
+    if compact:
+        fresh = update_all(quarters, sums, mixer_states)
+    else:
+        rates = (LRATE, LRATE, LRATE, CHANNEL_LRATE, LRATE, LRATE)
+        fresh = [
+            part
+            for state, gradient, rate in zip(mixer_states, mixer_grads, rates)
+            for part in renewed(*state, gradient, clip_factor, rate)
+        ]
     experts_new = renewed(experts, experts_mom, experts_ema, grad_experts, clip_factor, LRATE)
     return (
         loss_sum,
@@ -2046,24 +2580,7 @@
         table_new[0],
         table_new[1],
         table_new[2],
-        in_new[0],
-        in_new[1],
-        in_new[2],
-        x_new[0],
-        x_new[1],
-        x_new[2],
-        out_new[0],
-        out_new[1],
-        out_new[2],
-        channel_new[0],
-        channel_new[1],
-        channel_new[2],
-        gains_new[0],
-        gains_new[1],
-        gains_new[2],
-        router_new[0],
-        router_new[1],
-        router_new[2],
+        *fresh,
         experts_new[0],
         experts_new[1],
         experts_new[2],

time: 871 us -> 731 us (0.84)
  local copies, waits for them, and re-layouts: 96.7 us -> 26.2 us
  other arithmetic: 109 us -> 60.4 us
  matrix products: 59.2 us -> 34.9 us
    pallas_call x2 -> x3, Pallas kernels: 69 us -> 108 us  [the longest x1 58.4 us: mixer_backward_all(): pl.pallas_call(mixer_backward_kernel, out_shape=(jax.ShapeDtypeStruct((to...]
    dot_general x14 -> x1, matrix products: 22.3 us -> 1.53 us  [per_device(): jnp.dot(grad_router_logits, router_vals.T, precision=HIGHEST)]
    reshape x10 -> x2, local copies, waits for them, and re-layouts: 20.9 us -> 0.11 us  [the longest x1 0.11 us: small_weights(): packs[:, :, tall + rows:, D // 2:]]
    transpose x16 -> x2, local copies, waits for them, and re-layouts: 20.5 us -> 0.88 us  [the longest x1 0.81 us: own_pack_of(): extra = lax.dynamic_slice_in_dim(channel, seq_index * rows, rows, 1).T]
    pallas_call x1, Pallas kernels: 106 us -> 87.4 us  [start_all(): pl.pallas_call(functools.partial(start_kernel, sizes, pairs, pack_pairs,...]
    pallas_call x1, Pallas kernels: 105 us -> 93.2 us  [finish_all(): pl.pallas_call(functools.partial(finish_kernel, sizes, pairs, pack_pairs)...]
    mul x7 -> x2, other arithmetic: 9.38 us -> 0.17 us  [the longest x1 0.17 us: per_device(): grad_gain_out * 0.0]
    concatenate x19 -> x0, local copies, waits for them, and re-layouts: 8.71 us -> none  [the longest x17 7.67 us: mixer_backward(): jnp.concatenate([jnp.stack(grad_taps), jnp.sum(grad_conv, axis=0)[None],...]
  transfers between devices with their start and end apart: 2 -> 0, of which waited for: 0 -> 0; matrix products, arithmetic and copies ran while one was open for 9% -> 0% of each run, Pallas kernels for 0% -> 0%
where the time goes in v1:
time: 731 us; the launch traced here: 722 us
  Pallas kernels  597 us (82%)
  other arithmetic  60.4 us (8%)
  matrix products  34.9 us (5%)
  local copies, waits for them, and re-layouts  26.2 us (4%)
    pallas_call x1, Pallas kernels, finish_all(): pl.pallas_call(functools.partial(finish_kernel, sizes, pairs, pack_pairs)...  93.2 us
    pallas_call x2, Pallas kernels, scatter_all(): pl.pallas_call(functools.partial(scatter_kernel, sizes, pairs), out_shape...  90.9 us
    pallas_call x1, Pallas kernels, start_all(): pl.pallas_call(functools.partial(start_kernel, sizes, pairs, pack_pairs,...  87.4 us
    pallas_call x2, Pallas kernels, gather_all(): pl.pallas_call(functools.partial(gather_kernel, sizes, pieces), out_shape...  75 us
    pallas_call x1, Pallas kernels, head_backward(): pl.pallas_call(functools.partial(head_backward_kernel, sizes, pairs, own_...  72.1 us
    pallas_call x1, Pallas kernels, head_forward(): pl.pallas_call(functools.partial(head_forward_kernel, sizes, pairs, own_v...  69.7 us
    pallas_call x1, Pallas kernels, mixer_backward_all(): pl.pallas_call(mixer_backward_kernel, out_shape=(jax.ShapeDtypeStruct((to...  58.4 us
    pallas_call x1, Pallas kernels, mixer_forward_all(): pl.pallas_call(functools.partial(mixer_forward_kernel, router.shape[1]),...  44.2 us

profile of v1, /device:TPU:0, one launch (start us, length us, event | category | flops | bytes accessed | tf_op | source)
XLA Modules:
  0.0 721.6 jit_solution(18271145859843190991)
XLA Ops:
  0.7 0.7 convert_bitcast_fusion.1
  1.4 0.7 convert_element_type.229
  2.2 0.8 fusion.35
  3.1 0.8 dynamic-slice_convert_fusion.2
  3.8 0.9 dynamic-slice_convert_fusion.1
  4.8 1.0 dynamic-slice_convert_fusion
  5.7 0.7 maximum_maximum_fusion.pack_ref
  6.5 0.7 pad_add_fusion.1
  7.2 0.6 pad.31.number_ref
  7.8 87.4 %start_all.1 = (s32[2,2,4,2,16,128]{5,4,3,2,1,0:T(8,128)}, bf16[2,2,4,2,160,768]{5,4,3,2,1,0:T(8,128)(2,1)}, f32[128,768]{1,0:T(8,128)}, bf16[1584,768]{1,0:T(8,...) custom-call(s32[16,128]{1,0:T(8,128)} %pad.31.number_ref, ...), custom_call_target="tpu_custom_call" | custom-call | tf_op jit(solution)/shard_map/start_all/pallas_call | solution.py:1282
  95.2 1.1 slice.211
  96.9 0.6 convert_bitcast_fusion.gain_ref
  97.7 0.7 pad.37.router_ref
  98.6 0.7 pad_convert_fusion.vec_ref
  99.9 0.7 copy.179.mask_ref
  100.7 44.2 %mixer_forward.1 = (f32[128,768]{1,0:T(8,128)}, bf16[128,768]{1,0:T(8,128)(2,1)}, f32[128,128]{1,0:T(8,128)}, f32[128,1536]{1,0:T(8,128)}, f32[136,1536]{1,0:T(8...) custom-call(f32[128,768]{1,0:T(8,128)} %get-tuple-element.75.x_ref, ...), custom_call_target="tpu_custom_call" | custom-call | tf_op jit(solution)/shard_map/mixer_forward/pallas_call | solution.py:1685
  144.9 37.1 %gather_all.2 = bf16[32,128,768]{2,1,0:T(8,128)(2,1)} custom-call(bf16[128,768]{1,0:T(8,128)(2,1)} %get-tuple-element.80.own_ref), custom_call_target="tpu_custom_call" | custom-call | tf_op jit(solution)/shard_map/gather_all/pallas_call | solution.py:148
  182.1 0.9 slice.217
  183.1 1.7 fusion.10
  184.9 3.9 convolution_convert_fusion.5
  189.2 1.1 slice-done.2
  190.3 2.7 convert_element_type.246
  193.0 3.6 fusion.11
  196.6 1.8 convolution_convert_fusion.3
  198.8 4.5 convolution_convert_fusion.1
  203.4 46.5 %scatter_all.2 = f32[128,768]{1,0:T(8,128)} custom-call(bf16[2,2,4,2,128,768]{5,4,3,2,1,0:T(8,128)(2,1)} %bitcast.112), custom_call_target="tpu_custom_call" | custom-call | tf_op jit(solution)/shard_map/scatter_all/pallas_call | solution.py:341
  250.1 1.9 multiply_reduce_fusion.6
  252.0 0.8 multiply_convert_fusion.2.own_ref
  252.8 69.7 %head_forward.1 = (bf16[2,2,4,2,128,768]{5,4,3,2,1,0:T(8,128)(2,1)}, f32[2,16,256]{2,1,0:T(8,128)}) custom-call(bf16[128,768]{1,0:T(8,128)(2,1)} %multiply_convert_fusion.2.own_ref, bf16[1584,768]{1,0:T(8,128)(2,1)} %get-tuple-element.81.table_ref, s32[16,256]{1,0:T(8,128)} %get-tuple-element.82.target_ref), custom_call_target="tpu_custom_call" | custom-call | tf_op jit(solution)/shard_map/head_forward/pallas_call | solution.py:532
  322.6 1.3 slice_subtract_fusion
  326.9 0.7 select_add_fusion.weight_ref
  327.6 72.1 %head_backward.1 = (f32[128,768]{1,0:T(8,128)}, f32[1584,768]{1,0:T(8,128)}) custom-call(bf16[2,2,4,2,128,768]{5,4,3,2,1,0:T(8,128)(2,1)} %get-tuple-element.83.all_ref, bf16[1584,768]{1,0:T(8,128)(2,1)} %get-tuple-element.81.table_ref, bf16[768,1664]{1,0:T(8,128)(2,1)} %get-tuple-element.84.turned_ref, s32[16,256]{1,0:T(8,128)} %get-tuple-element.82.target_ref, ...), custom_call_target="tpu_custom_call" | custom-call | tf_op jit(solution)/shard_map/head_backward/pallas_call | solution.py:665
  399.8 1.1 multiply_reduce_fusion.1
  400.9 1.2 fusion.21
  402.1 0.8 multiply_convert_fusion.1.own_ref
  402.9 37.8 %gather_all.3 = bf16[32,128,768]{2,1,0:T(8,128)(2,1)} custom-call(bf16[128,768]{1,0:T(8,128)(2,1)} %multiply_convert_fusion.1.own_ref), custom_call_target="tpu_custom_call" | custom-call | tf_op jit(solution)/shard_map/gather_all/pallas_call | solution.py:148
  440.8 3.9 convolution_convert_fusion.4
  445.0 1.6 copy-done.17
  446.6 3.4 fusion.6
  450.1 1.5 convolution_bitcast_fusion.1
  451.6 1.7 convolution_bitcast_fusion
  453.8 3.0 multiply_reduce_fusion
  456.8 0.6 broadcast_in_dim.147
  457.6 0.7 fusion.50
  458.3 0.6 concatenate.29
  458.9 0.7 concatenate.30.scalar_ref
  460.1 3.9 convolution_convert_fusion.2
  464.4 4.5 convolution_convert_fusion
  469.0 44.4 %scatter_all.3 = f32[128,768]{1,0:T(8,128)} custom-call(bf16[2,2,4,2,128,768]{5,4,3,2,1,0:T(8,128)(2,1)} %bitcast.111), custom_call_target="tpu_custom_call" | custom-call | tf_op jit(solution)/shard_map/scatter_all/pallas_call | solution.py:341
  513.4 1.5 multiply_reduce_fusion.2
  515.4 1.2 fusion.23.side_ref
  516.7 0.9 subtract_add_fusion.grad_ref
  517.6 58.4 %mixer_backward.1 = (bf16[128,768]{1,0:T(8,128)(2,1)}, bf16[4,8,160,768]{3,2,1,0:T(8,128)(2,1)}) custom-call(f32[128,768]{1,0:T(8,128)} %subtract_add_fusion.grad_ref, f32[768,128]{1,0:T(8,128)} %fusion.23.side_ref, f32[128,768]{1,0:T(8,128)} %get-tuple-element.75.x_ref, bf16[4,8,160,768]{3,2,1,0:T(8,128)(2,1)} %bitcast.110, ...), custom_call_target="tpu_custom_call" | custom-call | tf_op jit(solution)/shard_map/mixer_backward/pallas_call | solution.py:1912
  576.0 93.2 %finish_all.1 = (f32[1584,768]{1,0:T(8,128)}, bf16[4,160,768]{2,1,0:T(8,128)(2,1)}, f32[8,128]{1,0:T(8,128)}) custom-call(bf16[128,768]{1,0:T(8,128)(2,1)} %get-tuple-element.98.own_ref, bf16[2,2,4,2,160,768]{5,4,3,2,1,0:T(8,128)(2,1)} %bitcast.119, s32[16,256]{1,0:T(8,128)} %get-tuple-element.100.token_ref, f32[1584,768]{1,0:T(8,128)} %get-tuple-element.101.head_ref, ...), custom_call_target="tpu_custom_call" | custom-call | tf_op jit(solution)/shard_map/finish_all/pallas_call | solution.py:1458
  669.1 1.3 fusion.54
  671.2 23.9 %multiply_add_fusion = (f32[2,4,384,768]{3,2,1,0:T(8,128)}, f32[2,4,384,768]{3,2,1,0:T(8,128)}, f32[2,4,384,768]{3,2,1,0:T(8,128)}) fusion(f32[2,4,384,768]{3,2,1,0:T(8,128)} %param.55, f32[2,4,384,768]{3,2,1,0:T(8,128)} %param.53, f32[1,4,384,768]{3,2,1,0:T(8,128)} %copy-done.3, f32[1,4,384,768]{3,2,1,0:T(8,128)} %copy-done, f32[]{:T(128)S(6)} %min.3, ...), kind=kLoop, calls=%fused_computation.1 | loop fusion | flops 25952256 | bytes 66060292 | tf_op jit(solution)/shard_map/add | solution.py:2293
  695.1 0.7 copy.195.refs_15_
  695.8 0.7 copy.196.refs_16_
  696.6 0.7 copy.197.refs_17_
  697.3 5.8 update_all.1
  703.1 1.5 copy.198
  704.6 1.5 copy.199
  706.1 1.5 copy.200
  707.5 12.7 %multiply_add_fusion.2 = (f32[1572,768]{1,0:T(8,128)}, f32[1572,768]{1,0:T(8,128)}, f32[1572,768]{1,0:T(8,128)}) fusion(f32[1572,768]{1,0:T(8,128)} %param.34, f32[1572,768]{1,0:T(8,128)} %master_ref.1, f32[1584,768]{1,0:T(8,128)} %get-tuple-element.103, f32[]{:T(128)S(6)} %min.3, f32[1572,768]{1,0:T(8,128)} %param.33), kind=kLoop, calls=%fused_computation.5 | loop fusion | flops 12072960 | bytes 33804292 | tf_op jit(solution)/shard_map/add | solution.py:2293
  (150 shorter events, 8.2 us)
Async XLA Ops:
  95.1 4.1 copy-start.10
  144.9 44.2 %slice-start = ((s8[9437184]{0:T(1024)(128)(4,1)}), s8[1048576]{0:T(1024)(128)(4,1)S(1)}, s32[]{:S(2)}) async-start(s8[9437184]{0:T(1024)(128)(4,1)} %bitcast.106), calls=%async_computation | async-start | bytes 2097152
  184.9 4.3 slice-start.1
  184.9 5.4 slice-start.2
  189.1 3.8 copy-start.1
  193.0 3.6 copy-start.4
  196.6 1.9 copy-start.16
  203.4 46.5 %copy-start.9 = (f32[128,128]{1,0:T(8,128)S(1)}, f32[128,128]{1,0:T(8,128)}, u32[]{:S(2)}) copy-start(f32[128,128]{1,0:T(8,128)} %get-tuple-element.78) | copy-start | bytes 196612
  203.4 46.5 %copy-start.13 = (s32[1,128,1]{1,2,0:T(1,128)S(1)}, s32[1,128,1]{1,2,0:T(1,128)}, u32[]{:S(2)}) copy-start(s32[1,128,1]{1,2,0:T(1,128)} %param.31) | copy-start | bytes 1540
  203.4 46.7 %copy-start.6 = (f32[128,768]{1,0:T(8,128)S(1)}, f32[128,768]{1,0:T(8,128)}, u32[]{:S(2)}) copy-start(f32[128,768]{1,0:T(8,128)} %get-tuple-element.77) | copy-start | bytes 1179652
  203.4 48.6 %copy-start.11 = (f32[3,768]{1,0:T(4,128)S(1)}, f32[3,768]{1,0:T(4,128)}, u32[]{:S(2)}) copy-start(f32[3,768]{1,0:T(4,128)} %convert_bitcast_fusion.gain_ref) | copy-start | bytes 27652
  327.6 73.3 %copy-start.5 = (f32[128,768]{1,0:T(8,128)S(1)}, f32[128,768]{1,0:T(8,128)}, u32[]{:S(2)}) copy-start(f32[128,768]{1,0:T(8,128)} %scatter_all.2) | copy-start | bytes 1179652
  402.9 42.0 %slice-start.3 = ((s8[4718592]{0:T(1024)(128)(4,1)}), s8[524288]{0:T(1024)(128)(4,1)S(1)}, s32[]{:S(2)}) async-start(s8[4718592]{0:T(1024)(128)(4,1)} %bitcast.124), calls=%async_computation.3 | async-start | bytes 1048576
  440.7 4.2 slice-start.4
  444.7 1.9 copy-start.17
  446.6 3.5 copy-start.2
  450.0 1.5 copy-start.7
  451.6 2.2 copy-start
  453.8 3.0 copy-start.3
  453.8 5.9 copy-start.8
  671.1 24.0 %copy-start.12 = (f32[96,16]{0,1:T(8,128)S(1)}, f32[96,16]{0,1:T(8,128)}, u32[]{:S(2)}) copy-start(f32[96,16]{0,1:T(8,128)} %param.50) | copy-start | bytes 18436
  671.2 24.7 %copy-start.14 = (f32[96,16]{0,1:T(8,128)S(1)}, f32[96,16]{0,1:T(8,128)}, u32[]{:S(2)}) copy-start(f32[96,16]{0,1:T(8,128)} %param.51) | copy-start | bytes 18436
  671.2 25.4 %copy-start.15 = (f32[96,16]{0,1:T(8,128)S(1)}, f32[96,16]{0,1:T(8,128)}, u32[]{:S(2)}) copy-start(f32[96,16]{0,1:T(8,128)} %param.52) | copy-start | bytes 18436

commit v2 on v1

--- a/solution.py
+++ b/solution.py
@@ -1984,8 +1984,8 @@
     renew(3, everything, turned_ref[...].T[0 : CONV + 3 + STATE, 0:width], CHANNEL_LRATE)
     gains = side_ref[...].T[:, 0:tall]
     renew(4, everything, jnp.concatenate([gains[-1:], gains[-3:-1]], axis=0), LRATE)
-    router_lanes = slice(SIDE_LANE, SIDE_LANE + inputs[15].shape[1])
-    renew(5, everything, side_ref[0:tall, router_lanes], LRATE)
+    router_lanes = slice(SIDE_LANE, SIDE_LANE + inputs[15].shape[0])
+    renew(5, everything, side_ref[...].T[router_lanes, 0:tall], LRATE)
 
 
 def update_all(quarters, sums, states):
@@ -2005,6 +2005,207 @@
         compiler_params=pltpu.CompilerParams(vmem_limit_bytes=VMEM_LIMIT),
         name="update_all",
     )(quarters, sums, *flat)
+
+
+def pick_slots(slot_ref, block, slots):
+    numbers = lax.broadcasted_iota(jnp.int32, (slots, slot_ref.shape[1]), 0)
+    return (numbers == slot_ref[pl.ds(block, 1)]).astype(jnp.float32).astype(jnp.bfloat16)
+
+
+def natural_place(block, sizes):
+    return unravel(block, tuple(sizes[a] for a in NATURAL))
+
+
+def rows_to_slots(sizes, capacity, slot_ref, all_ref, slots_ref):
+    experts_here = slots_ref.shape[0]
+
+    def one(block, carry):
+        select = pick_slots(slot_ref, block, experts_here * capacity)
+        picked = matmul(select, all_ref[block]).astype(jnp.bfloat16)
+        first = pl.multiple_of(block * capacity, capacity)
+        for expert in range(experts_here):
+            slots_ref[expert, pl.ds(first, capacity)] = picked[
+                expert * capacity : (expert + 1) * capacity
+            ]
+        return carry
+
+    lax.fori_loop(0, slot_ref.shape[0], one, 0, unroll=8)
+
+
+def slots_to_rows(sizes, capacity, slot_ref, slots_ref, full_ref):
+    experts_here = slots_ref.shape[0]
+
+    def one(block, carry):
+        select = pick_slots(slot_ref, block, experts_here * capacity)
+        first = pl.multiple_of(block * capacity, capacity)
+        held = jnp.concatenate(
+            [slots_ref[expert, pl.ds(first, capacity)] for expert in range(experts_here)], axis=0
+        )
+        full_ref[natural_place(block, sizes)] = matmul_tn(select, held).astype(jnp.bfloat16)
+        return carry
+
+    lax.fori_loop(0, slot_ref.shape[0], one, 0, unroll=8)
+
+
+def flat_gather_semaphores(devices, rows):
+    copies = (devices - 1) * len(split_rows(rows, GATHER_ORDERS))
+    return [pltpu.SemaphoreType.DMA((copies,)), pltpu.SemaphoreType.DMA((copies,))]
+
+
+def moe_forward_kernel(
+    sizes,
+    pairs,
+    capacity,
+    own_ref,
+    slot_ref,
+    weights_ref,
+    result_ref,
+    arrived_ref,
+    before_ref,
+    all_ref,
+    part_ref,
+    full_ref,
+    local_sem,
+    *scratch,
+):
+    pieces = split_rows(own_ref.shape[0], GATHER_ORDERS)
+    gather_kernel(sizes, pieces, own_ref, all_ref, local_sem, scratch[0], scratch[1])
+    scatter = Scatter(sizes, pairs, full_ref, result_ref, scratch[2:], False)
+    rows_to_slots(sizes, capacity, slot_ref, all_ref, arrived_ref)
+
+    def expert(number, carry):
+        before = matmul_nt(arrived_ref[number], weights_ref[0, number])
+        before_ref[number] = before
+        inner = jax.nn.gelu(before).astype(jnp.bfloat16)
+        part_ref[number] = matmul(inner, weights_ref[1, number]).astype(jnp.bfloat16)
+        return carry
+
+    lax.fori_loop(0, weights_ref.shape[1], expert, 0)
+    slots_to_rows(sizes, capacity, slot_ref, part_ref, full_ref)
+    for pair in range(pairs):
+        scatter.launch(pair, 0)
+    wave(pairs, 4, scatter.advance)
+    scatter.finish()
+
+
+def moe_forward(rows, slots, weights, capacity, collective_id):
+    sizes = axis_sizes()
+    natural = tuple(sizes[a] for a in NATURAL)
+    pairs = rows.shape[0] // SPAN
+    _, experts_here, hidden, _ = weights.shape
+    held = (experts_here, slots.shape[0] * capacity)
+    vmem = pl.BlockSpec(memory_space=pltpu.VMEM)
+    return pl.pallas_call(
+        functools.partial(moe_forward_kernel, sizes, pairs, capacity),
+        out_shape=(
+            jax.ShapeDtypeStruct(rows.shape, jnp.float32),
+            jax.ShapeDtypeStruct(held + (D,), jnp.bfloat16),
+            jax.ShapeDtypeStruct(held + (hidden,), jnp.float32),
+        ),
+        in_specs=[vmem] * 3,
+        out_specs=(vmem,) * 3,
+        scratch_shapes=[
+            pltpu.VMEM((slots.shape[0],) + rows.shape, jnp.bfloat16),
+            pltpu.VMEM(held + (D,), jnp.bfloat16),
+            pltpu.VMEM(natural + rows.shape, jnp.bfloat16),
+            pltpu.SemaphoreType.DMA,
+        ]
+        + flat_gather_semaphores(slots.shape[0], rows.shape[0])
+        + scatter_scratch(sizes, pairs, D, False),
+        compiler_params=pltpu.CompilerParams(
+            collective_id=collective_id, has_side_effects=True, vmem_limit_bytes=VMEM_LIMIT
+        ),
+        name="moe_forward",
+    )(rows, slots, weights)
+
+
+def moe_backward_kernel(
+    sizes,
+    pairs,
+    capacity,
+    own_ref,
+    slot_ref,
+    weights_ref,
+    arrived_ref,
+    before_ref,
+    result_ref,
+    grads_ref,
+    square_ref,
+    all_ref,
+    part_ref,
+    full_ref,
+    slots_ref,
+    local_sem,
+    *scratch,
+):
+    pieces = split_rows(own_ref.shape[0], GATHER_ORDERS)
+    gather_kernel(sizes, pieces, own_ref, all_ref, local_sem, scratch[0], scratch[1])
+    scatter = Scatter(sizes, pairs, full_ref, result_ref, scratch[2:], False)
+    rows_to_slots(sizes, capacity, slot_ref, all_ref, slots_ref)
+
+    def slope(number):
+        grad_inner = matmul_nt(slots_ref[number], weights_ref[1, number])
+        return jax.vjp(jax.nn.gelu, before_ref[number])[1](grad_inner)[0].astype(jnp.bfloat16)
+
+    def back(number, carry):
+        part_ref[number] = matmul(slope(number), weights_ref[0, number]).astype(jnp.bfloat16)
+        return carry
+
+    experts_here = weights_ref.shape[1]
+    lax.fori_loop(0, experts_here, back, 0)
+    slots_to_rows(sizes, capacity, slot_ref, part_ref, full_ref)
+    for pair in range(pairs):
+        scatter.launch(pair, 0)
+
+    def weight_grads(number, total):
+        grad_up = matmul_tn(slope(number), arrived_ref[number])
+        inner = jax.nn.gelu(before_ref[number]).astype(jnp.bfloat16)
+        grad_down = matmul_tn(inner, slots_ref[number])
+        grads_ref[0, number] = grad_up
+        grads_ref[1, number] = grad_down
+        return total + jnp.sum(grad_up * grad_up) + jnp.sum(grad_down * grad_down)
+
+    total = jnp.float32(0.0)
+    turns = pairs + 3
+    for turn in range(turns):
+        for phase in range(3, -1, -1):
+            if 0 <= turn - phase < pairs:
+                scatter.advance(turn - phase, phase)
+        first, last = (experts_here * turn // (turns - 1), experts_here * (turn + 1) // (turns - 1))
+        if last > first and first < experts_here:
+            total = lax.fori_loop(first, min(last, experts_here), weight_grads, total)
+    square_ref[...] = jnp.full(square_ref.shape, total, jnp.float32)
+    scatter.finish()
+
+
+def moe_backward(rows, slots, weights, arrived, before, capacity, collective_id):
+    sizes = axis_sizes()
+    natural = tuple(sizes[a] for a in NATURAL)
+    pairs = rows.shape[0] // SPAN
+    vmem = pl.BlockSpec(memory_space=pltpu.VMEM)
+    return pl.pallas_call(
+        functools.partial(moe_backward_kernel, sizes, pairs, capacity),
+        out_shape=(
+            jax.ShapeDtypeStruct(rows.shape, jnp.float32),
+            jax.ShapeDtypeStruct(weights.shape, jnp.float32),
+            jax.ShapeDtypeStruct((8, LANES), jnp.float32),
+        ),
+        in_specs=[vmem] * 5,
+        out_specs=(vmem,) * 3,
+        scratch_shapes=[
+            pltpu.VMEM((slots.shape[0],) + rows.shape, jnp.bfloat16),
+            pltpu.VMEM(arrived.shape, jnp.bfloat16),
+            pltpu.VMEM(natural + rows.shape, jnp.bfloat16),
+            pltpu.VMEM(arrived.shape, jnp.bfloat16),
+            pltpu.SemaphoreType.DMA,
+        ]
+        + flat_gather_semaphores(slots.shape[0], rows.shape[0])
+        + scatter_scratch(sizes, pairs, D, False),
+        compiler_params=pltpu.CompilerParams(
+            collective_id=collective_id, has_side_effects=True, vmem_limit_bytes=VMEM_LIMIT
+        ),
+        name="moe_backward",
+    )(rows, slots, weights, arrived, before)
 
 
 def from_behind(value, axis, by):
@@ -2227,7 +2428,7 @@
     )
 
 
-def dispatch_table(routes, first_expert, experts_here, capacity):
+def dispatch_slots(routes, first_expert, experts_here, capacity):
     tokens = routes.shape[1]
     chosen = (
         routes[:, :, None] == first_expert + jnp.arange(experts_here, dtype=jnp.int32)
@@ -2235,7 +2436,10 @@
     earlier = jnp.cumsum(chosen, axis=1) - chosen
     rank = jnp.sum(earlier * chosen, axis=2).astype(jnp.int32)
     local = routes - first_expert
-    slot = jnp.where((local >= 0) & (local < experts_here), local * capacity + rank, -1)
+    return jnp.where((local >= 0) & (local < experts_here), local * capacity + rank, -1)
+
+
+def dispatch_table(slot, experts_here, capacity):
     return (
         slot[:, None, :] == jnp.arange(experts_here * capacity, dtype=jnp.int32)[None, :, None]
     ).astype(jnp.bfloat16)
@@ -2412,15 +2616,21 @@
         scale_mid = inverse_rms(mixed_out)
         moe_in = (mixed_out * scale_mid * gain_vals[1]).astype(jnp.bfloat16)
         probability = jax.nn.softmax(matmul(moe_in, router_low), axis=-1)
-    select = dispatch_table(routes_all, seq_index * local_experts, local_experts, capacity)
+    slots = dispatch_slots(routes_all, seq_index * local_experts, local_experts, capacity)
     gate_value = jnp.sum(probability * chosen, axis=1)
-    arrived = to_slots(select, gather_all(moe_in, 6), local_experts, capacity)
-    before = jnp.einsum("erd,efd->erf", arrived, up_weight, preferred_element_type=jnp.float32)
-    inner_act = jax.nn.gelu(before).astype(jnp.bfloat16)
-    partial_out = jnp.einsum(
-        "erf,efd->erd", inner_act, down_weight, preferred_element_type=jnp.float32
-    )
-    returned = scatter_all(to_rows(select, partial_out, capacity), 3)
+    if compact:
+        returned, arrived, before = moe_forward(
+            moe_in, slots, experts_low, capacity, 11
+        )
+    else:
+        select = dispatch_table(slots, local_experts, capacity)
+        arrived = to_slots(select, gather_all(moe_in, 6), local_experts, capacity)
+        before = jnp.einsum("erd,efd->erf", arrived, up_weight, preferred_element_type=jnp.float32)
+        inner_act = jax.nn.gelu(before).astype(jnp.bfloat16)
+        partial_out = jnp.einsum(
+            "erf,efd->erd", inner_act, down_weight, preferred_element_type=jnp.float32
+        )
+        returned = scatter_all(to_rows(select, partial_out, capacity), 3)
     expert_value = returned.astype(jnp.bfloat16).astype(jnp.float32)
     branch = gate_value[:, None] * expert_value
     hidden = mixed_out + branch
@@ -2467,19 +2677,27 @@
     grad_hidden, grad_gain_out = norm_back(hidden, scale_out, gain_vals[2], grad_final)
     grad_gate = jnp.sum(grad_hidden * expert_value, axis=1)
     grad_expert = (gate_value[:, None] * grad_hidden).astype(jnp.bfloat16)
-    grad_arrived = to_slots(select, gather_all(grad_expert, 6), local_experts, capacity)
-    grad_inner = jnp.einsum(
-        "erd,efd->erf", grad_arrived, down_weight, preferred_element_type=jnp.float32
-    )
-    grad_before = jax.vjp(jax.nn.gelu, before)[1](grad_inner)[0].astype(jnp.bfloat16)
-    grad_down = jnp.einsum(
-        "erf,erd->efd", inner_act, grad_arrived, preferred_element_type=jnp.float32
-    )
-    grad_up = jnp.einsum("erf,erd->efd", grad_before, arrived, preferred_element_type=jnp.float32)
-    grad_part = jnp.einsum(
-        "erf,efd->erd", grad_before, up_weight, preferred_element_type=jnp.float32
-    )
-    grad_moe_in = scatter_all(to_rows(select, grad_part, capacity), 3)
+    if compact:
+        grad_moe_in, grad_experts, square_tile = moe_backward(
+            grad_expert, slots, experts_low, arrived, before, capacity, 12
+        )
+        experts_square = square_tile[0, 0]
+    else:
+        grad_arrived = to_slots(select, gather_all(grad_expert, 6), local_experts, capacity)
+        grad_inner = jnp.einsum(
+            "erd,efd->erf", grad_arrived, down_weight, preferred_element_type=jnp.float32
+        )
+        grad_before = jax.vjp(jax.nn.gelu, before)[1](grad_inner)[0].astype(jnp.bfloat16)
+        grad_down = jnp.einsum(
+            "erf,erd->efd", inner_act, grad_arrived, preferred_element_type=jnp.float32
+        )
+        grad_up = jnp.einsum("erf,erd->efd", grad_before, arrived, preferred_element_type=jnp.float32)
+        grad_part = jnp.einsum(
+            "erf,efd->erd", grad_before, up_weight, preferred_element_type=jnp.float32
+        )
+        grad_moe_in = scatter_all(to_rows(select, grad_part, capacity), 3)
+        grad_experts = jnp.stack([grad_up, grad_down])
+        experts_square = jnp.sum(grad_experts * grad_experts)
     grad_moe_in = grad_moe_in.astype(jnp.bfloat16).astype(jnp.float32)
     grad_router_logits = (grad_gate * gate_value)[:, None] * (chosen - probability)
     grad_moe_in = grad_moe_in + jnp.dot(
@@ -2514,8 +2732,6 @@
         )
         grad_gains = jnp.stack([grad_gain_in, grad_gain_mid, grad_gain_out])
         mixer_wholes = (grad_win, grad_wx, grad_wout, grad_channel, grad_gains, grad_router)
-    grad_experts = jnp.stack([grad_up, grad_down])
-    experts_square = jnp.sum(grad_experts * grad_experts)
     if compact:
         scalars = jnp.concatenate(
             [jnp.full((4, LANES), experts_square), jnp.full((4, LANES), loss_part)], axis=0
@@ -2564,7 +2780,9 @@
         (router, router_mom, router_ema),
     )
     if compact:
-        fresh = update_all(quarters, sums, mixer_states)
+        turned_states = mixer_states[:5] + (tuple(part.T for part in mixer_states[5]),)
+        fresh = update_all(quarters, sums, turned_states)
+        fresh = list(fresh[:15]) + [part.T for part in fresh[15:]]
     else:
         rates = (LRATE, LRATE, LRATE, CHANNEL_LRATE, LRATE, LRATE)
         fresh = [

time: 731 us -> 709 us (0.970)
  matrix products: 34.9 us -> 1.96 us
  Pallas kernels: 597 us -> 618 us
  local copies, waits for them, and re-layouts: 26.2 us -> 16.4 us
    dot_general x10 -> x0, matrix products: 33 us -> none  [the longest x2 9.09 us: to_rows(): jnp.einsum('bst,bsd->btd', select, slots, preferred_element_type=jnp.floa...]
    pallas_call x4 -> x2, Pallas kernels: 166 us -> 188 us  [the longest x1 95.7 us: moe_backward(): pl.pallas_call(functools.partial(moe_backward_kernel, sizes, pairs, capac...]
    unnamed x56 -> x21, local copies, waits for them, and re-layouts: 10.4 us -> 0.45 us
where the time goes in v2:
time: 709 us; the launch traced here: 698 us
  Pallas kernels  618 us (87%)
  other arithmetic  58.7 us (8%)
  local copies, waits for them, and re-layouts  16.4 us (2%)
    pallas_call x1, Pallas kernels, moe_backward(): pl.pallas_call(functools.partial(moe_backward_kernel, sizes, pairs, capac...  95.7 us
    pallas_call x1, Pallas kernels, finish_all(): pl.pallas_call(functools.partial(finish_kernel, sizes, pairs, pack_pairs)...  93.5 us
    pallas_call x1, Pallas kernels, moe_forward(): pl.pallas_call(functools.partial(moe_forward_kernel, sizes, pairs, capaci...  92.3 us
    pallas_call x1, Pallas kernels, start_all(): pl.pallas_call(functools.partial(start_kernel, sizes, pairs, pack_pairs,...  87.4 us
    pallas_call x1, Pallas kernels, head_backward(): pl.pallas_call(functools.partial(head_backward_kernel, sizes, pairs, own_...  72.1 us
    pallas_call x1, Pallas kernels, head_forward(): pl.pallas_call(functools.partial(head_forward_kernel, sizes, pairs, own_v...  70.5 us
    pallas_call x1, Pallas kernels, mixer_backward_all(): pl.pallas_call(mixer_backward_kernel, out_shape=(jax.ShapeDtypeStruct((to...  56.2 us
    pallas_call x1, Pallas kernels, mixer_forward_all(): pl.pallas_call(functools.partial(mixer_forward_kernel, router.shape[1]),...  44.5 us

profile of v2, /device:TPU:0, one launch (start us, length us, event | category | flops | bytes accessed | tf_op | source)
XLA Modules:
  0.0 698.4 jit_solution(2711174353923162412)
XLA Ops:
  0.7 0.7 convert_bitcast_fusion.1
  1.4 0.7 convert_element_type.194
  2.2 0.8 fusion.20
  3.1 0.8 dynamic-slice_convert_fusion.2
  3.8 0.9 dynamic-slice_convert_fusion.1
  4.8 1.0 dynamic-slice_convert_fusion
  5.7 0.7 maximum_maximum_fusion.pack_ref
  6.5 0.7 pad_add_fusion.1
  7.2 0.6 pad.31.number_ref
  7.8 87.4 %start_all.1 = (s32[2,2,4,2,16,128]{5,4,3,2,1,0:T(8,128)}, bf16[2,2,4,2,160,768]{5,4,3,2,1,0:T(8,128)(2,1)}, f32[128,768]{1,0:T(8,128)}, bf16[1584,768]{1,0:T(8,...) custom-call(s32[16,128]{1,0:T(8,128)} %pad.31.number_ref, ...), custom_call_target="tpu_custom_call" | custom-call | tf_op jit(solution)/shard_map/start_all/pallas_call | solution.py:1282
  95.2 1.1 copy.136
  96.3 0.1 copy.137
  96.4 1.7 fusion.3
  98.1 0.6 add_select_fusion.slot_ref
  98.8 1.0 slice.207
  99.8 0.1 reshape.452
  100.0 0.1 slice.210
  100.2 0.1 copy.148
  100.3 0.1 slice.211
  100.4 0.1 copy.149
  100.5 0.6 convert_bitcast_fusion.gain_ref
  101.2 0.1 slice.212
  101.3 0.7 pad.37.router_ref
  102.0 0.2 copy.147
  102.2 0.7 pad_convert_fusion.vec_ref
  102.9 0.2 reduce_window_sum.23
  103.1 0.1 convert_reduce_fusion.1
  103.3 0.1 convert_reduce_fusion
  103.6 0.7 copy.135.mask_ref
  104.3 44.5 %mixer_forward.1 = (f32[128,768]{1,0:T(8,128)}, bf16[128,768]{1,0:T(8,128)(2,1)}, f32[128,128]{1,0:T(8,128)}, f32[128,1536]{1,0:T(8,128)}, f32[136,1536]{1,0:T(8...) custom-call(f32[128,768]{1,0:T(8,128)} %get-tuple-element.81.x_ref, ...), custom_call_target="tpu_custom_call" | custom-call | tf_op jit(solution)/shard_map/mixer_forward/pallas_call | solution.py:1685
  148.8 6.4 convert_element_type.209.weights_ref
  155.2 92.3 %moe_forward.1 = (f32[128,768]{1,0:T(8,128)}, bf16[4,512,768]{2,1,0:T(8,128)(2,1)}, f32[4,512,384]{2,1,0:T(8,128)}) custom-call(bf16[128,768]{1,0:T(8,128)(2,1)} %get-tuple-element.85.own_ref, s32[32,128]{1,0:T(8,128)} %add_select_fusion.slot_ref, bf16[2,4,384,768]{3,2,1,0:T(8,128)(2,1)} %convert_element_type.209.weights_ref), custom_call_target="tpu_custom_call" | custom-call | tf_op jit(solution)/shard_map/moe_forward/pallas_call | solution.py:2098
  247.5 0.2 select_reduce_fusion
  247.7 1.9 multiply_reduce_fusion.5
  249.6 0.8 multiply_convert_fusion.1.own_ref
  250.4 70.5 %head_forward.1 = (bf16[2,2,4,2,128,768]{5,4,3,2,1,0:T(8,128)(2,1)}, f32[2,16,256]{2,1,0:T(8,128)}) custom-call(bf16[128,768]{1,0:T(8,128)(2,1)} %multiply_convert_fusion.1.own_ref, bf16[1584,768]{1,0:T(8,128)(2,1)} %get-tuple-element.88.table_ref, s32[16,256]{1,0:T(8,128)} %get-tuple-element.89.target_ref), custom_call_target="tpu_custom_call" | custom-call | tf_op jit(solution)/shard_map/head_forward/pallas_call | solution.py:532
  320.9 1.3 slice_subtract_fusion
  322.3 0.4 slice_reduce_fusion.16
  323.5 0.1 lt.225
  324.1 0.3 fusion.21
  325.3 0.7 select_add_fusion.weight_ref
  326.0 72.1 %head_backward.1 = (f32[128,768]{1,0:T(8,128)}, f32[1584,768]{1,0:T(8,128)}) custom-call(bf16[2,2,4,2,128,768]{5,4,3,2,1,0:T(8,128)(2,1)} %get-tuple-element.90.all_ref, bf16[1584,768]{1,0:T(8,128)(2,1)} %get-tuple-element.88.table_ref, bf16[768,1664]{1,0:T(8,128)(2,1)} %get-tuple-element.91.turned_ref, s32[16,256]{1,0:T(8,128)} %get-tuple-element.89.target_ref, ...), custom_call_target="tpu_custom_call" | custom-call | tf_op jit(solution)/shard_map/head_backward/pallas_call | solution.py:665
  398.1 1.1 multiply_reduce_fusion
  399.2 1.2 fusion.8
  400.5 0.8 multiply_convert_fusion.own_ref
  401.2 95.7 %moe_backward.1 = (f32[128,768]{1,0:T(8,128)}, f32[2,4,384,768]{3,2,1,0:T(8,128)}, f32[8,128]{1,0:T(8,128)}) custom-call(bf16[128,768]{1,0:T(8,128)(2,1)} %multiply_convert_fusion.own_ref, s32[32,128]{1,0:T(8,128)} %add_select_fusion.slot_ref, bf16[2,4,384,768]{3,2,1,0:T(8,128)(2,1)} %convert_element_type.209.weights_ref, ...), custom_call_target="tpu_custom_call" | custom-call | tf_op jit(solution)/shard_map/moe_backward/pallas_call | solution.py:2186
  497.0 1.2 slice.200
  498.2 0.6 broadcast_in_dim.145
  499.0 0.7 fusion.35
  499.7 0.6 concatenate.29
  500.3 0.7 concatenate.30.scalar_ref
  501.0 0.4 fusion.12
  501.5 1.5 multiply_reduce_fusion.1
  503.0 0.2 stack.21
  503.2 0.2 broadcast_multiply_fusion
  503.3 0.2 stack.22
  503.5 1.2 fusion.10.side_ref
  504.7 0.9 subtract_add_fusion.grad_ref
  505.6 56.2 %mixer_backward.1 = (bf16[128,768]{1,0:T(8,128)(2,1)}, bf16[4,8,160,768]{3,2,1,0:T(8,128)(2,1)}) custom-call(f32[128,768]{1,0:T(8,128)} %subtract_add_fusion.grad_ref, f32[768,128]{1,0:T(8,128)} %fusion.10.side_ref, f32[128,768]{1,0:T(8,128)} %get-tuple-element.81.x_ref, bf16[4,8,160,768]{3,2,1,0:T(8,128)(2,1)} %bitcast.68, ...), custom_call_target="tpu_custom_call" | custom-call | tf_op jit(solution)/shard_map/mixer_backward/pallas_call | solution.py:1912
  561.8 93.5 %finish_all.1 = (f32[1584,768]{1,0:T(8,128)}, bf16[4,160,768]{2,1,0:T(8,128)(2,1)}, f32[8,128]{1,0:T(8,128)}) custom-call(bf16[128,768]{1,0:T(8,128)(2,1)} %get-tuple-element.108.own_ref, bf16[2,2,4,2,160,768]{5,4,3,2,1,0:T(8,128)(2,1)} %bitcast.71, s32[16,256]{1,0:T(8,128)} %get-tuple-element.110.token_ref, f32[1584,768]{1,0:T(8,128)} %get-tuple-element.111.head_ref, ...), custom_call_target="tpu_custom_call" | custom-call | tf_op jit(solution)/shard_map/finish_all/pallas_call | solution.py:1458
  655.3 1.3 fusion.39
  657.3 24.0 %multiply_add_fusion = (f32[2,4,384,768]{3,2,1,0:T(8,128)}, f32[2,4,384,768]{3,2,1,0:T(8,128)}, f32[2,4,384,768]{3,2,1,0:T(8,128)}) fusion(f32[2,4,384,768]{3,2,1,0:T(8,128)} %param.55, f32[2,4,384,768]{3,2,1,0:T(8,128)} %param.53, f32[2,4,384,768]{3,2,1,0:T(8,128)} %get-tuple-element.134, f32[]{:T(128)S(6)} %min.3, f32[2,4,384,768]{3,2,1,0:T(8,128)} %param.54), kind=kLoop, calls=%fused_computation | loop fusion | flops 23592960 | bytes 66060292 | tf_op jit(solution)/shard_map/add | solution.py:2497
  681.3 5.8 update_all.1
  687.2 9.7 %multiply_add_fusion.2 = (f32[1572,768]{1,0:T(8,128)}, f32[1572,768]{1,0:T(8,128)}, f32[1572,768]{1,0:T(8,128)}) fusion(f32[1572,768]{1,0:T(8,128)} %param.34, f32[1572,768]{1,0:T(8,128)S(1)} %bitcast.70, f32[1584,768]{1,0:T(8,128)} %get-tuple-element.114, f32[]{:T(128)S(6)} %min.3, f32[1572,768]{1,0:T(8,128)} %param.33), kind=kLoop, calls=%fused_computation.3 | loop fusion | flops 12072960 | bytes 33804292 | tf_op jit(solution)/shard_map/add | solution.py:2497
  (100 shorter events, 3.0 us)
Async XLA Ops:
  7.8 95.1 %copy-start.4 = (s32[4,8]{1,0:T(4,128)S(1)}, s32[4,8]{1,0:T(4,128)}, u32[]{:S(2)}) copy-start(s32[4,8]{1,0:T(4,128)} %param.30) | copy-start | bytes 388
  155.2 92.3 %copy-start.3 = (f32[128,128]{1,0:T(8,128)S(1)}, f32[128,128]{1,0:T(8,128)}, u32[]{:S(2)}) copy-start(f32[128,128]{1,0:T(8,128)} %get-tuple-element.84) | copy-start | bytes 196612
  155.2 92.3 %copy-start.6 = (s32[1,128,1]{1,2,0:T(1,128)S(1)}, s32[1,128,1]{1,2,0:T(1,128)}, u32[]{:S(2)}) copy-start(s32[1,128,1]{1,2,0:T(1,128)} %param.31) | copy-start | bytes 1540
  155.2 92.5 %copy-start = (f32[128,768]{1,0:T(8,128)S(1)}, f32[128,768]{1,0:T(8,128)}, u32[]{:S(2)}) copy-start(f32[128,768]{1,0:T(8,128)} %get-tuple-element.83) | copy-start | bytes 1179652
  155.2 94.4 %copy-start.5 = (f32[3,768]{1,0:T(4,128)S(1)}, f32[3,768]{1,0:T(4,128)}, u32[]{:S(2)}) copy-start(f32[3,768]{1,0:T(4,128)} %convert_bitcast_fusion.gain_ref) | copy-start | bytes 27652
  326.0 73.2 %copy-start.1 = (f32[128,768]{1,0:T(8,128)S(1)}, f32[128,768]{1,0:T(8,128)}, u32[]{:S(2)}) copy-start(f32[128,768]{1,0:T(8,128)} %get-tuple-element.87) | copy-start | bytes 1179652
  401.2 99.8 %copy-start.2 = (bf16[128,768]{1,0:T(8,128)(2,1)S(1)}, bf16[128,768]{1,0:T(8,128)(2,1)}, u32[]{:S(2)}) copy-start(bf16[128,768]{1,0:T(8,128)(2,1)} %get-tuple-element.85.own_ref) | copy-start | bytes 589828
  657.3 29.9 %slice-start = ((s8[4841472]{0:T(1024)(128)(4,1)}), s8[4194304]{0:T(1024)(128)(4,1)S(1)}, s32[]{:S(2)}) async-start(s8[4841472]{0:T(1024)(128)(4,1)} %bitcast.69), calls=%async_computation | async-start | bytes 8388608
  657.3 29.8 %slice-start.1 = ((s8[4841472]{0:T(1024)(128)(4,1)}), s8[647168]{0:T(1024)(128)(4,1)S(1)}, s32[]{:S(2)}) async-start(s8[4841472]{0:T(1024)(128)(4,1)} %bitcast.69), calls=%async_computation.1 | async-start | bytes 1294336

commit v3 on v2

--- a/solution.py
+++ b/solution.py
@@ -887,7 +887,7 @@
 
 
 def spans(width):
-    size = 512 if width % 512 == 0 else width
+    size = 768 if width % 768 == 0 else width
     return [slice(first, first + size) for first in range(0, width, size)]
 
 
@@ -2058,22 +2058,30 @@
     capacity,
     own_ref,
     slot_ref,
-    weights_ref,
+    master_ref,
     result_ref,
     arrived_ref,
     before_ref,
+    weights_ref,
+    wide_ref,
+    wide_sem,
     all_ref,
     part_ref,
     full_ref,
     local_sem,
     *scratch,
 ):
+    fetch = pltpu.make_async_copy(master_ref, wide_ref, wide_sem)
+    fetch.start()
     pieces = split_rows(own_ref.shape[0], GATHER_ORDERS)
     gather_kernel(sizes, pieces, own_ref, all_ref, local_sem, scratch[0], scratch[1])
     scatter = Scatter(sizes, pairs, full_ref, result_ref, scratch[2:], False)
+    fetch.wait()
     rows_to_slots(sizes, capacity, slot_ref, all_ref, arrived_ref)
 
     def expert(number, carry):
+        for side in range(2):
+            weights_ref[side, number] = wide_ref[side, number].astype(jnp.bfloat16)
         before = matmul_nt(arrived_ref[number], weights_ref[0, number])
         before_ref[number] = before
         inner = jax.nn.gelu(before).astype(jnp.bfloat16)
@@ -2101,10 +2109,13 @@
             jax.ShapeDtypeStruct(rows.shape, jnp.float32),
             jax.ShapeDtypeStruct(held + (D,), jnp.bfloat16),
             jax.ShapeDtypeStruct(held + (hidden,), jnp.float32),
+            jax.ShapeDtypeStruct(weights.shape, jnp.bfloat16),
         ),
-        in_specs=[vmem] * 3,
-        out_specs=(vmem,) * 3,
+        in_specs=[vmem, vmem, pl.BlockSpec(memory_space=pl.ANY)],
+        out_specs=(vmem,) * 4,
         scratch_shapes=[
+            pltpu.VMEM(weights.shape, jnp.float32),
+            pltpu.SemaphoreType.DMA,
             pltpu.VMEM((slots.shape[0],) + rows.shape, jnp.bfloat16),
             pltpu.VMEM(held + (D,), jnp.bfloat16),
             pltpu.VMEM(natural + rows.shape, jnp.bfloat16),
@@ -2433,7 +2444,9 @@
     chosen = (
         routes[:, :, None] == first_expert + jnp.arange(experts_here, dtype=jnp.int32)
     ).astype(jnp.float32)
-    earlier = jnp.cumsum(chosen, axis=1) - chosen
+    order = jnp.arange(tokens, dtype=jnp.int32)
+    ahead = (order[None, :] < order[:, None]).astype(jnp.float32)
+    earlier = jnp.einsum("ij,bje->bie", ahead, chosen, preferred_element_type=jnp.float32)
     rank = jnp.sum(earlier * chosen, axis=2).astype(jnp.int32)
     local = routes - first_expert
     return jnp.where((local >= 0) & (local < experts_here), local * capacity + rank, -1)
@@ -2619,8 +2632,8 @@
     slots = dispatch_slots(routes_all, seq_index * local_experts, local_experts, capacity)
     gate_value = jnp.sum(probability * chosen, axis=1)
     if compact:
-        returned, arrived, before = moe_forward(
-            moe_in, slots, experts_low, capacity, 11
+        returned, arrived, before, experts_low = moe_forward(
+            moe_in, slots, experts, capacity, 11
         )
     else:
         select = dispatch_table(slots, local_experts, capacity)

time: 709 us -> 700 us (0.987)
  other arithmetic: 58.7 us -> 50.6 us
where the time goes in v3:
time: 700 us; the launch traced here: 689 us
  Pallas kernels  617 us (88%)
  other arithmetic  50.6 us (7%)
  local copies, waits for them, and re-layouts  16.3 us (2%)
    pallas_call x1, Pallas kernels, moe_backward(): pl.pallas_call(functools.partial(moe_backward_kernel, sizes, pairs, capac...  95.5 us
    pallas_call x1, Pallas kernels, finish_all(): pl.pallas_call(functools.partial(finish_kernel, sizes, pairs, pack_pairs)...  93.1 us
    pallas_call x1, Pallas kernels, moe_forward(): pl.pallas_call(functools.partial(moe_forward_kernel, sizes, pairs, capaci...  92.3 us
    pallas_call x1, Pallas kernels, start_all(): pl.pallas_call(functools.partial(start_kernel, sizes, pairs, pack_pairs,...  87.3 us
    pallas_call x1, Pallas kernels, head_backward(): pl.pallas_call(functools.partial(head_backward_kernel, sizes, pairs, own_...  71.7 us
    pallas_call x1, Pallas kernels, head_forward(): pl.pallas_call(functools.partial(head_forward_kernel, sizes, pairs, own_v...  70.4 us
    pallas_call x1, Pallas kernels, mixer_backward_all(): pl.pallas_call(mixer_backward_kernel, out_shape=(jax.ShapeDtypeStruct((to...  56.9 us
    pallas_call x1, Pallas kernels, mixer_forward_all(): pl.pallas_call(functools.partial(mixer_forward_kernel, router.shape[1]),...  43.8 us

profile of v3, /device:TPU:0, one launch (start us, length us, event | category | flops | bytes accessed | tf_op | source)
XLA Modules:
  0.0 689.3 jit_solution(10730180019151564416)
XLA Ops:
  0.7 0.7 convert_bitcast_fusion.1
  1.4 0.7 convert_element_type.190
  2.2 0.8 fusion.21
  3.1 0.8 dynamic-slice_convert_fusion.2
  3.8 0.9 dynamic-slice_convert_fusion.1
  4.8 1.0 dynamic-slice_convert_fusion
  5.7 0.7 maximum_maximum_fusion.pack_ref
  6.5 0.7 pad_add_fusion.1
  7.2 0.6 pad.31.number_ref
  7.8 87.3 %start_all.1 = (s32[2,2,4,2,16,128]{5,4,3,2,1,0:T(8,128)}, bf16[2,2,4,2,160,768]{5,4,3,2,1,0:T(8,128)(2,1)}, f32[128,768]{1,0:T(8,128)}, bf16[1584,768]{1,0:T(8,...) custom-call(s32[16,128]{1,0:T(8,128)} %pad.31.number_ref, ...), custom_call_target="tpu_custom_call" | custom-call | tf_op jit(solution)/shard_map/start_all/pallas_call | solution.py:1282
  95.1 1.1 copy.130
  96.2 0.2 fusion.1
  96.4 0.6 add_select_fusion.slot_ref
  97.0 1.0 slice.207
  98.1 0.1 reshape.452
  98.3 0.1 slice.210
  98.4 0.1 copy.140
  98.5 0.1 slice.211
  98.7 0.1 copy.141
  98.8 0.6 convert_bitcast_fusion.gain_ref
  99.4 0.1 slice.212
  99.6 0.7 pad.37.router_ref
  100.3 0.2 copy.139
  100.5 0.7 pad_convert_fusion.vec_ref
  101.2 0.2 reduce_window_sum.12
  101.3 0.1 convert_reduce_fusion.1
  101.6 0.1 convert_reduce_fusion
  101.8 0.7 copy.129.mask_ref
  102.6 43.8 %mixer_forward.1 = (f32[128,768]{1,0:T(8,128)}, bf16[128,768]{1,0:T(8,128)(2,1)}, f32[128,128]{1,0:T(8,128)}, f32[128,1536]{1,0:T(8,128)}, f32[136,1536]{1,0:T(8...) custom-call(f32[128,768]{1,0:T(8,128)} %get-tuple-element.82.x_ref, ...), custom_call_target="tpu_custom_call" | custom-call | tf_op jit(solution)/shard_map/mixer_forward/pallas_call | solution.py:1685
  146.5 92.3 %moe_forward.1 = (f32[128,768]{1,0:T(8,128)}, bf16[4,512,768]{2,1,0:T(8,128)(2,1)}, f32[4,512,384]{2,1,0:T(8,128)}, bf16[2,4,384,768]{3,2,1,0:T(8,128)(2,1)}) custom-call(bf16[128,768]{1,0:T(8,128)(2,1)} %get-tuple-element.86.own_ref, s32[32,128]{1,0:T(8,128)} %add_select_fusion.slot_ref, f32[2,4,384,768]{3,2,1,0:T(8,128)} %master_ref.3), custom_call_target="tpu_custom_call" | custom-call | tf_op jit(solution)/shard_map/moe_forward/pallas_call | solution.py:2106
  238.8 0.2 select_reduce_fusion
  239.0 1.9 multiply_reduce_fusion.5
  240.9 0.8 multiply_convert_fusion.1.own_ref
  241.7 70.4 %head_forward.1 = (bf16[2,2,4,2,128,768]{5,4,3,2,1,0:T(8,128)(2,1)}, f32[2,16,256]{2,1,0:T(8,128)}) custom-call(bf16[128,768]{1,0:T(8,128)(2,1)} %multiply_convert_fusion.1.own_ref, bf16[1584,768]{1,0:T(8,128)(2,1)} %get-tuple-element.89.table_ref, s32[16,256]{1,0:T(8,128)} %get-tuple-element.90.target_ref), custom_call_target="tpu_custom_call" | custom-call | tf_op jit(solution)/shard_map/head_forward/pallas_call | solution.py:532
  312.1 1.3 slice_subtract_fusion
  313.4 0.4 slice_reduce_fusion.16
  314.6 0.1 lt.236
  314.7 0.1 lt.241
  314.8 0.1 lt.246
  315.3 0.3 fusion.22
  316.5 0.7 select_add_fusion.weight_ref
  317.2 71.7 %head_backward.1 = (f32[128,768]{1,0:T(8,128)}, f32[1584,768]{1,0:T(8,128)}) custom-call(bf16[2,2,4,2,128,768]{5,4,3,2,1,0:T(8,128)(2,1)} %get-tuple-element.91.all_ref, bf16[1584,768]{1,0:T(8,128)(2,1)} %get-tuple-element.89.table_ref, bf16[768,1664]{1,0:T(8,128)(2,1)} %get-tuple-element.92.turned_ref, s32[16,256]{1,0:T(8,128)} %get-tuple-element.90.target_ref, ...), custom_call_target="tpu_custom_call" | custom-call | tf_op jit(solution)/shard_map/head_backward/pallas_call | solution.py:665
  388.9 1.1 multiply_reduce_fusion
  390.0 1.2 fusion.4
  391.3 0.8 multiply_convert_fusion.own_ref
  392.0 95.5 %moe_backward.1 = (f32[128,768]{1,0:T(8,128)}, f32[2,4,384,768]{3,2,1,0:T(8,128)}, f32[8,128]{1,0:T(8,128)}) custom-call(bf16[128,768]{1,0:T(8,128)(2,1)} %multiply_convert_fusion.own_ref, s32[32,128]{1,0:T(8,128)} %add_select_fusion.slot_ref, bf16[2,4,384,768]{3,2,1,0:T(8,128)(2,1)} %get-tuple-element.95.weights_ref, ...), custom_call_target="tpu_custom_call" | custom-call | tf_op jit(solution)/shard_map/moe_backward/pallas_call | solution.py:2197
  487.6 1.2 slice.200
  488.8 0.6 broadcast_in_dim.147
  489.6 0.7 fusion.36
  490.3 0.6 concatenate.29
  491.0 0.7 concatenate.30.scalar_ref
  491.6 0.4 fusion.11
  492.1 1.5 multiply_reduce_fusion.1
  493.6 0.2 stack.21
  493.8 0.2 broadcast_multiply_fusion
  494.0 0.2 stack.22
  494.1 1.2 fusion.6.side_ref
  495.3 0.9 subtract_add_fusion.grad_ref
  496.2 56.9 %mixer_backward.1 = (bf16[128,768]{1,0:T(8,128)(2,1)}, bf16[4,8,160,768]{3,2,1,0:T(8,128)(2,1)}) custom-call(f32[128,768]{1,0:T(8,128)} %subtract_add_fusion.grad_ref, f32[768,128]{1,0:T(8,128)} %fusion.6.side_ref, f32[128,768]{1,0:T(8,128)} %get-tuple-element.82.x_ref, bf16[4,8,160,768]{3,2,1,0:T(8,128)(2,1)} %bitcast.77, ...), custom_call_target="tpu_custom_call" | custom-call | tf_op jit(solution)/shard_map/mixer_backward/pallas_call | solution.py:1912
  553.1 93.1 %finish_all.1 = (f32[1584,768]{1,0:T(8,128)}, bf16[4,160,768]{2,1,0:T(8,128)(2,1)}, f32[8,128]{1,0:T(8,128)}) custom-call(bf16[128,768]{1,0:T(8,128)(2,1)} %get-tuple-element.110.own_ref, bf16[2,2,4,2,160,768]{5,4,3,2,1,0:T(8,128)(2,1)} %bitcast.80, s32[16,256]{1,0:T(8,128)} %get-tuple-element.112.token_ref, f32[1584,768]{1,0:T(8,128)} %get-tuple-element.113.head_ref, ...), custom_call_target="tpu_custom_call" | custom-call | tf_op jit(solution)/shard_map/finish_all/pallas_call | solution.py:1458
  646.2 1.3 fusion.40
  648.2 24.0 %multiply_add_fusion = (f32[2,4,384,768]{3,2,1,0:T(8,128)}, f32[2,4,384,768]{3,2,1,0:T(8,128)}, f32[2,4,384,768]{3,2,1,0:T(8,128)}) fusion(f32[2,4,384,768]{3,2,1,0:T(8,128)} %param.55, f32[2,4,384,768]{3,2,1,0:T(8,128)} %master_ref.3, f32[2,4,384,768]{3,2,1,0:T(8,128)} %get-tuple-element.136, f32[]{:T(128)S(6)} %min.3, f32[2,4,384,768]{3,2,1,0:T(8,128)} %param.54), kind=kLoop, calls=%fused_computation | loop fusion | flops 23592960 | bytes 66060292 | tf_op jit(solution)/shard_map/add | solution.py:2510
  672.2 5.8 update_all.1
  678.1 9.7 %multiply_add_fusion.2 = (f32[1572,768]{1,0:T(8,128)}, f32[1572,768]{1,0:T(8,128)}, f32[1572,768]{1,0:T(8,128)}) fusion(f32[1572,768]{1,0:T(8,128)} %param.34, f32[1572,768]{1,0:T(8,128)S(1)} %bitcast.79, f32[1584,768]{1,0:T(8,128)} %get-tuple-element.116, f32[]{:T(128)S(6)} %min.3, f32[1572,768]{1,0:T(8,128)} %param.33), kind=kLoop, calls=%fused_computation.3 | loop fusion | flops 12072960 | bytes 33804292 | tf_op jit(solution)/shard_map/add | solution.py:2510
  (97 shorter events, 2.8 us)
Async XLA Ops:
  7.8 93.4 %copy-start.4 = (s32[4,8]{1,0:T(4,128)S(1)}, s32[4,8]{1,0:T(4,128)}, u32[]{:S(2)}) copy-start(s32[4,8]{1,0:T(4,128)} %param.30) | copy-start | bytes 388
  146.4 92.4 %copy-start.3 = (f32[128,128]{1,0:T(8,128)S(1)}, f32[128,128]{1,0:T(8,128)}, u32[]{:S(2)}) copy-start(f32[128,128]{1,0:T(8,128)} %get-tuple-element.85) | copy-start | bytes 196612
  146.4 92.4 %copy-start.6 = (s32[1,128,1]{1,2,0:T(1,128)S(1)}, s32[1,128,1]{1,2,0:T(1,128)}, u32[]{:S(2)}) copy-start(s32[1,128,1]{1,2,0:T(1,128)} %param.31) | copy-start | bytes 1540
  146.4 92.6 %copy-start = (f32[128,768]{1,0:T(8,128)S(1)}, f32[128,768]{1,0:T(8,128)}, u32[]{:S(2)}) copy-start(f32[128,768]{1,0:T(8,128)} %get-tuple-element.84) | copy-start | bytes 1179652
  146.5 94.4 %copy-start.5 = (f32[3,768]{1,0:T(4,128)S(1)}, f32[3,768]{1,0:T(4,128)}, u32[]{:S(2)}) copy-start(f32[3,768]{1,0:T(4,128)} %convert_bitcast_fusion.gain_ref) | copy-start | bytes 27652
  317.2 72.8 %copy-start.1 = (f32[128,768]{1,0:T(8,128)S(1)}, f32[128,768]{1,0:T(8,128)}, u32[]{:S(2)}) copy-start(f32[128,768]{1,0:T(8,128)} %get-tuple-element.88) | copy-start | bytes 1179652
  392.0 99.6 %copy-start.2 = (bf16[128,768]{1,0:T(8,128)(2,1)S(1)}, bf16[128,768]{1,0:T(8,128)(2,1)}, u32[]{:S(2)}) copy-start(bf16[128,768]{1,0:T(8,128)(2,1)} %get-tuple-element.86.own_ref) | copy-start | bytes 589828
  648.2 29.9 %slice-start = ((s8[4841472]{0:T(1024)(128)(4,1)}), s8[4194304]{0:T(1024)(128)(4,1)S(1)}, s32[]{:S(2)}) async-start(s8[4841472]{0:T(1024)(128)(4,1)} %bitcast.78), calls=%async_computation | async-start | bytes 8388608
  648.2 29.8 %slice-start.1 = ((s8[4841472]{0:T(1024)(128)(4,1)}), s8[647168]{0:T(1024)(128)(4,1)S(1)}, s32[]{:S(2)}) async-start(s8[4841472]{0:T(1024)(128)(4,1)} %bitcast.78), calls=%async_computation.1 | async-start | bytes 1294336
